TPU v7x, 256 devices: a whole 4x4x8 slice. The times are simulated.
256 devices in a mesh: seq: 32 (over x, z), chan: 8 (over y, core).
Axes of the slice: x: 4, y: 4, z: 8, core: 2. Of those that a mesh axis runs over, the one named last changes fastest.
Arguments:
- input_triple_streams: bfloat16 [10240, 3, 8192], P('seq', None, 'chan'), may hold values from -6 to 6
- former_piece_sizes: int32 [32], replicated, may hold values from 1 to 320, 8192 in all
- updated_piece_sizes: int32 [28], replicated, may hold values from 1 to 320, 8192 in all
- remaining_indices: int32 [28], replicated, may hold values from 0 to 31, as said below
- short_causal_filters: float32 [3, 3, 8192], P(None, None, 'chan'), may hold values from -3 to 3
- pole_coefficients: float32 [16, 8192], P(None, 'chan'), may hold values from -0.4375 to 0.4375
- pole_damping: float32 [16, 8192], P(None, 'chan'), may hold values from 6.1035156e-05 to 0.03125
- direct_coefficient: float32 [8192], P('chan'), may hold values from 0.5 to 1.5
- final_projector: bfloat16 [8192, 8192], P('seq', 'chan'), may hold values from -0.0625 to 0.0625
Outputs:
- mixed_rows: bfloat16 [10240, 8192], P('seq', 'chan')
Inputs may be any that keep to these rules, and one draw needn't show every extreme that they name: `former_piece_sizes`: the counts sum to 8192; an index's rows fill its first slots in sequence order. `updated_piece_sizes`: the counts sum to 8192. `remaining_indices`: distinct indices of seq.
All inputs are finite; a program needn't handle non-finite values.
Results may differ from a plain program's by a relative error of at most 0.0064.
Values may be sent and summed in bfloat16 or wider, within the bound.
A program may use at most 128 MiB of HBM per device.

v0:
```python
import jax
import jax.numpy as jnp
from jax import lax
from jax.sharding import PartitionSpec as P

GROUP = 128


def long_mix(queries, gated_prod, pole_coefficients, pole_damping, direct_coefficient):
    chan_count, length = gated_prod.shape
    group_count = length // GROUP
    gated_full = gated_prod.astype(jnp.float32)
    signal = gated_full.reshape(chan_count, group_count, GROUP)
    offsets = jnp.arange(GROUP, dtype=jnp.float32)
    decay_rates = pole_damping[:, :, None]
    lag_value = offsets[:, None] - offsets[None, :]
    lag_clip = jnp.maximum(lag_value, 0.0)
    lag_powers = jnp.exp(-pole_damping[:, :, None, None] * lag_clip[None, None, :, :])
    toeplitz_full = jnp.einsum(
        "mc,mcij->cij", pole_coefficients, lag_powers, precision=lax.Precision.HIGHEST
    )
    toeplitz = jnp.where(lag_value[None] >= 0.0, toeplitz_full, 0.0)
    within_sum = jnp.einsum("cij,cnj->cni", toeplitz, signal, precision=lax.Precision.HIGHEST)
    tail_weights = jnp.exp(-decay_rates * (GROUP - 1.0 - offsets)[None, None, :])
    summary = jnp.einsum("mcj,cnj->mcn", tail_weights, signal, precision=lax.Precision.HIGHEST)
    step_decay = jnp.broadcast_to(jnp.exp(-pole_damping * GROUP)[:, :, None], summary.shape)

    def combine(earlier, later):
        return (earlier[0] * later[0], earlier[1] * later[0] + later[1])

    carried = lax.associative_scan(combine, (step_decay, summary), axis=2)[1]
    before = jnp.concatenate([jnp.zeros_like(carried[:, :, :1]), carried[:, :, :-1]], axis=2)
    head_weights = pole_coefficients[:, :, None] * jnp.exp(
        -decay_rates * (offsets + 1.0)[None, None, :]
    )
    remote = jnp.einsum("mci,mcn->cni", head_weights, before, precision=lax.Precision.HIGHEST)
    conv_total = (within_sum + remote).reshape(chan_count, length) + direct_coefficient[
        :, None
    ] * gated_full
    return (queries.astype(jnp.float32) * conv_total).astype(jnp.bfloat16)


def compact_rows(moved_rows, former_piece_sizes, capacity, seq_len, seq_count):
    old_end = jnp.cumsum(former_piece_sizes)
    old_start = old_end - former_piece_sizes
    lead_shape = moved_rows.shape[:2]
    buffer = jnp.zeros(lead_shape + (seq_len + capacity,), moved_rows.dtype)

    def place(source, current):
        piece = lax.dynamic_slice_in_dim(moved_rows, source * capacity, capacity, 2)
        return lax.dynamic_update_slice_in_dim(current, piece, old_start[source], 2)

    filled = lax.fori_loop(0, seq_count, place, buffer)
    return filled[:, :, :seq_len]


def shards(
    input_triple_streams,
    former_piece_sizes,
    updated_piece_sizes,
    remaining_indices,
    short_causal_filters,
    pole_coefficients,
    pole_damping,
    direct_coefficient,
    final_projector,
):
    seq_count = lax.axis_size("seq")
    own_index = lax.axis_index("seq")
    capacity = input_triple_streams.shape[0]
    chan_width = input_triple_streams.shape[2]
    narrow = chan_width // seq_count
    seq_len = capacity * 4 // 5 * seq_count
    first_chan = own_index * narrow
    moved_rows = lax.all_to_all(
        jnp.transpose(input_triple_streams, (1, 2, 0)),
        "seq",
        split_axis=1,
        concat_axis=2,
        tiled=True,
    )
    compact = compact_rows(moved_rows, former_piece_sizes, capacity, seq_len, seq_count)
    signal = compact.astype(jnp.float32)
    lag_one = jnp.pad(signal, ((0, 0), (0, 0), (1, 0)))[:, :, :-1]
    lag_two = jnp.pad(signal, ((0, 0), (0, 0), (2, 0)))[:, :, :-2]
    taps = lax.dynamic_slice_in_dim(short_causal_filters, first_chan, narrow, 2)
    featured = (
        taps[:, 0, :, None] * signal + taps[:, 1, :, None] * lag_one + taps[:, 2, :, None] * lag_two
    )
    queries = lax.optimization_barrier(featured[0].astype(jnp.bfloat16))
    gated_prod = lax.optimization_barrier((featured[1] * featured[2]).astype(jnp.bfloat16))
    residue_mine = lax.dynamic_slice_in_dim(pole_coefficients, first_chan, narrow, 1)
    decay_mine = lax.dynamic_slice_in_dim(pole_damping, first_chan, narrow, 1)
    skip_mine = lax.dynamic_slice_in_dim(direct_coefficient, first_chan, narrow, 0)
    hidden = long_mix(queries, gated_prod, residue_mine, decay_mine, skip_mine)
    new_end = jnp.cumsum(updated_piece_sizes)
    new_start = new_end - updated_piece_sizes
    device_names = jnp.arange(seq_count, dtype=jnp.int32)
    partner_table = (remaining_indices[None, :] == device_names[:, None]).astype(jnp.int32)
    start_dev = jnp.sum(partner_table * new_start[None, :], axis=1)
    count_dev = jnp.sum(partner_table * updated_piece_sizes[None, :], axis=1)
    offsets = jnp.arange(capacity, dtype=jnp.int32)
    hidden_padded = jnp.concatenate(
        [hidden, jnp.zeros((hidden.shape[0], capacity), hidden.dtype)], axis=1
    )
    outgoing_init = jnp.zeros((hidden.shape[0], capacity * seq_count), hidden.dtype)

    def pick(target, current):
        piece = lax.dynamic_slice_in_dim(hidden_padded, start_dev[target], capacity, 1)
        kept = jnp.where((offsets < count_dev[target])[None, :], piece, jnp.zeros_like(piece))
        return lax.dynamic_update_slice_in_dim(current, kept, target * capacity, 1)

    outgoing = lax.fori_loop(0, seq_count, pick, outgoing_init)
    arrived = lax.all_to_all(outgoing, "seq", split_axis=1, concat_axis=0, tiled=True)
    all_channels = lax.all_gather(arrived, "chan", axis=0, tiled=True)
    projected = lax.dot_general(
        all_channels,
        lax.all_gather(final_projector, "seq", axis=0, tiled=True),
        (((0,), (0,)), ((), ())),
        preferred_element_type=jnp.float32,
    )
    return projected.astype(jnp.bfloat16)


def solution(mesh):
    return jax.shard_map(
        shards,
        mesh=mesh,
        in_specs=(
            P("seq", None, "chan"),
            P(),
            P(),
            P(),
            P(None, None, "chan"),
            P(None, "chan"),
            P(None, "chan"),
            P("chan"),
            P("seq", "chan"),
        ),
        out_specs=P("seq", "chan"),
        check_vma=False,
    )
```

profile of v0, /device:TPU:32, one launch (start us, length us, event | category | flops | bytes accessed | tf_op | source)
XLA Modules:
  0.0 738.5 jit_solution(2049985253487504112)
XLA Ops:
  6.5 5.7 copy.76
  12.3 11.3 %all-to-all-start = ((bf16[3,1024,320]{2,0,1:T(4,128)(2,1)}), bf16[3,1024,320]{2,0,1:T(4,128)(2,1)S(1)}, u32[]{:S(2)}, u32[]{:S(2)}) async-start(bf16[3,1024,320]{2,0,1:T(4,128)(2,1)} %bitcast.2), calls=%async_computation | async-start | bytes 6291456 | tf_op jit(solution)/shard_map/all_to_all | solution.py:75
  29.8 11.4 %multiply_exponential_fusion = f32[16,32,128,128]{3,2,1,0:T(8,128)} fusion(f32[128,128]{1,0:T(8,128)S(1)} %fusion.36, f32[16,32]{1,0:T(8,128)S(1)} %get-tuple-element.228), kind=kLoop, calls=%fused_computation.6 | loop fusion | flops 8388608 | bytes 33622016 | tf_op jit(solution)/shard_map/exp | solution.py:18
  41.2 46.0 %fusion.2 = f32[32,1,128,128]{3,1,2,0:T(1,128)} fusion(f32[16,32,1,1]{0,2,3,1:T(1,128)S(1)} %copy.94, f32[16,32,128,128]{3,2,1,0:T(8,128)} %multiply_exponential_fusion), kind=kOutput, calls=%fused_computation.4 | convolution fusion | flops 100663296 | bytes 35653632 | tf_op jit(solution)/shard_map/mc,mcij->cij/dot_general | solution.py:19
  87.2 7.4 %all-to-all-done = bf16[3,1024,320]{2,0,1:T(4,128)(2,1)S(1)} async-done(((bf16[3,1024,320]{2,0,1:T(4,128)(2,1)}), bf16[3,1024,320]{2,0,1:T(4,128)(2,1)S(1)}, u32[]{:S(2)}, u32[]{:S(2)}) %all-to-all-start) | async-done | bytes 1966112 | tf_op jit(solution)/shard_map/all_to_all | solution.py:75
  95.8 3.4 all_to_all.30
  99.4 147.3 %while.27 = (s32[]{:T(128)}, bf16[3,32,8512]{2,1,0:T(8,128)(2,1)S(1)}, bf16[3,32,10240]{2,1,0:T(8,128)(2,1)}, s32[32]{0:T(128)S(1)}, s32[]{:T(128)}, /*index=5*/s32[]{:T(128)}, s32[]{:T(128)}, s32[]{:T(128)}, s32[]{:T(128)}) while((s32[]{:T(128)}, bf16[3,32,8512]{2,1,0:T(8,128)(2,1)S(1)}, bf16[3,32,10240]{2,1,0:T(8,128)(2,1)}, ...), condition=%wide.region_4.5_spmd, body=%wide.region_3.4_spmd.sunk | while | flops 9 | bytes 245953 | solution.py:53
  251.4 3.7 slice.164
  255.1 3.8 slice.166
  260.8 3.3 slice.168
  264.1 3.4 slice.170
  272.1 2.9 slice.174
  291.9 3.3 slice.197
  295.2 4.5 slice.200
  316.2 2.9 pad.55
  320.2 3.2 pad.57
  323.4 13.0 %pad.58 = f32[16,32,32]{2,0,1:T(8,128)S(1)} pad(f32[16,32,16]{2,0,1:T(8,128)} %add.197, f32[]{:T(128)} %constant.118.clone.1), padding=0_0_0x0_0_0x1_0_1 | pad | bytes 98308 | tf_op jit(solution)/shard_map/pad | solution.py:31
  337.1 16.6 %pad.100 = f32[16,32,64]{2,0,1:T(8,128)} pad(f32[16,32,32]{2,0,1:T(8,128)} %add.199, f32[]{:T(128)} %constant.118.clone.1), padding=0_0_0x0_0_0x1_0_1 | pad | bytes 196612
  355.0 4.3 pad.72
  365.3 139.6 %while.28 = (s32[]{:T(128)}, bf16[32,10240]{1,0:T(8,128)(2,1)S(1)}, s32[32]{0:T(128)S(1)}, s32[32]{0:T(128)S(1)}, bf16[32,8512]{1,0:T(8,128)(2,1)S(1)}, /*index=...) while((s32[]{:T(128)}, bf16[32,10240]{1,0:T(8,128)(2,1)S(1)}, s32[32]{0:T(128)S(1)}, ...), condition=%wide.region_7.8_spmd.clone, body=%wide.region_6.7_spmd.clone.sunk | while | flops 10569 | bytes 82777 | solution.py:113
  506.1 32.4 %all_to_all.37 = bf16[32,32,320]{2,0,1:T(8,128)(2,1)} all-to-all(bf16[32,32,320]{2,0,1:T(8,128)(2,1)S(1)} %copy.93), channel_id=1, replica_groups=mesh['seq'=32,'chan'=8] {'seq'}, dimensions={1} | all-to-all | bytes 1310720 | tf_op jit(solution)/shard_map/all_to_all | solution.py:114
  539.2 39.2 %all-gather.3.cloned.1.call-done = bf16[8192,320]{1,0:T(8,128)(2,1)} async-done(((bf16[1024,320]{1,0:T(8,128)(2,1)}), bf16[8192,320]{1,0:T(8,128)(2,1)}) %all-gather.3.cloned.1.call-update) | async-done | bytes 5242896 | tf_op jit(solution)/shard_map/all_gather | solution.py:115
  578.5 141.4 %all-gather.5.cloned.1.call-done = bf16[8192,1024]{1,0:T(8,128)(2,1)} async-done(((bf16[256,1024]{1,0:T(8,128)(2,1)}), bf16[8192,1024]{1,0:T(8,128)(2,1)}) %all-gather.5.cloned.1.call-update) | async-done | bytes 16777232 | tf_op jit(solution)/shard_map/all_gather | solution.py:118
  719.9 11.7 %convolution_convert_fusion = bf16[320,1024]{1,0:T(8,128)(2,1)} fusion(bf16[8192,320]{1,0:T(8,128)(2,1)} %all-gather.3.cloned.1.call-done, bf16[8192,1024]{1,0:T(8,128)(2,1)} %all-gather.5.cloned.1.call-done), kind=kOutput, calls=%fused_computation.17 | convolution fusion | flops 5369036800 | bytes 22675456 | tf_op jit(solution)/shard_map/dot_general | solution.py:116
  (377 shorter events, 220.2 us)
Async XLA Ops:
  12.3 13.3 %copy-start.16 = (s32[32]{0:T(128)S(1)}, s32[32]{0:T(128)}, u32[]{:S(2)}) copy-start(s32[32]{0:T(128)} %param.14) | copy-start | bytes 388
  12.3 17.1 %copy-start.15 = (s32[28]{0:T(128)S(1)}, s32[28]{0:T(128)}, u32[]{:S(2)}) copy-start(s32[28]{0:T(128)} %param.15) | copy-start | bytes 340
  12.3 17.4 %copy-start.17 = (s32[28]{0:T(128)S(1)}, s32[28]{0:T(128)}, u32[]{:S(2)}) copy-start(s32[28]{0:T(128)} %param.16) | copy-start | bytes 340
  12.3 82.3 %all-to-all-start = ((bf16[3,1024,320]{2,0,1:T(4,128)(2,1)}), bf16[3,1024,320]{2,0,1:T(4,128)(2,1)S(1)}, u32[]{:S(2)}, u32[]{:S(2)}) async-start(bf16[3,1024,320]{2,0,1:T(4,128)(2,1)} %bitcast.2), calls=%async_computation | async-start | bytes 6291456 | tf_op jit(solution)/shard_map/all_to_all | solution.py:75
  23.6 554.9 %all-gather.3.cloned.1.call-start = ((), (), s32[]{:S(2)}) async-start(), calls=%async_computation.2 | async-start | bytes 7077888 | tf_op jit(solution)/shard_map/all_gather | solution.py:115
  248.8 0.8 copy-start.8
  249.6 0.8 copy-start.6
  251.4 28.1 %copy-start.1 = (f32[16,32,64]{2,0,1:T(8,128)}, f32[16,32,64]{2,0,1:T(8,128)S(1)}, u32[]{:S(2)}) copy-start(f32[16,32,64]{2,0,1:T(8,128)S(1)} %convolution_bitcast_fusion) | copy-start | bytes 393220
  299.7 3.3 copy-start.11
  301.7 6.3 copy-start.14
  302.9 5.3 copy-start.5
  305.5 10.4 %copy-start.13 = (f32[16,32,7]{2,0,1:T(8,128)S(1)}, f32[16,32,7]{2,0,1:T(8,128)}, u32[]{:S(2)}) copy-start(f32[16,32,7]{2,0,1:T(8,128)} %slice.194) | copy-start | bytes 43012
  307.9 8.1 %copy-start.4 = (f32[16,32,16]{2,0,1:T(8,128)S(1)}, f32[16,32,16]{2,0,1:T(8,128)}, u32[]{:S(2)}) copy-start(f32[16,32,16]{2,0,1:T(8,128)} %multiply_add_fusion.3) | copy-start | bytes 98308
  308.2 11.7 %copy-start.12 = (f32[16,32,15]{2,0,1:T(8,128)S(1)}, f32[16,32,15]{2,0,1:T(8,128)}, u32[]{:S(2)}) copy-start(f32[16,32,15]{2,0,1:T(8,128)} %slice.197) | copy-start | bytes 92164
  310.7 9.3 %copy-start.3 = (f32[16,32,32]{2,0,1:T(8,128)S(1)}, f32[16,32,32]{2,0,1:T(8,128)}, u32[]{:S(2)}) copy-start(f32[16,32,32]{2,0,1:T(8,128)} %multiply_add_fusion.4) | copy-start | bytes 196612
  319.1 35.7 %copy-start.2 = (f32[16,32,64]{2,0,1:T(8,128)S(1)}, f32[16,32,64]{2,0,1:T(8,128)}, u32[]{:S(2)}) copy-start(f32[16,32,64]{2,0,1:T(8,128)} %copy-done.1) | copy-start | bytes 393220
  323.4 39.0 %copy-start = (f32[32,1,128,128]{3,1,2,0:T(1,128)S(1)}, f32[32,1,128,128]{3,1,2,0:T(1,128)}, u32[]{:S(2)}) copy-start(f32[32,1,128,128]{3,1,2,0:T(1,128)} %fusion.2) | copy-start | bytes 6291460
  323.4 39.0 %copy-start.7 = (bf16[4,8,64,128]{3,2,1,0:T(8,128)(2,1)S(1)}, bf16[4,8,64,128]{3,2,1,0:T(8,128)(2,1)}, u32[]{:S(2)}) copy-start(bf16[4,8,64,128]{3,2,1,0:T(8,128)(2,1)} %copy-done.6) | copy-start | bytes 1572868
  360.2 4.3 copy-start.9
  360.2 4.3 copy-start.10
  360.3 4.3 copy-start.18
  538.5 181.4 %all-gather.5.cloned.1.call-start = ((), (), s32[]{:S(2)}) async-start(), calls=%async_computation.3 | async-start | bytes 17301504 | tf_op jit(solution)/shard_map/all_gather | solution.py:118
Sparse Core Ops, SparseCore 0:
  538.6 39.8 all-gather.2
  581.1 138.8 all-gather.4
where the time goes:
time: 748 us; the launch traced here: 739 us
  local copies, waits for them, and re-layouts  246 us (33%)
  waiting for transfers between devices  189 us (25%)
  loops' own time  129 us (17%)
  matrix products  62.9 us (8%)
  other arithmetic  53.4 us (7%)
  blocking collectives  32.4 us (4%)
  between operations  13.9 us (2%)
  starting transfers between devices  11.4 us (2%)
    all_gather x1, waiting for transfers between devices, shards(): lax.all_gather(final_projector, 'seq', axis=0, tiled=True)  141 us
    another operation x1, loops' own time, compact_rows(): filled = lax.fori_loop(0, seq_count, place, buffer)  65.9 us
    another operation x1, loops' own time, shards(): outgoing = lax.fori_loop(0, seq_count, pick, outgoing_init)  63.5 us
    dot_general x1, matrix products, long_mix(): jnp.einsum('mc,mcij->cij', pole_coefficients, lag_powers, precision=lax.P...  46 us
    slice x16, local copies, waits for them, and re-layouts, long_mix(): carried = lax.associative_scan(combine, (step_decay, summary), axis=2)[1]  43.3 us
    all_gather x1, waiting for transfers between devices, shards(): all_channels = lax.all_gather(arrived, 'chan', axis=0, tiled=True)  39.2 us
    all_to_all x1, blocking collectives, shards(): lax.all_to_all(outgoing, 'seq', split_axis=1, concat_axis=0, tiled=True)  32.4 us
    dynamic_slice x32, local copies, waits for them, and re-layouts, place(): piece = lax.dynamic_slice_in_dim(moved_rows, source * capacity, capacity, 2)  31.6 us
  transfers between devices with their start and end apart: 3, of which 3 were waited for; matrix products, arithmetic and copies ran while one was open for 9% of the time, Pallas kernels for 0%

commit v1 on v0

--- a/solution.py
+++ b/solution.py
@@ -40,8 +40,13 @@
     return (queries.astype(jnp.float32) * conv_total).astype(jnp.bfloat16)
 
 
+def running_ends(sizes):
+    index = jnp.arange(sizes.shape[0], dtype=jnp.int32)
+    return jnp.sum(jnp.where(index[None, :] <= index[:, None], sizes[None, :], 0), axis=1)
+
+
 def compact_rows(moved_rows, former_piece_sizes, capacity, seq_len, seq_count):
-    old_end = jnp.cumsum(former_piece_sizes)
+    old_end = running_ends(former_piece_sizes)
     old_start = old_end - former_piece_sizes
     lead_shape = moved_rows.shape[:2]
     buffer = jnp.zeros(lead_shape + (seq_len + capacity,), moved_rows.dtype)
@@ -93,7 +98,7 @@
     decay_mine = lax.dynamic_slice_in_dim(pole_damping, first_chan, narrow, 1)
     skip_mine = lax.dynamic_slice_in_dim(direct_coefficient, first_chan, narrow, 0)
     hidden = long_mix(queries, gated_prod, residue_mine, decay_mine, skip_mine)
-    new_end = jnp.cumsum(updated_piece_sizes)
+    new_end = running_ends(updated_piece_sizes)
     new_start = new_end - updated_piece_sizes
     device_names = jnp.arange(seq_count, dtype=jnp.int32)
     partner_table = (remaining_indices[None, :] == device_names[:, None]).astype(jnp.int32)

time: 748 us -> 742 us (level)
  no operation moved by 1% of the time
where the time goes in v1:
time: 742 us; the launch traced here: 733 us
  local copies, waits for them, and re-layouts  245 us (33%)
  waiting for transfers between devices  189 us (25%)
  loops' own time  125 us (17%)
  matrix products  62.9 us (8%)
  other arithmetic  53.2 us (7%)
  blocking collectives  32.4 us (4%)
  between operations  13.9 us (2%)
  starting transfers between devices  11.4 us (2%)
    all_gather x1, waiting for transfers between devices, shards(): lax.all_gather(final_projector, 'seq', axis=0, tiled=True)  141 us
    another operation x1, loops' own time, shards(): outgoing = lax.fori_loop(0, seq_count, pick, outgoing_init)  63.5 us
    another operation x1, loops' own time, compact_rows(): filled = lax.fori_loop(0, seq_count, place, buffer)  61.3 us
    dot_general x1, matrix products, long_mix(): jnp.einsum('mc,mcij->cij', pole_coefficients, lag_powers, precision=lax.P...  45.9 us
    slice x16, local copies, waits for them, and re-layouts, long_mix(): carried = lax.associative_scan(combine, (step_decay, summary), axis=2)[1]  43.3 us
    all_gather x1, waiting for transfers between devices, shards(): all_channels = lax.all_gather(arrived, 'chan', axis=0, tiled=True)  39.2 us
    all_to_all x1, blocking collectives, shards(): lax.all_to_all(outgoing, 'seq', split_axis=1, concat_axis=0, tiled=True)  32.4 us
    dynamic_slice x32, local copies, waits for them, and re-layouts, place(): piece = lax.dynamic_slice_in_dim(moved_rows, source * capacity, capacity, 2)  31.6 us
  transfers between devices with their start and end apart: 3, of which 3 were waited for; matrix products, arithmetic and copies ran while one was open for 9% of the time, Pallas kernels for 0%

profile of v1, /device:TPU:32, one launch (start us, length us, event | category | flops | bytes accessed | tf_op | source)
XLA Modules:
  0.0 733.2 jit_solution(1492705692727548347)
XLA Ops:
  6.5 5.7 copy.67
  12.3 11.3 %all-to-all-start = ((bf16[3,1024,320]{2,0,1:T(4,128)(2,1)}), bf16[3,1024,320]{2,0,1:T(4,128)(2,1)S(1)}, u32[]{:S(2)}, u32[]{:S(2)}) async-start(bf16[3,1024,320]{2,0,1:T(4,128)(2,1)} %bitcast.1), calls=%async_computation | async-start | bytes 6291456 | tf_op jit(solution)/shard_map/all_to_all | solution.py:80
  29.5 11.4 %multiply_exponential_fusion = f32[16,32,128,128]{3,2,1,0:T(8,128)} fusion(f32[128,128]{1,0:T(8,128)S(1)} %fusion.36, f32[16,32]{1,0:T(8,128)S(1)} %get-tuple-element.228), kind=kLoop, calls=%fused_computation.6 | loop fusion | flops 8388608 | bytes 33622016 | tf_op jit(solution)/shard_map/exp | solution.py:18
  41.0 45.9 %fusion.2 = f32[32,1,128,128]{3,1,2,0:T(1,128)} fusion(f32[16,32,1,1]{0,2,3,1:T(1,128)S(1)} %copy.84, f32[16,32,128,128]{3,2,1,0:T(8,128)} %multiply_exponential_fusion), kind=kOutput, calls=%fused_computation.4 | convolution fusion | flops 100663296 | bytes 35653632 | tf_op jit(solution)/shard_map/mc,mcij->cij/dot_general | solution.py:19
  86.9 7.7 %all-to-all-done = bf16[3,1024,320]{2,0,1:T(4,128)(2,1)S(1)} async-done(((bf16[3,1024,320]{2,0,1:T(4,128)(2,1)}), bf16[3,1024,320]{2,0,1:T(4,128)(2,1)S(1)}, u32[]{:S(2)}, u32[]{:S(2)}) %all-to-all-start) | async-done | bytes 1966112 | tf_op jit(solution)/shard_map/all_to_all | solution.py:80
  95.8 3.5 all_to_all.30
  99.4 141.9 %while.27 = (s32[]{:T(128)}, bf16[3,32,8512]{2,1,0:T(8,128)(2,1)S(1)}, bf16[3,32,10240]{2,1,0:T(8,128)(2,1)}, s32[32]{0:T(128)S(1)}, s32[]{:T(128)}, /*index=5*/s32[]{:T(128)}, s32[]{:T(128)}, s32[]{:T(128)}, s32[]{:T(128)}) while((s32[]{:T(128)}, bf16[3,32,8512]{2,1,0:T(8,128)(2,1)S(1)}, bf16[3,32,10240]{2,1,0:T(8,128)(2,1)}, ...), condition=%wide.region_4.5_spmd, body=%wide.region_3.4_spmd.sunk | while | flops 9 | bytes 245953 | solution.py:58
  246.1 3.7 slice.164
  249.8 3.8 slice.166
  255.4 3.3 slice.168
  258.7 3.4 slice.170
  266.8 2.9 slice.174
  286.6 3.3 slice.197
  289.9 4.5 slice.200
  310.9 2.9 pad.55
  314.9 3.2 pad.57
  318.1 13.0 %pad.58 = f32[16,32,32]{2,0,1:T(8,128)S(1)} pad(f32[16,32,16]{2,0,1:T(8,128)} %add.197, f32[]{:T(128)} %constant.112.clone.1), padding=0_0_0x0_0_0x1_0_1 | pad | bytes 98308 | tf_op jit(solution)/shard_map/pad | solution.py:31
  331.8 16.6 %pad.100 = f32[16,32,64]{2,0,1:T(8,128)} pad(f32[16,32,32]{2,0,1:T(8,128)} %add.199, f32[]{:T(128)} %constant.112.clone.1), padding=0_0_0x0_0_0x1_0_1 | pad | bytes 196612
  349.6 4.3 pad.72
  360.0 139.6 %while.28 = (s32[]{:T(128)}, bf16[32,10240]{1,0:T(8,128)(2,1)S(1)}, s32[32]{0:T(128)S(1)}, s32[32]{0:T(128)S(1)}, bf16[32,8512]{1,0:T(8,128)(2,1)S(1)}, /*index=...) while((s32[]{:T(128)}, bf16[32,10240]{1,0:T(8,128)(2,1)S(1)}, s32[32]{0:T(128)S(1)}, ...), condition=%wide.region_7.8_spmd.clone, body=%wide.region_6.7_spmd.clone.sunk | while | flops 10569 | bytes 82777 | solution.py:118
  500.7 32.4 %all_to_all.37 = bf16[32,32,320]{2,0,1:T(8,128)(2,1)} all-to-all(bf16[32,32,320]{2,0,1:T(8,128)(2,1)S(1)} %copy.83), channel_id=1, replica_groups=mesh['seq'=32,'chan'=8] {'seq'}, dimensions={1} | all-to-all | bytes 1310720 | tf_op jit(solution)/shard_map/all_to_all | solution.py:119
  533.9 39.2 %all-gather.3.cloned.1.call-done = bf16[8192,320]{1,0:T(8,128)(2,1)} async-done(((bf16[1024,320]{1,0:T(8,128)(2,1)}), bf16[8192,320]{1,0:T(8,128)(2,1)}) %all-gather.3.cloned.1.call-update) | async-done | bytes 5242896 | tf_op jit(solution)/shard_map/all_gather | solution.py:120
  573.1 141.4 %all-gather.5.cloned.1.call-done = bf16[8192,1024]{1,0:T(8,128)(2,1)} async-done(((bf16[256,1024]{1,0:T(8,128)(2,1)}), bf16[8192,1024]{1,0:T(8,128)(2,1)}) %all-gather.5.cloned.1.call-update) | async-done | bytes 16777232 | tf_op jit(solution)/shard_map/all_gather | solution.py:123
  714.6 11.7 %convolution_convert_fusion = bf16[320,1024]{1,0:T(8,128)(2,1)} fusion(bf16[8192,320]{1,0:T(8,128)(2,1)} %all-gather.3.cloned.1.call-done, bf16[8192,1024]{1,0:T(8,128)(2,1)} %all-gather.5.cloned.1.call-done), kind=kOutput, calls=%fused_computation.17 | convolution fusion | flops 5369036800 | bytes 22675456 | tf_op jit(solution)/shard_map/dot_general | solution.py:121
  (373 shorter events, 219.2 us)
Async XLA Ops:
  12.3 13.3 %copy-start.18 = (s32[32]{0:T(128)S(1)}, s32[32]{0:T(128)}, u32[]{:S(2)}) copy-start(s32[32]{0:T(128)} %param.14) | copy-start | bytes 388
  12.3 17.0 %copy-start.15 = (s32[28]{0:T(128)S(1)}, s32[28]{0:T(128)}, u32[]{:S(2)}) copy-start(s32[28]{0:T(128)} %param.15) | copy-start | bytes 340
  12.3 17.1 %copy-start.16 = (s32[28]{0:T(128)S(1)}, s32[28]{0:T(128)}, u32[]{:S(2)}) copy-start(s32[28]{0:T(128)} %param.16) | copy-start | bytes 340
  12.3 82.3 %all-to-all-start = ((bf16[3,1024,320]{2,0,1:T(4,128)(2,1)}), bf16[3,1024,320]{2,0,1:T(4,128)(2,1)S(1)}, u32[]{:S(2)}, u32[]{:S(2)}) async-start(bf16[3,1024,320]{2,0,1:T(4,128)(2,1)} %bitcast.1), calls=%async_computation | async-start | bytes 6291456 | tf_op jit(solution)/shard_map/all_to_all | solution.py:80
  23.6 549.5 %all-gather.3.cloned.1.call-start = ((), (), s32[]{:S(2)}) async-start(), calls=%async_computation.2 | async-start | bytes 7077888 | tf_op jit(solution)/shard_map/all_gather | solution.py:120
  243.5 0.8 copy-start.8
  244.3 0.8 copy-start.6
  246.0 28.1 %copy-start.1 = (f32[16,32,64]{2,0,1:T(8,128)}, f32[16,32,64]{2,0,1:T(8,128)S(1)}, u32[]{:S(2)}) copy-start(f32[16,32,64]{2,0,1:T(8,128)S(1)} %convolution_bitcast_fusion) | copy-start | bytes 393220
  294.4 3.3 copy-start.11
  296.4 6.3 copy-start.14
  297.6 5.3 copy-start.5
  300.2 10.4 %copy-start.13 = (f32[16,32,7]{2,0,1:T(8,128)S(1)}, f32[16,32,7]{2,0,1:T(8,128)}, u32[]{:S(2)}) copy-start(f32[16,32,7]{2,0,1:T(8,128)} %slice.194) | copy-start | bytes 43012
  302.6 8.1 %copy-start.4 = (f32[16,32,16]{2,0,1:T(8,128)S(1)}, f32[16,32,16]{2,0,1:T(8,128)}, u32[]{:S(2)}) copy-start(f32[16,32,16]{2,0,1:T(8,128)} %multiply_add_fusion.3) | copy-start | bytes 98308
  302.9 11.7 %copy-start.12 = (f32[16,32,15]{2,0,1:T(8,128)S(1)}, f32[16,32,15]{2,0,1:T(8,128)}, u32[]{:S(2)}) copy-start(f32[16,32,15]{2,0,1:T(8,128)} %slice.197) | copy-start | bytes 92164
  305.4 9.3 %copy-start.3 = (f32[16,32,32]{2,0,1:T(8,128)S(1)}, f32[16,32,32]{2,0,1:T(8,128)}, u32[]{:S(2)}) copy-start(f32[16,32,32]{2,0,1:T(8,128)} %multiply_add_fusion.4) | copy-start | bytes 196612
  313.8 35.7 %copy-start.2 = (f32[16,32,64]{2,0,1:T(8,128)S(1)}, f32[16,32,64]{2,0,1:T(8,128)}, u32[]{:S(2)}) copy-start(f32[16,32,64]{2,0,1:T(8,128)} %copy-done.1) | copy-start | bytes 393220
  318.0 38.9 %copy-start = (f32[32,1,128,128]{3,1,2,0:T(1,128)S(1)}, f32[32,1,128,128]{3,1,2,0:T(1,128)}, u32[]{:S(2)}) copy-start(f32[32,1,128,128]{3,1,2,0:T(1,128)} %fusion.2) | copy-start | bytes 6291460
  318.0 38.9 %copy-start.7 = (bf16[4,8,64,128]{3,2,1,0:T(8,128)(2,1)S(1)}, bf16[4,8,64,128]{3,2,1,0:T(8,128)(2,1)}, u32[]{:S(2)}) copy-start(bf16[4,8,64,128]{3,2,1,0:T(8,128)(2,1)} %copy-done.6) | copy-start | bytes 1572868
  354.9 4.3 copy-start.9
  354.9 4.3 copy-start.10
  354.9 4.3 copy-start.17
  533.2 181.4 %all-gather.5.cloned.1.call-start = ((), (), s32[]{:S(2)}) async-start(), calls=%async_computation.3 | async-start | bytes 17301504 | tf_op jit(solution)/shard_map/all_gather | solution.py:123
Sparse Core Ops, SparseCore 0:
  533.3 39.8 all-gather.2
  575.7 138.8 all-gather.4

commit v2 on v1

v2 whole, which is shorter than its diff:
```python
import functools

import jax
import jax.numpy as jnp
from jax import lax
from jax.experimental import pallas as pl
from jax.experimental.pallas import tpu as pltpu
from jax.sharding import Mesh
from jax.sharding import PartitionSpec as P

MESH = pl.DeviceIdType.MESH
LANES = 128
SUBS = 8
AXES = ("x", "z", "y", "core")


def shift_down(value, by):
    row = lax.broadcasted_iota(jnp.int32, value.shape, 0)
    return jnp.where(row >= by, pltpu.roll(value, by, 0), 0.0)


def tree_sum(terms):
    while len(terms) > 1:
        terms = [a + b for a, b in zip(terms[::2], terms[1::2], strict=True)]
    return terms[0]


def conv_kernel(
    x_count, z_count,
    sizes, streams, tail, taps, residue, damping, damping_tiles, direct,
    gathered,
    padded, query, gated, mixed, partial, ends, end_in, carry_out, carry_in, hidden, halo,
    halo_send, halo_recv, end_send, end_recv, carry_send, carry_recv,
    z_send, z_recv, right_send, right_recv, left_send, left_recv,
    far_a_send, far_a_recv, far_b_send, far_b_recv, local_sem,
):
    modes = residue.shape[0]
    cap = streams.shape[1]
    groups = z_count
    step_rows = cap // SUBS
    seq_count = x_count * z_count
    per_owner = max(1, modes // seq_count)
    owners = modes // per_owner
    my_x, my_z = lax.axis_index("x"), lax.axis_index("z")
    me = my_x * z_count + my_z
    valid = sizes[me]

    def seq_device(index):
        return {"x": index // z_count, "z": lax.rem(index, z_count)}

    barrier = pltpu.get_barrier_semaphore()

    @pl.loop(1, seq_count)
    def _(k):
        pl.semaphore_signal(
            barrier, inc=1, device_id=seq_device(lax.rem(me + k, seq_count)), device_id_type=MESH
        )

    pl.semaphore_wait(barrier, seq_count - 1)

    def halo_copy(distance):
        target = lax.rem(me + distance, seq_count)
        return pltpu.make_async_remote_copy(
            src_ref=tail, dst_ref=halo.at[distance - 1], send_sem=halo_send.at[distance - 1],
            recv_sem=halo_recv.at[distance - 1], device_id=seq_device(target), device_id_type=MESH,
        )

    for distance in (1, 2):
        halo_copy(distance).start()
    for distance in (1, 2):
        halo_copy(distance).wait_recv()

    row = lax.broadcasted_iota(jnp.int32, (cap, LANES), 0)
    before_size = sizes[lax.rem(me + seq_count - 1, seq_count)]

    def lanes(g):
        return pl.ds(pl.multiple_of(g * LANES, LANES), LANES)

    @pl.loop(0, groups)
    def _(g):
        at = lanes(g)
        features = []
        for p in range(3):
            last_one = jnp.where(me >= 1, halo[0, p : p + 1, at], 0.0)
            own_second = halo[0, 3 + p : 4 + p, at]
            far_last = jnp.where(me >= 2, halo[1, p : p + 1, at], 0.0)
            last_two = jnp.where(me >= 1, jnp.where(before_size >= 2, own_second, far_last), 0.0)
            padded[p, 6:7, :] = last_two
            padded[p, 7:8, :] = last_one
            padded[p, 8 : 8 + cap, :] = streams[p, :, at].astype(jnp.float32)
            features.append(
                taps[3 * p : 3 * p + 1, at] * padded[p, 8 : 8 + cap, :]
                + taps[3 * p + 1 : 3 * p + 2, at] * padded[p, 7 : 7 + cap, :]
                + taps[3 * p + 2 : 3 * p + 3, at] * padded[p, 6 : 6 + cap, :]
            )
        query[g] = features[0].astype(jnp.bfloat16).astype(jnp.float32)
        product = (features[1] * features[2]).astype(jnp.bfloat16).astype(jnp.float32)
        gated[g] = jnp.where(row < valid, product, 0.0)

    def mode_rows(ref, at):
        return [jnp.broadcast_to(ref[m : m + 1, at], (SUBS, LANES)) for m in range(modes)]

    @pl.loop(0, groups)
    def _(g):
        at = lanes(g)
        decay = [jnp.exp(-d) for d in mode_rows(damping, at)]
        weight = mode_rows(residue, at)

        def step(i, states):
            u = gated[g, pl.ds(i, SUBS, stride=step_rows), :]
            return tuple(a * h + r * u for a, h, r in zip(decay, states, weight, strict=True))

        zero = jnp.zeros((SUBS, LANES), jnp.float32)
        states = lax.fori_loop(0, step_rows, step, (zero,) * modes, unroll=4)
        left_over = (cap - valid).astype(jnp.float32)
        for m in range(modes):
            rate = damping[m : m + 1, at]
            total = states[m]
            for by in (1, 2, 4):
                total = total + jnp.exp(-rate * (step_rows * by)) * shift_down(total, by)
            partial[g, m] = shift_down(total, 1)
            ends[m, pl.ds(g, 1), :] = total[SUBS - 1 : SUBS, :] * jnp.exp(rate * left_over)

    def end_copy(owner):
        return pltpu.make_async_remote_copy(
            src_ref=ends.at[pl.ds(owner * per_owner, per_owner)], dst_ref=end_in.at[me],
            send_sem=end_send.at[owner], recv_sem=end_recv.at[me],
            device_id=seq_device(owner), device_id_type=MESH,
        )

    def end_arrival(source):
        return pltpu.make_async_remote_copy(
            src_ref=ends.at[pl.ds(0, per_owner)], dst_ref=end_in.at[source],
            send_sem=end_send.at[0], recv_sem=end_recv.at[source],
            device_id=seq_device(source), device_id_type=MESH,
        )

    def carry_copy(target):
        return pltpu.make_async_remote_copy(
            src_ref=carry_out.at[target], dst_ref=carry_in.at[me],
            send_sem=carry_send.at[target], recv_sem=carry_recv.at[me],
            device_id=seq_device(target), device_id_type=MESH,
        )

    def carry_arrival(owner):
        return pltpu.make_async_remote_copy(
            src_ref=carry_out.at[0], dst_ref=carry_in.at[owner],
            send_sem=carry_send.at[0], recv_sem=carry_recv.at[owner],
            device_id=seq_device(owner), device_id_type=MESH,
        )

    @pl.loop(0, owners)
    def _(k):
        owner = lax.rem(me + k, owners)

        @pl.when(owner != me)
        def _():
            end_copy(owner).start()

    @pl.when(me < owners)
    def _():
        end_in[me] = ends[pl.ds(me * per_owner, per_owner)]

        @pl.loop(0, seq_count)
        def _(source):
            @pl.when(source != me)
            def _():
                end_arrival(source).wait_recv()

        rate = damping_tiles[pl.ds(me * per_owner, per_owner)]

        def advance(source, carry):
            carry_out[source] = carry
            return jnp.exp(-rate * sizes[source].astype(jnp.float32)) * carry + end_in[source]

        lax.fori_loop(0, seq_count, advance, jnp.zeros_like(rate))
        carry_in[me] = carry_out[me]

        @pl.loop(0, seq_count)
        def _(target):
            @pl.when(target != me)
            def _():
                carry_copy(target).start()

    @pl.loop(0, owners)
    def _(owner):
        @pl.when(owner != me)
        def _():
            carry_arrival(owner).wait_recv()

    def z_copy(g):
        return pltpu.make_async_remote_copy(
            src_ref=hidden.at[g], dst_ref=gathered.at[me], send_sem=z_send.at[g],
            recv_sem=z_recv.at[my_z], device_id={"z": g}, device_id_type=MESH,
        )

    def z_arrival(z):
        return pltpu.make_async_remote_copy(
            src_ref=hidden.at[0], dst_ref=gathered.at[my_x * z_count + z], send_sem=z_send.at[0],
            recv_sem=z_recv.at[z], device_id={"z": z}, device_id_type=MESH,
        )

    own_copy = pltpu.make_async_copy(hidden.at[my_z], gathered.at[me], local_sem)

    @pl.loop(0, groups)
    def _(k):
        g = lax.rem(my_z + 1 + k, groups)
        at = lanes(g)
        rates = mode_rows(damping, at)
        decay = [jnp.exp(-d) for d in rates]
        weight = mode_rows(residue, at)
        sub = lax.broadcasted_iota(jnp.int32, (SUBS, LANES), 0).astype(jnp.float32) * step_rows
        start = tuple(
            partial[g, m]
            + jnp.exp(-rates[m] * sub)
            * carry_in[m // per_owner, m % per_owner, pl.ds(g, 1), :]
            for m in range(modes)
        )

        def step(i, states):
            rows = pl.ds(i, SUBS, stride=step_rows)
            u = gated[g, rows, :]
            states = tuple(a * h + r * u for a, h, r in zip(decay, states, weight, strict=True))
            mixed[rows, :] = tree_sum(list(states))
            return states

        lax.fori_loop(0, step_rows, step, start, unroll=4)
        conv = mixed[...] + direct[0:1, at] * gated[g]
        hidden[g] = (query[g] * conv).astype(jnp.bfloat16)

        @pl.when(g != my_z)
        def _():
            z_copy(g).start()

        @pl.when(g == my_z)
        def _():
            own_copy.start()

    right, left = lax.rem(my_x + 1, x_count), lax.rem(my_x + x_count - 1, x_count)
    half = cap // 2

    def x_copy(source_x, z, to, send, recv, first, rows):
        slot = source_x * z_count + z
        view = gathered.at[slot, pl.ds(first, rows)]
        return pltpu.make_async_remote_copy(
            src_ref=view, dst_ref=view, send_sem=send.at[z], recv_sem=recv.at[z],
            device_id={"x": to}, device_id_type=MESH,
        )

    def to_right(source_x, z):
        return x_copy(source_x, z, right, right_send, right_recv, 0, cap)

    def to_left(source_x, z):
        return x_copy(source_x, z, left, left_send, left_recv, 0, cap)

    def far_right(source_x, z):
        return x_copy(source_x, z, right, far_a_send, far_a_recv, 0, half)

    def far_left(source_x, z):
        return x_copy(source_x, z, left, far_b_send, far_b_recv, half, half)

    @pl.loop(0, z_count)
    def _(k):
        z = lax.rem(my_z + 2 * z_count - 1 - k, z_count)

        @pl.when(z != my_z)
        def _():
            z_arrival(z).wait_recv()

        @pl.when(z == my_z)
        def _():
            own_copy.wait()

        to_right(my_x, z).start()
        to_left(my_x, z).start()

    @pl.loop(0, z_count)
    def _(k):
        z = lax.rem(my_z + 2 * z_count - 1 - k, z_count)
        to_right(left, z).wait_recv()
        far_right(left, z).start()
        to_left(right, z).wait_recv()
        far_left(right, z).start()

    opposite = lax.rem(my_x + 2, x_count)

    @pl.loop(0, z_count)
    def _(z):
        far_right(opposite, z).wait_recv()
        far_left(opposite, z).wait_recv()
        far_right(left, z).wait_send()
        far_left(right, z).wait_send()
        to_right(my_x, z).wait_send()
        to_left(my_x, z).wait_send()

        @pl.when(z != my_z)
        def _():
            z_copy(z).wait_send()

    for distance in (1, 2):
        halo_copy(distance).wait_send()

    @pl.loop(0, owners)
    def _(owner):
        @pl.when(owner != me)
        def _():
            end_copy(owner).wait_send()

    @pl.when(me < owners)
    def _():
        @pl.loop(0, seq_count)
        def _(target):
            @pl.when(target != me)
            def _():
                carry_copy(target).wait_send()


def conv_call(dims, streams, tail, sizes, taps, residue, damping, direct):
    x_count, z_count = dims["x"], dims["z"]
    cap, width = streams.shape[1:]
    modes = residue.shape[0]
    seq_count = x_count * z_count
    per_owner = max(1, modes // seq_count)
    owners = modes // per_owner
    f32, bf16 = jnp.float32, jnp.bfloat16
    dma = pltpu.SemaphoreType.DMA
    vmem = pl.BlockSpec(memory_space=pltpu.VMEM)
    return pl.pallas_call(
        functools.partial(conv_kernel, x_count, z_count),
        out_shape=jax.ShapeDtypeStruct((seq_count, cap, LANES), bf16),
        in_specs=[pl.BlockSpec(memory_space=pltpu.SMEM)] + [vmem] * 7,
        out_specs=pl.BlockSpec(memory_space=pl.ANY),
        scratch_shapes=[
            pltpu.VMEM((3, cap + SUBS, LANES), f32),
            pltpu.VMEM((z_count, cap, LANES), f32),
            pltpu.VMEM((z_count, cap, LANES), f32),
            pltpu.VMEM((cap, LANES), f32),
            pltpu.VMEM((z_count, modes, SUBS, LANES), f32),
            pltpu.VMEM((modes, z_count, LANES), f32),
            pltpu.VMEM((seq_count, per_owner, z_count, LANES), f32),
            pltpu.VMEM((seq_count, per_owner, z_count, LANES), f32),
            pltpu.VMEM((owners, per_owner, z_count, LANES), f32),
            pltpu.VMEM((z_count, cap, LANES), bf16),
            pltpu.VMEM((2,) + tail.shape, f32),
            dma((2,)), dma((2,)),
            dma((owners,)), dma((seq_count,)), dma((seq_count,)), dma((owners,)),
        ]
        + [dma((z_count,))] * 10
        + [dma],
        compiler_params=pltpu.CompilerParams(
            collective_id=0, has_side_effects=True, vmem_limit_bytes=24 << 20
        ),
        name="conv_shuffle",
    )(
        sizes, streams, tail, taps, residue, damping,
        damping.reshape(modes, width // LANES, LANES), direct,
    )


def select_kernel(old_start, new_start, counts, pieces, chosen, sequence):
    seq_count, cap, _ = pieces.shape

    @pl.loop(0, seq_count)
    def _(s):
        sequence[pl.ds(old_start[s], cap), :] = pieces[s].astype(jnp.float32)

    row = lax.broadcasted_iota(jnp.int32, (cap, LANES), 0)

    @pl.loop(0, chosen.shape[0])
    def _(k):
        rows = sequence[pl.ds(new_start[k], cap), :]
        chosen[k] = jnp.where(row < counts[k], rows, 0.0).astype(jnp.bfloat16)


def select_call(dims, seq_len, pieces, old_start, new_start, counts):
    cap = pieces.shape[1]
    smem = pl.BlockSpec(memory_space=pltpu.SMEM)
    vmem = pl.BlockSpec(memory_space=pltpu.VMEM)
    return pl.pallas_call(
        select_kernel,
        out_shape=jax.ShapeDtypeStruct((dims["z"], cap, LANES), jnp.bfloat16),
        in_specs=[smem] * 3 + [vmem],
        out_specs=vmem,
        scratch_shapes=[pltpu.VMEM((seq_len + cap, LANES), jnp.float32)],
        compiler_params=pltpu.CompilerParams(vmem_limit_bytes=24 << 20),
        name="reorder_rows",
    )(old_start, new_start, counts, pieces)


def spread_kernel(
    x_count, z_count, y_count,
    chosen, rows_out,
    z_send, z_recv, right_send, right_recv, left_send, left_recv,
    far_a_send, far_a_recv, far_b_send, far_b_recv, core_send, core_recv, local_sem,
):
    cap = rows_out.shape[0]
    my_z, my_y, my_core = lax.axis_index("z"), lax.axis_index("y"), lax.axis_index("core")
    right, left = lax.rem(my_y + 1, y_count), lax.rem(my_y + y_count - 1, y_count)
    opposite = lax.rem(my_y + 2, y_count)
    other = 1 - my_core
    half = cap // 2

    barrier = pltpu.get_barrier_semaphore()

    @pl.loop(1, z_count)
    def _(k):
        pl.semaphore_signal(
            barrier, inc=1, device_id={"z": lax.rem(my_z + k, z_count)}, device_id_type=MESH
        )

    for to in ({"y": right}, {"y": left}, {"core": other}):
        pl.semaphore_signal(barrier, inc=1, device_id=to, device_id_type=MESH)
    pl.semaphore_wait(barrier, z_count + 2)

    def columns(y, core, z):
        return pl.ds(pl.multiple_of(((y * 2 + core) * z_count + z) * LANES, LANES), LANES)

    def z_copy(z):
        return pltpu.make_async_remote_copy(
            src_ref=chosen.at[z], dst_ref=rows_out.at[:, columns(my_y, my_core, my_z)],
            send_sem=z_send.at[z], recv_sem=z_recv.at[my_z], device_id={"z": z}, device_id_type=MESH,
        )

    def z_arrival(z):
        return pltpu.make_async_remote_copy(
            src_ref=chosen.at[0], dst_ref=rows_out.at[:, columns(my_y, my_core, z)],
            send_sem=z_send.at[0], recv_sem=z_recv.at[z], device_id={"z": z}, device_id_type=MESH,
        )

    own_copy = pltpu.make_async_copy(
        chosen.at[my_z], rows_out.at[:, columns(my_y, my_core, my_z)], local_sem
    )
    own_copy.start()

    @pl.loop(1, z_count)
    def _(k):
        z_copy(lax.rem(my_z + k, z_count)).start()

    def onward(y, core, z, to, send, recv, first, rows):
        view = rows_out.at[pl.ds(first, rows), columns(y, core, z)]
        return pltpu.make_async_remote_copy(
            src_ref=view, dst_ref=view, send_sem=send, recv_sem=recv,
            device_id=to, device_id_type=MESH,
        )

    def to_right(y, z):
        return onward(y, my_core, z, {"y": right}, right_send.at[z], right_recv.at[z], 0, cap)

    def to_left(y, z):
        return onward(y, my_core, z, {"y": left}, left_send.at[z], left_recv.at[z], 0, cap)

    def far_right(y, z):
        return onward(y, my_core, z, {"y": right}, far_a_send.at[z], far_a_recv.at[z], 0, half)

    def far_left(y, z):
        return onward(y, my_core, z, {"y": left}, far_b_send.at[z], far_b_recv.at[z], half, half)

    def to_core(y, core, z):
        return onward(y, core, z, {"core": other}, core_send.at[y, z], core_recv.at[y, z], 0, cap)

    def arrival_order(k):
        return lax.rem(my_z + z_count - k, z_count)

    @pl.loop(0, z_count)
    def _(k):
        z = arrival_order(k)

        @pl.when(z != my_z)
        def _():
            z_arrival(z).wait_recv()

        @pl.when(z == my_z)
        def _():
            own_copy.wait()

        to_right(my_y, z).start()
        to_left(my_y, z).start()
        to_core(my_y, my_core, z).start()

    @pl.loop(0, z_count)
    def _(k):
        z = arrival_order(k)
        to_right(left, z).wait_recv()
        far_right(left, z).start()
        to_core(left, my_core, z).start()
        to_left(right, z).wait_recv()
        far_left(right, z).start()
        to_core(right, my_core, z).start()

    @pl.loop(0, z_count)
    def _(k):
        z = arrival_order(k)
        far_right(opposite, z).wait_recv()
        far_left(opposite, z).wait_recv()
        to_core(opposite, my_core, z).start()

    @pl.loop(0, z_count)
    def _(z):
        for y in range(y_count):
            to_core(y, other, z).wait_recv()
            to_core(y, my_core, z).wait_send()
        to_right(my_y, z).wait_send()
        to_left(my_y, z).wait_send()
        far_right(left, z).wait_send()
        far_left(right, z).wait_send()

        @pl.when(z != my_z)
        def _():
            z_copy(z).wait_send()


def spread_call(dims, chosen):
    z_count, cap, _ = chosen.shape
    y_count = dims["y"]
    dma = pltpu.SemaphoreType.DMA
    return pl.pallas_call(
        functools.partial(spread_kernel, dims["x"], z_count, y_count),
        out_shape=jax.ShapeDtypeStruct((cap, y_count * 2 * z_count * LANES), jnp.bfloat16),
        in_specs=[pl.BlockSpec(memory_space=pltpu.VMEM)],
        out_specs=pl.BlockSpec(memory_space=pl.ANY),
        scratch_shapes=[dma((z_count,))] * 10 + [dma((y_count, z_count))] * 2 + [dma],
        compiler_params=pltpu.CompilerParams(collective_id=1, has_side_effects=True),
        name="spread_rows",
    )(chosen)


def running_ends(sizes):
    index = jnp.arange(sizes.shape[0], dtype=jnp.int32)
    return jnp.sum(jnp.where(index[None, :] <= index[:, None], sizes[None, :], 0), axis=1)


def shards(
    dims,
    input_triple_streams,
    former_piece_sizes,
    updated_piece_sizes,
    remaining_indices,
    short_causal_filters,
    pole_coefficients,
    pole_damping,
    direct_coefficient,
    final_projector,
):
    x_count, z_count = dims["x"], dims["z"]
    seq_count = x_count * z_count
    my_x = lax.axis_index("x")
    me = my_x * z_count + lax.axis_index("z")
    cap, _, width = input_triple_streams.shape
    seq_len = cap * 4 // 5 * seq_count

    projector = lax.all_gather(final_projector, ("x", "z"), axis=0, tiled=True)

    last = former_piece_sizes[me] - 1
    last_row = lax.dynamic_slice_in_dim(input_triple_streams, last, 1, 0)[0]
    second_row = lax.dynamic_slice_in_dim(input_triple_streams, jnp.maximum(last - 1, 0), 1, 0)[0]
    tail = jnp.concatenate([last_row, second_row, last_row[:2]], axis=0).astype(jnp.float32)

    pieces = conv_call(
        dims,
        jnp.transpose(input_triple_streams, (1, 0, 2)),
        tail,
        former_piece_sizes,
        short_causal_filters.reshape(9, width),
        pole_coefficients,
        pole_damping,
        direct_coefficient[None, :],
    )

    old_start = running_ends(former_piece_sizes) - former_piece_sizes
    new_start = running_ends(updated_piece_sizes) - updated_piece_sizes
    device_names = my_x * z_count + jnp.arange(z_count, dtype=jnp.int32)
    partner_table = (remaining_indices[None, :] == device_names[:, None]).astype(jnp.int32)
    start_dev = jnp.sum(partner_table * new_start[None, :], axis=1)
    count_dev = jnp.sum(partner_table * updated_piece_sizes[None, :], axis=1)
    chosen = select_call(dims, seq_len, pieces, old_start, start_dev, count_dev)

    hidden = spread_call(dims, chosen)
    projected = jnp.dot(hidden, projector, preferred_element_type=jnp.float32)
    return projected.astype(jnp.bfloat16)


def solution(mesh):
    grid = (4, mesh.shape["seq"] // 4, mesh.shape["chan"] // 2, 2)
    dims = dict(zip(AXES, grid, strict=True))
    rows, channels = ("x", "z"), ("y", "core")
    return jax.shard_map(
        functools.partial(shards, dims),
        mesh=Mesh(mesh.devices.reshape(grid), AXES),
        in_specs=(
            P(rows, None, channels),
            P(),
            P(),
            P(),
            P(None, None, channels),
            P(None, channels),
            P(None, channels),
            P(channels),
            P(rows, channels),
        ),
        out_specs=P(rows, channels),
        check_vma=False,
    )
```

time: 742 us -> 200 us (0.27)
  local copies, waits for them, and re-layouts: 245 us -> 9.25 us
  waiting for transfers between devices: 189 us -> 35.5 us
  loops' own time: 125 us -> 0 us
  Pallas kernels: 0 us -> 123 us
  matrix products: 62.9 us -> 11.5 us
  other arithmetic: 53.2 us -> 3.07 us
  blocking collectives: 32.4 us -> 0 us
  starting transfers between devices: 11.4 us -> 0.01 us
    all_gather x2 -> x1, waiting for transfers between devices: 181 us -> 34.7 us  [shards(): projector = lax.all_gather(final_projector, ('x', 'z'), axis=0, tiled=True)]
    another operation x2 -> x0, loops' own time: 125 us -> none  [the longest x1 63.5 us: shards(): outgoing = lax.fori_loop(0, seq_count, pick, outgoing_init)]
    pallas_call x0 -> x3, Pallas kernels: none -> 123 us  [the longest x1 79.3 us: conv_call(): pl.pallas_call(functools.partial(conv_kernel, x_count, z_count), out_shap...]
    dynamic_slice x131 -> x2, local copies, waits for them, and re-layouts: 89.8 us -> 2.15 us  [the longest x1 1.24 us: shards(): last = former_piece_sizes[me] - 1]
    dot_general x5 -> x1, matrix products: 62.9 us -> 11.5 us  [shards(): projected = jnp.dot(hidden, projector, preferred_element_type=jnp.float32)]
    slice x18 -> x1, local copies, waits for them, and re-layouts: 48.5 us -> 0.01 us  [shards(): last_row[:2]]
    dynamic_update_slice x64 -> x0, local copies, waits for them, and re-layouts: 44.7 us -> none  [the longest x32 29.9 us: place(): return lax.dynamic_update_slice_in_dim(current, piece, old_start[source], 2)]
    all_to_all x1 -> x0, blocking collectives: 32.4 us -> none  [shards(): lax.all_to_all(outgoing, 'seq', split_axis=1, concat_axis=0, tiled=True)]
  transfers between devices with their start and end apart: 3 -> 1, of which waited for: 3 -> 1; matrix products, arithmetic and copies ran while one was open for 9% -> 3% of each run, Pallas kernels for 0% -> 62%
where the time goes in v2:
time: 200 us; the launch traced here: 198 us
  Pallas kernels  123 us (62%)
  waiting for transfers between devices  35.5 us (18%)
  between operations  15.5 us (8%)
  matrix products  11.5 us (6%)
  local copies, waits for them, and re-layouts  9.25 us (5%)
  other arithmetic  3.07 us (2%)
    pallas_call x1, Pallas kernels, conv_call(): pl.pallas_call(functools.partial(conv_kernel, x_count, z_count), out_shap...  79.3 us
    pallas_call x1, Pallas kernels, spread_call(): pl.pallas_call(functools.partial(spread_kernel, dims['x'], z_count, y_cou...  42.4 us
    all_gather x1, waiting for transfers between devices, shards(): projector = lax.all_gather(final_projector, ('x', 'z'), axis=0, tiled=True)  34.7 us
    dot_general x1, matrix products, shards(): projected = jnp.dot(hidden, projector, preferred_element_type=jnp.float32)  11.5 us
    unnamed x20, local copies, waits for them, and re-layouts  6.27 us
  transfers between devices with their start and end apart: 1, of which 1 were waited for; matrix products, arithmetic and copies ran while one was open for 3% of the time, Pallas kernels for 62%

profile of v2, /device:TPU:32, one launch (start us, length us, event | category | flops | bytes accessed | tf_op | source)
XLA Modules:
  0.0 197.6 jit_solution(2538242006773089151)
XLA Ops:
  6.5 0.0 all-gather.2.cloned.1.call-start
  6.5 0.7 all-gather.2.cloned.1.call-update
  7.3 1.2 dynamic_slice.9
  10.5 0.9 constant_dynamic-slice_fusion
  11.4 0.8 select_reduce_fusion
  12.2 0.7 sub.15
  12.8 0.8 select_reduce_fusion.1
  13.6 0.7 sub.14.old_start
  14.3 0.8 reshape.23.taps
  15.1 0.9 copy.15
  16.0 0.0 copy-start.1
  16.0 1.5 copy-done.1
  17.5 0.8 copy-done.2
  18.4 0.8 copy-done.3
  19.2 0.7 copy-done.4
  19.9 0.7 copy-done.5
  20.6 79.3 %conv_shuffle.1.pieces = bf16[32,320,128]{2,1,0:T(8,128)(2,1)S(1)} custom-call(s32[32]{0:T(128)S(1)} %copy-done.5, bf16[3,320,1024]{2,1,0:T(8,128)(2,1)S(1)} %bitcast.17, f32[8,1024]{1,0:T(8,128)S(1)} %maximum_convert_fusion.tail, f32[9,1024]{1,0:T(8,128)S(1)} %reshape.23.taps, f32[16,1024]{1,0:T(8,128)S(1)} %copy-done.3, f32[16,1024]{1,0:T(8,128)S(1)} %copy-done.2, ...), custom_call_target="tpu_custom_call" | custom-call | tf_op jit(solution)/shard_map/conv_shuffle/pallas_call | solution.py:328
  99.9 0.2 fusion.1
  100.1 1.2 reorder_rows.1.chosen
  101.3 0.0 copy-start
  101.3 0.8 copy-done
  102.1 42.4 %spread_rows.1 = bf16[320,8192]{1,0:T(8,128)(2,1)} custom-call(bf16[8,320,128]{2,1,0:T(8,128)(2,1)} %copy-done), custom_call_target="tpu_custom_call" | custom-call | tf_op jit(solution)/shard_map/spread_rows/pallas_call | solution.py:516
  144.6 34.7 %all-gather.2.cloned.1.call-done = bf16[8192,1024]{1,0:T(8,128)(2,1)} async-done(((bf16[256,1024]{1,0:T(8,128)(2,1)}), bf16[8192,1024]{1,0:T(8,128)(2,1)}) %all-gather.2.cloned.1.call-update) | async-done | bytes 16777232 | tf_op jit(solution)/shard_map/all_gather | solution.py:551
  179.3 11.5 %convolution_convert_fusion = bf16[320,1024]{1,0:T(8,128)(2,1)} fusion(bf16[320,8192]{1,0:T(8,128)(2,1)} %spread_rows.1, bf16[8192,1024]{1,0:T(8,128)(2,1)} %all-gather.2.cloned.1.call-done), kind=kOutput, calls=%fused_computation | convolution fusion | flops 5369036800 | bytes 22675456 | tf_op jit(solution)/shard_map/dot_general | solution.py:578
  (14 shorter events, 0.1 us)
Async XLA Ops:
  6.5 93.4 %copy-start.6 = (s32[28]{0:T(128)S(1)}, s32[28]{0:T(128)}, u32[]{:S(2)}) copy-start(s32[28]{0:T(128)} %param.11) | copy-start | bytes 340
  6.5 93.4 %copy-start.7 = (s32[28]{0:T(128)S(1)}, s32[28]{0:T(128)}, u32[]{:S(2)}) copy-start(s32[28]{0:T(128)} %param.12) | copy-start | bytes 340
  6.5 172.8 %all-gather.2.cloned.1.call-start = ((), (), s32[]{:S(2)}) async-start(), calls=%async_computation | async-start | bytes 17301504 | tf_op jit(solution)/shard_map/all_gather | solution.py:551
  16.0 1.5 copy-start.1
  17.5 0.8 copy-start.2
  18.4 0.8 copy-start.3
  19.2 0.7 copy-start.4
  19.9 0.7 copy-start.5
  101.3 0.8 copy-start
Sparse Core Ops, SparseCore 0:
  10.0 169.3 all-gather.1

commit v3 on v2

--- a/solution.py
+++ b/solution.py
@@ -27,9 +27,9 @@
 
 def conv_kernel(
     x_count, z_count,
-    sizes, streams, tail, taps, residue, damping, damping_tiles, direct,
+    sizes, streams, taps, residue, damping, direct,
     gathered,
-    padded, query, gated, mixed, partial, ends, end_in, carry_out, carry_in, hidden, halo,
+    padded, tail, rates_own, query, gated, mixed, partial, ends, end_in, carry_out, carry_in, hidden, halo,
     halo_send, halo_recv, end_send, end_recv, carry_send, carry_recv,
     z_send, z_recv, right_send, right_recv, left_send, left_recv,
     far_a_send, far_a_recv, far_b_send, far_b_recv, local_sem,
@@ -48,6 +48,9 @@
     def seq_device(index):
         return {"x": index // z_count, "z": lax.rem(index, z_count)}
 
+    def lanes(g):
+        return pl.ds(pl.multiple_of(g * LANES, LANES), LANES)
+
     barrier = pltpu.get_barrier_semaphore()
 
     @pl.loop(1, seq_count)
@@ -56,6 +59,17 @@
             barrier, inc=1, device_id=seq_device(lax.rem(me + k, seq_count)), device_id_type=MESH
         )
 
+    last = SUBS - 1 + valid
+    second = jnp.maximum(last - 1, SUBS)
+
+    @pl.loop(0, groups)
+    def _(g):
+        for p in range(3):
+            padded[p, g, SUBS : SUBS + cap, :] = streams[p, :, lanes(g)].astype(jnp.float32)
+            tail[g, p : p + 1, :] = padded[p, g, pl.ds(last, 1), :]
+            tail[g, 3 + p : 4 + p, :] = padded[p, g, pl.ds(second, 1), :]
+        tail[g, 6:8, :] = jnp.zeros((2, LANES), jnp.float32)
+
     pl.semaphore_wait(barrier, seq_count - 1)
 
     def halo_copy(distance):
@@ -72,26 +86,22 @@
 
     row = lax.broadcasted_iota(jnp.int32, (cap, LANES), 0)
     before_size = sizes[lax.rem(me + seq_count - 1, seq_count)]
-
-    def lanes(g):
-        return pl.ds(pl.multiple_of(g * LANES, LANES), LANES)
 
     @pl.loop(0, groups)
     def _(g):
         at = lanes(g)
         features = []
         for p in range(3):
-            last_one = jnp.where(me >= 1, halo[0, p : p + 1, at], 0.0)
-            own_second = halo[0, 3 + p : 4 + p, at]
-            far_last = jnp.where(me >= 2, halo[1, p : p + 1, at], 0.0)
+            last_one = jnp.where(me >= 1, halo[0, g, p : p + 1, :], 0.0)
+            own_second = halo[0, g, 3 + p : 4 + p, :]
+            far_last = jnp.where(me >= 2, halo[1, g, p : p + 1, :], 0.0)
             last_two = jnp.where(me >= 1, jnp.where(before_size >= 2, own_second, far_last), 0.0)
-            padded[p, 6:7, :] = last_two
-            padded[p, 7:8, :] = last_one
-            padded[p, 8 : 8 + cap, :] = streams[p, :, at].astype(jnp.float32)
+            padded[p, g, 6:7, :] = last_two
+            padded[p, g, 7:8, :] = last_one
             features.append(
-                taps[3 * p : 3 * p + 1, at] * padded[p, 8 : 8 + cap, :]
-                + taps[3 * p + 1 : 3 * p + 2, at] * padded[p, 7 : 7 + cap, :]
-                + taps[3 * p + 2 : 3 * p + 3, at] * padded[p, 6 : 6 + cap, :]
+                taps[p, 0:1, at] * padded[p, g, 8 : 8 + cap, :]
+                + taps[p, 1:2, at] * padded[p, g, 7 : 7 + cap, :]
+                + taps[p, 2:3, at] * padded[p, g, 6 : 6 + cap, :]
             )
         query[g] = features[0].astype(jnp.bfloat16).astype(jnp.float32)
         product = (features[1] * features[2]).astype(jnp.bfloat16).astype(jnp.float32)
@@ -160,6 +170,13 @@
     @pl.when(me < owners)
     def _():
         end_in[me] = ends[pl.ds(me * per_owner, per_owner)]
+        mode = lax.broadcasted_iota(jnp.int32, (modes, LANES), 0)
+        for j in range(per_owner):
+            for g in range(groups):
+                block = damping[:, g * LANES : (g + 1) * LANES]
+                rates_own[j, g : g + 1, :] = jnp.sum(
+                    jnp.where(mode == me * per_owner + j, block, 0.0), axis=0, keepdims=True
+                )
 
         @pl.loop(0, seq_count)
         def _(source):
@@ -167,13 +184,13 @@
             def _():
                 end_arrival(source).wait_recv()
 
-        rate = damping_tiles[pl.ds(me * per_owner, per_owner)]
+        rate = rates_own[...]
 
         def advance(source, carry):
             carry_out[source] = carry
             return jnp.exp(-rate * sizes[source].astype(jnp.float32)) * carry + end_in[source]
 
-        lax.fori_loop(0, seq_count, advance, jnp.zeros_like(rate))
+        lax.fori_loop(0, seq_count, advance, jnp.zeros_like(rate), unroll=8)
         carry_in[me] = carry_out[me]
 
         @pl.loop(0, seq_count)
@@ -259,28 +276,35 @@
     def far_left(source_x, z):
         return x_copy(source_x, z, left, far_b_send, far_b_recv, half, half)
 
-    @pl.loop(0, z_count)
+    def arrival_order(k):
+        return lax.rem(my_z + 2 * z_count - 1 - k, z_count)
+
+    lag = min(2, z_count)
+
+    @pl.loop(0, z_count + lag)
     def _(k):
-        z = lax.rem(my_z + 2 * z_count - 1 - k, z_count)
-
-        @pl.when(z != my_z)
-        def _():
-            z_arrival(z).wait_recv()
-
-        @pl.when(z == my_z)
-        def _():
-            own_copy.wait()
-
-        to_right(my_x, z).start()
-        to_left(my_x, z).start()
-
-    @pl.loop(0, z_count)
-    def _(k):
-        z = lax.rem(my_z + 2 * z_count - 1 - k, z_count)
-        to_right(left, z).wait_recv()
-        far_right(left, z).start()
-        to_left(right, z).wait_recv()
-        far_left(right, z).start()
+        @pl.when(k < z_count)
+        def _():
+            z = arrival_order(k)
+
+            @pl.when(z != my_z)
+            def _():
+                z_arrival(z).wait_recv()
+
+            @pl.when(z == my_z)
+            def _():
+                own_copy.wait()
+
+            to_right(my_x, z).start()
+            to_left(my_x, z).start()
+
+        @pl.when(k >= lag)
+        def _():
+            z = arrival_order(k - lag)
+            to_right(left, z).wait_recv()
+            far_right(left, z).start()
+            to_left(right, z).wait_recv()
+            far_left(right, z).start()
 
     opposite = lax.rem(my_x + 2, x_count)
 
@@ -315,7 +339,7 @@
                 carry_copy(target).wait_send()
 
 
-def conv_call(dims, streams, tail, sizes, taps, residue, damping, direct):
+def conv_call(dims, streams, sizes, taps, residue, damping, direct):
     x_count, z_count = dims["x"], dims["z"]
     cap, width = streams.shape[1:]
     modes = residue.shape[0]
@@ -328,10 +352,12 @@
     return pl.pallas_call(
         functools.partial(conv_kernel, x_count, z_count),
         out_shape=jax.ShapeDtypeStruct((seq_count, cap, LANES), bf16),
-        in_specs=[pl.BlockSpec(memory_space=pltpu.SMEM)] + [vmem] * 7,
+        in_specs=[pl.BlockSpec(memory_space=pltpu.SMEM)] + [vmem] * 5,
         out_specs=pl.BlockSpec(memory_space=pl.ANY),
         scratch_shapes=[
-            pltpu.VMEM((3, cap + SUBS, LANES), f32),
+            pltpu.VMEM((3, z_count, cap + SUBS, LANES), f32),
+            pltpu.VMEM((z_count, SUBS, LANES), f32),
+            pltpu.VMEM((per_owner, z_count, LANES), f32),
             pltpu.VMEM((z_count, cap, LANES), f32),
             pltpu.VMEM((z_count, cap, LANES), f32),
             pltpu.VMEM((cap, LANES), f32),
@@ -341,7 +367,7 @@
             pltpu.VMEM((seq_count, per_owner, z_count, LANES), f32),
             pltpu.VMEM((owners, per_owner, z_count, LANES), f32),
             pltpu.VMEM((z_count, cap, LANES), bf16),
-            pltpu.VMEM((2,) + tail.shape, f32),
+            pltpu.VMEM((2, z_count, SUBS, LANES), f32),
             dma((2,)), dma((2,)),
             dma((owners,)), dma((seq_count,)), dma((seq_count,)), dma((owners,)),
         ]
@@ -351,93 +377,132 @@
             collective_id=0, has_side_effects=True, vmem_limit_bytes=24 << 20
         ),
         name="conv_shuffle",
-    )(
-        sizes, streams, tail, taps, residue, damping,
-        damping.reshape(modes, width // LANES, LANES), direct,
-    )
-
-
-def select_kernel(old_start, new_start, counts, pieces, chosen, sequence):
+    )(sizes, streams, taps, residue, damping, direct)
+
+
+def select_kernel(z_count, former, updated, remaining, pieces, chosen, sequence):
     seq_count, cap, _ = pieces.shape
 
-    @pl.loop(0, seq_count)
-    def _(s):
-        sequence[pl.ds(old_start[s], cap), :] = pieces[s].astype(jnp.float32)
-
+    def place(s, start):
+        sequence[pl.ds(start, cap), :] = pieces[s].astype(jnp.float32)
+        return start + former[s]
+
+    lax.fori_loop(0, seq_count, place, 0)
     row = lax.broadcasted_iota(jnp.int32, (cap, LANES), 0)
-
-    @pl.loop(0, chosen.shape[0])
-    def _(k):
-        rows = sequence[pl.ds(new_start[k], cap), :]
-        chosen[k] = jnp.where(row < counts[k], rows, 0.0).astype(jnp.bfloat16)
-
-
-def select_call(dims, seq_len, pieces, old_start, new_start, counts):
+    first = lax.axis_index("x") * z_count
+    chosen[...] = jnp.zeros_like(chosen)
+
+    def pick(k, start):
+        own = remaining[k] - first
+
+        @pl.when(jnp.logical_and(own >= 0, own < z_count))
+        def _():
+            rows = sequence[pl.ds(start, cap), :]
+            chosen[own] = jnp.where(row < updated[k], rows, 0.0).astype(jnp.bfloat16)
+
+        return start + updated[k]
+
+    lax.fori_loop(0, updated.shape[0], pick, 0)
+
+
+def select_call(dims, seq_len, pieces, former, updated, remaining):
     cap = pieces.shape[1]
     smem = pl.BlockSpec(memory_space=pltpu.SMEM)
     vmem = pl.BlockSpec(memory_space=pltpu.VMEM)
     return pl.pallas_call(
-        select_kernel,
+        functools.partial(select_kernel, dims["z"]),
         out_shape=jax.ShapeDtypeStruct((dims["z"], cap, LANES), jnp.bfloat16),
         in_specs=[smem] * 3 + [vmem],
         out_specs=vmem,
         scratch_shapes=[pltpu.VMEM((seq_len + cap, LANES), jnp.float32)],
         compiler_params=pltpu.CompilerParams(vmem_limit_bytes=24 << 20),
         name="reorder_rows",
-    )(old_start, new_start, counts, pieces)
-
-
-def spread_kernel(
+    )(former, updated, remaining, pieces)
+
+
+def project_kernel(
     x_count, z_count, y_count,
-    chosen, rows_out,
+    chosen, projector, out,
+    rows_in, own_sum, partial_out, partial_in,
     z_send, z_recv, right_send, right_recv, left_send, left_recv,
-    far_a_send, far_a_recv, far_b_send, far_b_recv, core_send, core_recv, local_sem,
+    far_a_send, far_a_recv, far_b_send, far_b_recv, core_send, core_recv,
+    sum_send, sum_recv, local_sem,
 ):
-    cap = rows_out.shape[0]
-    my_z, my_y, my_core = lax.axis_index("z"), lax.axis_index("y"), lax.axis_index("core")
+    cap = out.shape[0]
+    parts, tile = partial_out.shape[1], partial_out.shape[3]
+    my_x, my_z = lax.axis_index("x"), lax.axis_index("z")
+    my_y, my_core = lax.axis_index("y"), lax.axis_index("core")
     right, left = lax.rem(my_y + 1, y_count), lax.rem(my_y + y_count - 1, y_count)
     opposite = lax.rem(my_y + 2, y_count)
     other = 1 - my_core
     half = cap // 2
+    diagonal = my_x == my_y
+
+    def crossed(z):
+        return {"x": my_y, "y": my_x, "z": z}
+
+    def is_me(z):
+        return jnp.logical_and(diagonal, z == my_z)
 
     barrier = pltpu.get_barrier_semaphore()
 
-    @pl.loop(1, z_count)
+    @pl.loop(0, z_count)
     def _(k):
-        pl.semaphore_signal(
-            barrier, inc=1, device_id={"z": lax.rem(my_z + k, z_count)}, device_id_type=MESH
-        )
+        z = lax.rem(my_z + k, z_count)
+
+        @pl.when(jnp.logical_not(is_me(z)))
+        def _():
+            pl.semaphore_signal(barrier, inc=1, device_id=crossed(z), device_id_type=MESH)
 
     for to in ({"y": right}, {"y": left}, {"core": other}):
         pl.semaphore_signal(barrier, inc=1, device_id=to, device_id_type=MESH)
-    pl.semaphore_wait(barrier, z_count + 2)
-
-    def columns(y, core, z):
-        return pl.ds(pl.multiple_of(((y * 2 + core) * z_count + z) * LANES, LANES), LANES)
+    for k in range(1, x_count):
+        to = {"x": lax.rem(my_x + k, x_count)}
+        pl.semaphore_signal(barrier, inc=1, device_id=to, device_id_type=MESH)
+
+    @pl.when(diagonal)
+    def _():
+        pl.semaphore_wait(barrier, z_count - 1 + 3 + x_count - 1)
+
+    @pl.when(jnp.logical_not(diagonal))
+    def _():
+        pl.semaphore_wait(barrier, z_count + 3 + x_count - 1)
+
+    def columns(core, z):
+        return pl.ds(pl.multiple_of((core * z_count + z) * LANES, LANES), LANES)
 
     def z_copy(z):
         return pltpu.make_async_remote_copy(
-            src_ref=chosen.at[z], dst_ref=rows_out.at[:, columns(my_y, my_core, my_z)],
-            send_sem=z_send.at[z], recv_sem=z_recv.at[my_z], device_id={"z": z}, device_id_type=MESH,
+            src_ref=chosen.at[z], dst_ref=rows_in.at[my_x, :, columns(my_core, my_z)],
+            send_sem=z_send.at[z], recv_sem=z_recv.at[my_z],
+            device_id=crossed(z), device_id_type=MESH,
         )
 
     def z_arrival(z):
         return pltpu.make_async_remote_copy(
-            src_ref=chosen.at[0], dst_ref=rows_out.at[:, columns(my_y, my_core, z)],
-            send_sem=z_send.at[0], recv_sem=z_recv.at[z], device_id={"z": z}, device_id_type=MESH,
+            src_ref=chosen.at[0], dst_ref=rows_in.at[my_y, :, columns(my_core, z)],
+            send_sem=z_send.at[0], recv_sem=z_recv.at[z],
+            device_id=crossed(z), device_id_type=MESH,
         )
 
     own_copy = pltpu.make_async_copy(
-        chosen.at[my_z], rows_out.at[:, columns(my_y, my_core, my_z)], local_sem
+        chosen.at[my_z], rows_in.at[my_x, :, columns(my_core, my_z)], local_sem
     )
-    own_copy.start()
-
-    @pl.loop(1, z_count)
+
+    @pl.when(diagonal)
+    def _():
+        own_copy.start()
+
+    @pl.loop(0, z_count)
     def _(k):
-        z_copy(lax.rem(my_z + k, z_count)).start()
+        z = lax.rem(my_z + k, z_count)
+
+        @pl.when(jnp.logical_not(is_me(z)))
+        def _():
+            z_copy(z).start()
 
     def onward(y, core, z, to, send, recv, first, rows):
-        view = rows_out.at[pl.ds(first, rows), columns(y, core, z)]
+        view = rows_in.at[y, pl.ds(first, rows), columns(core, z)]
         return pltpu.make_async_remote_copy(
             src_ref=view, dst_ref=view, send_sem=send, recv_sem=recv,
             device_id=to, device_id_type=MESH,
@@ -458,34 +523,77 @@
     def to_core(y, core, z):
         return onward(y, core, z, {"core": other}, core_send.at[y, z], core_recv.at[y, z], 0, cap)
 
+    def sum_copy(owner, part):
+        return pltpu.make_async_remote_copy(
+            src_ref=partial_out.at[owner, part], dst_ref=partial_in.at[my_x, part],
+            send_sem=sum_send.at[owner, part], recv_sem=sum_recv.at[my_x, part],
+            device_id={"x": owner}, device_id_type=MESH,
+        )
+
+    def sum_arrival(source, part):
+        return pltpu.make_async_remote_copy(
+            src_ref=partial_out.at[0, part], dst_ref=partial_in.at[source, part],
+            send_sem=sum_send.at[0, part], recv_sem=sum_recv.at[source, part],
+            device_id={"x": source}, device_id_type=MESH,
+        )
+
+    def project(owner):
+        @pl.loop(0, z_count)
+        def _(z):
+            to_core(owner, other, z).wait_recv()
+
+        @pl.loop(0, parts)
+        def _(part):
+            at = pl.ds(pl.multiple_of(part * tile, tile), tile)
+            total = jnp.dot(
+                rows_in[owner], projector[:, at], preferred_element_type=jnp.float32
+            )
+
+            @pl.when(owner == my_x)
+            def _():
+                own_sum[:, at] = total
+
+            @pl.when(owner != my_x)
+            def _():
+                partial_out[owner, part] = total.astype(jnp.bfloat16)
+                sum_copy(owner, part).start()
+
     def arrival_order(k):
         return lax.rem(my_z + z_count - k, z_count)
 
-    @pl.loop(0, z_count)
+    lag = min(2, z_count)
+
+    @pl.loop(0, z_count + lag)
     def _(k):
-        z = arrival_order(k)
-
-        @pl.when(z != my_z)
-        def _():
-            z_arrival(z).wait_recv()
-
-        @pl.when(z == my_z)
-        def _():
-            own_copy.wait()
-
-        to_right(my_y, z).start()
-        to_left(my_y, z).start()
-        to_core(my_y, my_core, z).start()
-
-    @pl.loop(0, z_count)
-    def _(k):
-        z = arrival_order(k)
-        to_right(left, z).wait_recv()
-        far_right(left, z).start()
-        to_core(left, my_core, z).start()
-        to_left(right, z).wait_recv()
-        far_left(right, z).start()
-        to_core(right, my_core, z).start()
+        @pl.when(k < z_count)
+        def _():
+            z = arrival_order(k)
+
+            @pl.when(jnp.logical_not(is_me(z)))
+            def _():
+                z_arrival(z).wait_recv()
+
+            @pl.when(is_me(z))
+            def _():
+                own_copy.wait()
+
+            to_right(my_y, z).start()
+            to_left(my_y, z).start()
+            to_core(my_y, my_core, z).start()
+
+        @pl.when(k >= lag)
+        def _():
+            z = arrival_order(k - lag)
+            to_right(left, z).wait_recv()
+            far_right(left, z).start()
+            to_core(left, my_core, z).start()
+            to_left(right, z).wait_recv()
+            far_left(right, z).start()
+            to_core(right, my_core, z).start()
+
+    project(my_y)
+    project(left)
+    project(right)
 
     @pl.loop(0, z_count)
     def _(k):
@@ -494,39 +602,63 @@
         far_left(opposite, z).wait_recv()
         to_core(opposite, my_core, z).start()
 
+    project(opposite)
+
+    @pl.loop(0, parts)
+    def _(part):
+        at = pl.ds(pl.multiple_of(part * tile, tile), tile)
+        total = own_sum[:, at]
+        for k in range(1, x_count):
+            source = lax.rem(my_x + k, x_count)
+            sum_arrival(source, part).wait_recv()
+            total = total + partial_in[source, part].astype(jnp.float32)
+        out[:, at] = total.astype(jnp.bfloat16)
+        for k in range(1, x_count):
+            sum_copy(lax.rem(my_x + k, x_count), part).wait_send()
+
     @pl.loop(0, z_count)
     def _(z):
         for y in range(y_count):
-            to_core(y, other, z).wait_recv()
             to_core(y, my_core, z).wait_send()
         to_right(my_y, z).wait_send()
         to_left(my_y, z).wait_send()
         far_right(left, z).wait_send()
         far_left(right, z).wait_send()
 
-        @pl.when(z != my_z)
+        @pl.when(jnp.logical_not(is_me(z)))
         def _():
             z_copy(z).wait_send()
 
 
-def spread_call(dims, chosen):
+def project_call(dims, chosen, projector):
+    x_count, y_count = dims["x"], dims["y"]
     z_count, cap, _ = chosen.shape
-    y_count = dims["y"]
+    depth, width = projector.shape
+    tile = min(256, width)
+    parts = width // tile
+    f32, bf16 = jnp.float32, jnp.bfloat16
     dma = pltpu.SemaphoreType.DMA
+    vmem = pl.BlockSpec(memory_space=pltpu.VMEM)
     return pl.pallas_call(
-        functools.partial(spread_kernel, dims["x"], z_count, y_count),
-        out_shape=jax.ShapeDtypeStruct((cap, y_count * 2 * z_count * LANES), jnp.bfloat16),
-        in_specs=[pl.BlockSpec(memory_space=pltpu.VMEM)],
-        out_specs=pl.BlockSpec(memory_space=pl.ANY),
-        scratch_shapes=[dma((z_count,))] * 10 + [dma((y_count, z_count))] * 2 + [dma],
-        compiler_params=pltpu.CompilerParams(collective_id=1, has_side_effects=True),
-        name="spread_rows",
-    )(chosen)
-
-
-def running_ends(sizes):
-    index = jnp.arange(sizes.shape[0], dtype=jnp.int32)
-    return jnp.sum(jnp.where(index[None, :] <= index[:, None], sizes[None, :], 0), axis=1)
+        functools.partial(project_kernel, x_count, z_count, y_count),
+        out_shape=jax.ShapeDtypeStruct((cap, width), bf16),
+        in_specs=[vmem, vmem],
+        out_specs=vmem,
+        scratch_shapes=[
+            pltpu.VMEM((y_count, cap, depth), bf16),
+            pltpu.VMEM((cap, width), f32),
+            pltpu.VMEM((x_count, parts, cap, tile), bf16),
+            pltpu.VMEM((x_count, parts, cap, tile), bf16),
+        ]
+        + [dma((z_count,))] * 10
+        + [dma((y_count, z_count))] * 2
+        + [dma((x_count, parts))] * 2
+        + [dma],
+        compiler_params=pltpu.CompilerParams(
+            collective_id=1, has_side_effects=True, vmem_limit_bytes=40 << 20
+        ),
+        name="project_rows",
+    )(chosen, projector)
 
 
 def shards(
@@ -541,42 +673,23 @@
     direct_coefficient,
     final_projector,
 ):
-    x_count, z_count = dims["x"], dims["z"]
-    seq_count = x_count * z_count
-    my_x = lax.axis_index("x")
-    me = my_x * z_count + lax.axis_index("z")
-    cap, _, width = input_triple_streams.shape
-    seq_len = cap * 4 // 5 * seq_count
-
-    projector = lax.all_gather(final_projector, ("x", "z"), axis=0, tiled=True)
-
-    last = former_piece_sizes[me] - 1
-    last_row = lax.dynamic_slice_in_dim(input_triple_streams, last, 1, 0)[0]
-    second_row = lax.dynamic_slice_in_dim(input_triple_streams, jnp.maximum(last - 1, 0), 1, 0)[0]
-    tail = jnp.concatenate([last_row, second_row, last_row[:2]], axis=0).astype(jnp.float32)
-
+    cap = input_triple_streams.shape[0]
+    seq_len = cap * 4 // 5 * dims["x"] * dims["z"]
+
+    projector = lax.all_gather(final_projector, "z", axis=0, tiled=True)
     pieces = conv_call(
         dims,
         jnp.transpose(input_triple_streams, (1, 0, 2)),
-        tail,
         former_piece_sizes,
-        short_causal_filters.reshape(9, width),
+        short_causal_filters,
         pole_coefficients,
         pole_damping,
         direct_coefficient[None, :],
     )
-
-    old_start = running_ends(former_piece_sizes) - former_piece_sizes
-    new_start = running_ends(updated_piece_sizes) - updated_piece_sizes
-    device_names = my_x * z_count + jnp.arange(z_count, dtype=jnp.int32)
-    partner_table = (remaining_indices[None, :] == device_names[:, None]).astype(jnp.int32)
-    start_dev = jnp.sum(partner_table * new_start[None, :], axis=1)
-    count_dev = jnp.sum(partner_table * updated_piece_sizes[None, :], axis=1)
-    chosen = select_call(dims, seq_len, pieces, old_start, start_dev, count_dev)
-
-    hidden = spread_call(dims, chosen)
-    projected = jnp.dot(hidden, projector, preferred_element_type=jnp.float32)
-    return projected.astype(jnp.bfloat16)
+    chosen = select_call(
+        dims, seq_len, pieces, former_piece_sizes, updated_piece_sizes, remaining_indices
+    )
+    return project_call(dims, chosen, projector)
 
 
 def solution(mesh):

time: 200 us -> 193 us (0.965)
  Pallas kernels: 123 us -> 167 us
  waiting for transfers between devices: 35.5 us -> 0.73 us
  matrix products: 11.5 us -> 0 us
  other arithmetic: 3.07 us -> 0 us
  between operations: 15.5 us -> 13.5 us
    pallas_call x2, Pallas kernels: 43.6 us -> 95.4 us  [the longest x1 93.8 us: project_call(): pl.pallas_call(functools.partial(project_kernel, x_count, z_count, y_coun...]
    all_gather x1, waiting for transfers between devices: 34.7 us -> 0.02 us  [shards(): projector = lax.all_gather(final_projector, 'z', axis=0, tiled=True)]
    dot_general x1 -> x0, matrix products: 11.5 us -> none  [shards(): projected = jnp.dot(hidden, projector, preferred_element_type=jnp.float32)]
    pallas_call x1, Pallas kernels: 79.3 us -> 72 us  [conv_call(): pl.pallas_call(functools.partial(conv_kernel, x_count, z_count), out_shap...]
    dynamic_slice x2 -> x0, local copies, waits for them, and re-layouts: 2.15 us -> none  [the longest x1 1.24 us: shards(): last = former_piece_sizes[me] - 1]
    unnamed x20 -> x19, local copies, waits for them, and re-layouts: 6.27 us -> 8.38 us
  transfers between devices with their start and end apart: 1 -> 1, of which waited for: 1 -> 0; matrix products, arithmetic and copies ran while one was open for 3% -> 0% of each run, Pallas kernels for 62% -> 39%
where the time goes in v3:
time: 193 us; the launch traced here: 190 us
  Pallas kernels  167 us (87%)
  between operations  13.5 us (7%)
  local copies, waits for them, and re-layouts  8.38 us (4%)
    pallas_call x1, Pallas kernels, project_call(): pl.pallas_call(functools.partial(project_kernel, x_count, z_count, y_coun...  93.8 us
    pallas_call x1, Pallas kernels, conv_call(): pl.pallas_call(functools.partial(conv_kernel, x_count, z_count), out_shap...  72 us
    unnamed x19, local copies, waits for them, and re-layouts  8.38 us
  transfers between devices with their start and end apart: 1, of which 0 were waited for; matrix products, arithmetic and copies ran while one was open for 0% of the time, Pallas kernels for 39%

profile of v3, /device:TPU:32, one launch (start us, length us, event | category | flops | bytes accessed | tf_op | source)
XLA Modules:
  0.0 190.0 jit_solution(5762597055500198624)
XLA Ops:
  6.5 0.0 copy-start.7
  6.5 0.0 copy-start.8
  6.5 0.0 all-gather.2.cloned.1.call-start
  6.5 0.7 all-gather.2.cloned.1.call-update
  7.3 0.0 copy-start.1
  7.3 1.5 copy-done.1
  8.8 0.0 copy-start.2
  8.8 0.8 copy-done.2
  9.6 0.0 copy-start.3
  9.6 0.8 copy-done.3
  10.5 0.0 copy-start.4
  10.5 0.8 copy-done.4
  11.3 0.0 copy-start.5
  11.3 0.7 copy-done.5
  12.0 0.7 copy-done.6
  12.6 72.0 %conv_shuffle.1.pieces = bf16[32,320,128]{2,1,0:T(8,128)(2,1)S(1)} custom-call(s32[32]{0:T(128)S(1)} %copy-done.6, bf16[3,320,1024]{2,1,0:T(8,128)(2,1)S(1)} %bitcast.2, f32[3,3,1024]{2,1,0:T(4,128)S(1)} %copy-done.4, f32[16,1024]{1,0:T(8,128)S(1)} %copy-done.2, f32[16,1024]{1,0:T(8,128)S(1)} %copy-done.3, f32[1,1024]{1,0:T(1,128)S(1)} %bitcast.3), custom_call_target="tpu_custom_call" | custom-call | tf_op jit(solution)/shard_map/conv_shuffle/pallas_call | solution.py:352
  84.7 0.0 copy-done.7
  84.7 0.0 copy-done.8
  84.7 1.6 reorder_rows.1.chosen
  86.3 0.0 all-gather.2.cloned.1.call-done.projector
  86.3 0.0 copy-start
  86.3 2.2 %copy-done = bf16[2048,1024]{1,0:T(8,128)(2,1)S(1)} copy-done((bf16[2048,1024]{1,0:T(8,128)(2,1)S(1)}, bf16[2048,1024]{1,0:T(8,128)(2,1)}, u32[]{:S(2)}) %copy-start) | copy-done | bytes 4194328
  88.5 93.8 %project_rows.1 = bf16[320,1024]{1,0:T(8,128)(2,1)S(1)} custom-call(bf16[8,320,128]{2,1,0:T(8,128)(2,1)S(1)} %reorder_rows.1.chosen, bf16[2048,1024]{1,0:T(8,128)(2,1)S(1)} %copy-done), custom_call_target="tpu_custom_call" | custom-call | tf_op jit(solution)/shard_map/project_rows/pallas_call | solution.py:642
  182.3 0.8 copy.11
  (1 shorter events, 0.0 us)
Async XLA Ops:
  6.5 78.1 %copy-start.7 = (s32[28]{0:T(128)S(1)}, s32[28]{0:T(128)}, u32[]{:S(2)}) copy-start(s32[28]{0:T(128)} %updated.1) | copy-start | bytes 340
  6.5 78.1 %copy-start.8 = (s32[28]{0:T(128)S(1)}, s32[28]{0:T(128)}, u32[]{:S(2)}) copy-start(s32[28]{0:T(128)} %remaining.1) | copy-start | bytes 340
  6.5 79.8 %all-gather.2.cloned.1.call-start = ((), (), s32[]{:S(2)}) async-start(), calls=%async_computation | async-start | bytes 4718592 | tf_op jit(solution)/shard_map/all_gather | solution.py:679
  7.3 1.5 copy-start.1
  8.8 0.8 copy-start.2
  9.6 0.8 copy-start.3
  10.5 0.8 copy-start.4
  11.3 0.7 copy-start.5
  12.0 0.7 copy-start.6
  86.3 2.2 %copy-start = (bf16[2048,1024]{1,0:T(8,128)(2,1)S(1)}, bf16[2048,1024]{1,0:T(8,128)(2,1)}, u32[]{:S(2)}) copy-start(bf16[2048,1024]{1,0:T(8,128)(2,1)} %all-gather.2.cloned.1.call-done.projector) | copy-start | bytes 12582916
Sparse Core Ops, SparseCore 0:
  9.1 74.7 all-gather.1

commit v4 on v3

--- a/solution.py
+++ b/solution.py
@@ -11,7 +11,16 @@
 MESH = pl.DeviceIdType.MESH
 LANES = 128
 SUBS = 8
-AXES = ("x", "z", "y", "core")
+AXES = ("x_high", "x_low", "z", "y", "core")
+SEQ = ("x_high", "x_low", "z")
+
+
+def x_index():
+    return lax.axis_index("x_high") * 2 + lax.axis_index("x_low")
+
+
+def at_x(x):
+    return {"x_high": x // 2, "x_low": lax.rem(x, 2)}
 
 
 def shift_down(value, by):
@@ -41,12 +50,12 @@
     seq_count = x_count * z_count
     per_owner = max(1, modes // seq_count)
     owners = modes // per_owner
-    my_x, my_z = lax.axis_index("x"), lax.axis_index("z")
+    my_x, my_z = x_index(), lax.axis_index("z")
     me = my_x * z_count + my_z
     valid = sizes[me]
 
     def seq_device(index):
-        return {"x": index // z_count, "z": lax.rem(index, z_count)}
+        return {**at_x(index // z_count), "z": lax.rem(index, z_count)}
 
     def lanes(g):
         return pl.ds(pl.multiple_of(g * LANES, LANES), LANES)
@@ -261,7 +270,7 @@
         view = gathered.at[slot, pl.ds(first, rows)]
         return pltpu.make_async_remote_copy(
             src_ref=view, dst_ref=view, send_sem=send.at[z], recv_sem=recv.at[z],
-            device_id={"x": to}, device_id_type=MESH,
+            device_id=at_x(to), device_id_type=MESH,
         )
 
     def to_right(source_x, z):
@@ -389,7 +398,7 @@
 
     lax.fori_loop(0, seq_count, place, 0)
     row = lax.broadcasted_iota(jnp.int32, (cap, LANES), 0)
-    first = lax.axis_index("x") * z_count
+    first = x_index() * z_count
     chosen[...] = jnp.zeros_like(chosen)
 
     def pick(k, start):
@@ -420,29 +429,29 @@
     )(former, updated, remaining, pieces)
 
 
-def project_kernel(
-    x_count, z_count, y_count,
-    chosen, projector, out,
-    rows_in, own_sum, partial_out, partial_in,
+def spread_kernel(
+    z_count, y_count,
+    chosen, rows_in,
     z_send, z_recv, right_send, right_recv, left_send, left_recv,
     far_a_send, far_a_recv, far_b_send, far_b_recv, core_send, core_recv,
-    sum_send, sum_recv, local_sem,
+    local_sem,
 ):
-    cap = out.shape[0]
-    parts, tile = partial_out.shape[1], partial_out.shape[3]
-    my_x, my_z = lax.axis_index("x"), lax.axis_index("z")
+    cap = rows_in.shape[1]
+    my_x, my_z = x_index(), lax.axis_index("z")
     my_y, my_core = lax.axis_index("y"), lax.axis_index("core")
     right, left = lax.rem(my_y + 1, y_count), lax.rem(my_y + y_count - 1, y_count)
     opposite = lax.rem(my_y + 2, y_count)
     other = 1 - my_core
     half = cap // 2
-    diagonal = my_x == my_y
+    stays = my_x // 2 == my_y // 2
+    target_x = jnp.where(stays, my_x, 3 - my_x)
+    target_y = jnp.where(stays, my_y, 3 - my_y)
 
     def crossed(z):
-        return {"x": my_y, "y": my_x, "z": z}
+        return {**at_x(target_x), "y": target_y, "z": z}
 
     def is_me(z):
-        return jnp.logical_and(diagonal, z == my_z)
+        return jnp.logical_and(stays, z == my_z)
 
     barrier = pltpu.get_barrier_semaphore()
 
@@ -456,40 +465,44 @@
 
     for to in ({"y": right}, {"y": left}, {"core": other}):
         pl.semaphore_signal(barrier, inc=1, device_id=to, device_id_type=MESH)
-    for k in range(1, x_count):
-        to = {"x": lax.rem(my_x + k, x_count)}
-        pl.semaphore_signal(barrier, inc=1, device_id=to, device_id_type=MESH)
-
-    @pl.when(diagonal)
+    @pl.when(stays)
     def _():
-        pl.semaphore_wait(barrier, z_count - 1 + 3 + x_count - 1)
-
-    @pl.when(jnp.logical_not(diagonal))
+        pl.semaphore_wait(barrier, z_count - 1 + 3)
+
+    @pl.when(jnp.logical_not(stays))
     def _():
-        pl.semaphore_wait(barrier, z_count + 3 + x_count - 1)
-
-    def columns(core, z):
-        return pl.ds(pl.multiple_of((core * z_count + z) * LANES, LANES), LANES)
+        pl.semaphore_wait(barrier, z_count + 3)
+
+    def columns(source_y, core, z):
+        block = (lax.rem(source_y, 2) * 2 + core) * z_count + z
+        return pl.ds(pl.multiple_of(block * LANES, LANES), LANES)
+
+    def place(y, core, z, first, rows):
+        native = y // 2 == my_x // 2
+        source_y = jnp.where(native, y, 3 - y)
+        return rows_in.at[
+            jnp.where(native, 0, 1), pl.ds(first, rows), columns(source_y, core, z)
+        ]
 
     def z_copy(z):
         return pltpu.make_async_remote_copy(
-            src_ref=chosen.at[z], dst_ref=rows_in.at[my_x, :, columns(my_core, my_z)],
+            src_ref=chosen.at[z], dst_ref=rows_in.at[jnp.where(stays, 0, 1), :, columns(my_y, my_core, my_z)],
             send_sem=z_send.at[z], recv_sem=z_recv.at[my_z],
             device_id=crossed(z), device_id_type=MESH,
         )
 
     def z_arrival(z):
         return pltpu.make_async_remote_copy(
-            src_ref=chosen.at[0], dst_ref=rows_in.at[my_y, :, columns(my_core, z)],
+            src_ref=chosen.at[0], dst_ref=place(my_y, my_core, z, 0, cap),
             send_sem=z_send.at[0], recv_sem=z_recv.at[z],
             device_id=crossed(z), device_id_type=MESH,
         )
 
     own_copy = pltpu.make_async_copy(
-        chosen.at[my_z], rows_in.at[my_x, :, columns(my_core, my_z)], local_sem
+        chosen.at[my_z], rows_in.at[0, :, columns(my_y, my_core, my_z)], local_sem
     )
 
-    @pl.when(diagonal)
+    @pl.when(stays)
     def _():
         own_copy.start()
 
@@ -502,7 +515,7 @@
             z_copy(z).start()
 
     def onward(y, core, z, to, send, recv, first, rows):
-        view = rows_in.at[y, pl.ds(first, rows), columns(core, z)]
+        view = place(y, core, z, first, rows)
         return pltpu.make_async_remote_copy(
             src_ref=view, dst_ref=view, send_sem=send, recv_sem=recv,
             device_id=to, device_id_type=MESH,
@@ -522,41 +535,6 @@
 
     def to_core(y, core, z):
         return onward(y, core, z, {"core": other}, core_send.at[y, z], core_recv.at[y, z], 0, cap)
-
-    def sum_copy(owner, part):
-        return pltpu.make_async_remote_copy(
-            src_ref=partial_out.at[owner, part], dst_ref=partial_in.at[my_x, part],
-            send_sem=sum_send.at[owner, part], recv_sem=sum_recv.at[my_x, part],
-            device_id={"x": owner}, device_id_type=MESH,
-        )
-
-    def sum_arrival(source, part):
-        return pltpu.make_async_remote_copy(
-            src_ref=partial_out.at[0, part], dst_ref=partial_in.at[source, part],
-            send_sem=sum_send.at[0, part], recv_sem=sum_recv.at[source, part],
-            device_id={"x": source}, device_id_type=MESH,
-        )
-
-    def project(owner):
-        @pl.loop(0, z_count)
-        def _(z):
-            to_core(owner, other, z).wait_recv()
-
-        @pl.loop(0, parts)
-        def _(part):
-            at = pl.ds(pl.multiple_of(part * tile, tile), tile)
-            total = jnp.dot(
-                rows_in[owner], projector[:, at], preferred_element_type=jnp.float32
-            )
-
-            @pl.when(owner == my_x)
-            def _():
-                own_sum[:, at] = total
-
-            @pl.when(owner != my_x)
-            def _():
-                partial_out[owner, part] = total.astype(jnp.bfloat16)
-                sum_copy(owner, part).start()
 
     def arrival_order(k):
         return lax.rem(my_z + z_count - k, z_count)
@@ -591,10 +569,6 @@
             far_left(right, z).start()
             to_core(right, my_core, z).start()
 
-    project(my_y)
-    project(left)
-    project(right)
-
     @pl.loop(0, z_count)
     def _(k):
         z = arrival_order(k)
@@ -602,23 +576,10 @@
         far_left(opposite, z).wait_recv()
         to_core(opposite, my_core, z).start()
 
-    project(opposite)
-
-    @pl.loop(0, parts)
-    def _(part):
-        at = pl.ds(pl.multiple_of(part * tile, tile), tile)
-        total = own_sum[:, at]
-        for k in range(1, x_count):
-            source = lax.rem(my_x + k, x_count)
-            sum_arrival(source, part).wait_recv()
-            total = total + partial_in[source, part].astype(jnp.float32)
-        out[:, at] = total.astype(jnp.bfloat16)
-        for k in range(1, x_count):
-            sum_copy(lax.rem(my_x + k, x_count), part).wait_send()
-
     @pl.loop(0, z_count)
     def _(z):
         for y in range(y_count):
+            to_core(y, other, z).wait_recv()
             to_core(y, my_core, z).wait_send()
         to_right(my_y, z).wait_send()
         to_left(my_y, z).wait_send()
@@ -630,9 +591,80 @@
             z_copy(z).wait_send()
 
 
-def project_call(dims, chosen, projector):
-    x_count, y_count = dims["x"], dims["y"]
+def spread_call(dims, chosen):
     z_count, cap, _ = chosen.shape
+    y_count = dims["y"]
+    dma = pltpu.SemaphoreType.DMA
+    return pl.pallas_call(
+        functools.partial(spread_kernel, z_count, y_count),
+        out_shape=jax.ShapeDtypeStruct((2, cap, y_count * z_count * LANES), jnp.bfloat16),
+        in_specs=[pl.BlockSpec(memory_space=pltpu.VMEM)],
+        out_specs=pl.BlockSpec(memory_space=pl.ANY),
+        scratch_shapes=[dma((z_count,))] * 10 + [dma((y_count, z_count))] * 2 + [dma],
+        compiler_params=pltpu.CompilerParams(
+            collective_id=1, has_side_effects=True, vmem_limit_bytes=16 << 20
+        ),
+        name="spread_rows",
+    )(chosen)
+
+
+def project_kernel(
+    rows, projector, out,
+    weights, own_sum, partial_out, partial_in,
+    load_sem, sum_send, sum_recv,
+):
+    parts, _, tile = weights.shape
+    partner = at_x(3 - x_index())
+
+    barrier = pltpu.get_barrier_semaphore()
+    pl.semaphore_signal(barrier, inc=1, device_id=partner, device_id_type=MESH)
+
+    def span(part):
+        return pl.ds(pl.multiple_of(part * tile, tile), tile)
+
+    def load(part):
+        return pltpu.make_async_copy(
+            projector.at[:, span(part)], weights.at[part], load_sem.at[part]
+        )
+
+    def exchange(part):
+        return pltpu.make_async_remote_copy(
+            src_ref=partial_out.at[part], dst_ref=partial_in.at[part],
+            send_sem=sum_send.at[part], recv_sem=sum_recv.at[part],
+            device_id=partner, device_id_type=MESH,
+        )
+
+    @pl.loop(0, parts)
+    def _(part):
+        load(part).start()
+
+    pl.semaphore_wait(barrier, 1)
+
+    @pl.loop(0, parts)
+    def _(part):
+        load(part).wait()
+        partial_out[part] = jnp.dot(
+            rows[1], weights[part], preferred_element_type=jnp.float32
+        ).astype(jnp.bfloat16)
+        exchange(part).start()
+
+    @pl.loop(0, parts)
+    def _(part):
+        own_sum[part] = jnp.dot(rows[0], weights[part], preferred_element_type=jnp.float32)
+
+    @pl.loop(0, parts)
+    def _(part):
+        exchange(part).wait_recv()
+        total = own_sum[part] + partial_in[part].astype(jnp.float32)
+        out[:, span(part)] = total.astype(jnp.bfloat16)
+
+    @pl.loop(0, parts)
+    def _(part):
+        exchange(part).wait_send()
+
+
+def project_call(rows, projector):
+    cap = rows.shape[1]
     depth, width = projector.shape
     tile = min(256, width)
     parts = width // tile
@@ -640,25 +672,22 @@
     dma = pltpu.SemaphoreType.DMA
     vmem = pl.BlockSpec(memory_space=pltpu.VMEM)
     return pl.pallas_call(
-        functools.partial(project_kernel, x_count, z_count, y_count),
+        project_kernel,
         out_shape=jax.ShapeDtypeStruct((cap, width), bf16),
-        in_specs=[vmem, vmem],
+        in_specs=[vmem, pl.BlockSpec(memory_space=pl.ANY)],
         out_specs=vmem,
         scratch_shapes=[
-            pltpu.VMEM((y_count, cap, depth), bf16),
-            pltpu.VMEM((cap, width), f32),
-            pltpu.VMEM((x_count, parts, cap, tile), bf16),
-            pltpu.VMEM((x_count, parts, cap, tile), bf16),
-        ]
-        + [dma((z_count,))] * 10
-        + [dma((y_count, z_count))] * 2
-        + [dma((x_count, parts))] * 2
-        + [dma],
+            pltpu.VMEM((parts, depth, tile), bf16),
+            pltpu.VMEM((parts, cap, tile), f32),
+            pltpu.VMEM((parts, cap, tile), bf16),
+            pltpu.VMEM((parts, cap, tile), bf16),
+            dma((parts,)), dma((parts,)), dma((parts,)),
+        ],
         compiler_params=pltpu.CompilerParams(
-            collective_id=1, has_side_effects=True, vmem_limit_bytes=40 << 20
+            collective_id=2, has_side_effects=True, vmem_limit_bytes=32 << 20
         ),
         name="project_rows",
-    )(chosen, projector)
+    )(rows, projector)
 
 
 def shards(
@@ -676,7 +705,7 @@
     cap = input_triple_streams.shape[0]
     seq_len = cap * 4 // 5 * dims["x"] * dims["z"]
 
-    projector = lax.all_gather(final_projector, "z", axis=0, tiled=True)
+    projector = lax.all_gather(final_projector, ("x_low", "z"), axis=0, tiled=True)
     pieces = conv_call(
         dims,
         jnp.transpose(input_triple_streams, (1, 0, 2)),
@@ -689,13 +718,13 @@
     chosen = select_call(
         dims, seq_len, pieces, former_piece_sizes, updated_piece_sizes, remaining_indices
     )
-    return project_call(dims, chosen, projector)
+    return project_call(spread_call(dims, chosen), projector)
 
 
 def solution(mesh):
-    grid = (4, mesh.shape["seq"] // 4, mesh.shape["chan"] // 2, 2)
-    dims = dict(zip(AXES, grid, strict=True))
-    rows, channels = ("x", "z"), ("y", "core")
+    grid = (2, 2, mesh.shape["seq"] // 4, mesh.shape["chan"] // 2, 2)
+    dims = {"x": 4, "z": grid[2], "y": grid[3]}
+    rows, channels = SEQ, ("y", "core")
     return jax.shard_map(
         functools.partial(shards, dims),
         mesh=Mesh(mesh.devices.reshape(grid), AXES),

time: 193 us -> 228 us (1.18)
  Pallas kernels: 167 us -> 198 us
  local copies, waits for them, and re-layouts: 8.38 us -> 14.5 us
    pallas_call x1 -> x2, Pallas kernels: 93.8 us -> 125 us  [the longest x1 105 us: spread_call(): pl.pallas_call(functools.partial(spread_kernel, z_count, y_count), out_sh...]
    unnamed x19 -> x23, local copies, waits for them, and re-layouts: 8.38 us -> 14.5 us
  transfers between devices with their start and end apart: 1 -> 1, of which waited for: 0 -> 0; matrix products, arithmetic and copies ran while one was open for 0% -> 0% of each run, Pallas kernels for 39% -> 79%
where the time goes in v4:
time: 228 us; the launch traced here: 227 us
  Pallas kernels  198 us (87%)
  local copies, waits for them, and re-layouts  14.5 us (6%)
  between operations  13.5 us (6%)
    pallas_call x1, Pallas kernels, spread_call(): pl.pallas_call(functools.partial(spread_kernel, z_count, y_count), out_sh...  105 us
    pallas_call x1, Pallas kernels, conv_call(): pl.pallas_call(functools.partial(conv_kernel, x_count, z_count), out_shap...  72.1 us
    pallas_call x1, Pallas kernels, project_call(): pl.pallas_call(project_kernel, out_shape=jax.ShapeDtypeStruct((cap, width...  19.2 us
    unnamed x23, local copies, waits for them, and re-layouts  14.5 us
  transfers between devices with their start and end apart: 1, of which 0 were waited for; matrix products, arithmetic and copies ran while one was open for 0% of the time, Pallas kernels for 79%

profile of v4, /device:TPU:32, one launch (start us, length us, event | category | flops | bytes accessed | tf_op | source)
XLA Modules:
  0.0 226.9 jit_solution(13625739345204543704)
XLA Ops:
  6.5 0.0 copy-start.10
  6.5 0.0 copy-start.9
  6.5 0.0 all-gather.2.cloned.1.call-start
  6.5 0.7 all-gather.2.cloned.1.call-update
  7.3 0.0 copy-start.3
  7.3 1.5 copy-done.3
  8.8 0.0 copy-start.4
  8.8 0.8 copy-done.4
  9.6 0.0 copy-start.5
  9.6 0.8 copy-done.5
  10.5 0.8 copy-done.6
  11.3 0.7 copy-done.7
  12.0 0.7 copy-done.8
  12.6 72.1 %conv_shuffle.1.pieces = bf16[32,320,128]{2,1,0:T(8,128)(2,1)S(1)} custom-call(s32[32]{0:T(128)S(1)} %copy-done.8, bf16[3,320,1024]{2,1,0:T(8,128)(2,1)S(1)} %bitcast.2, f32[3,3,1024]{2,1,0:T(4,128)S(1)} %copy-done.6, f32[16,1024]{1,0:T(8,128)S(1)} %copy-done.4, f32[16,1024]{1,0:T(8,128)S(1)} %copy-done.5, f32[1,1024]{1,0:T(1,128)S(1)} %bitcast.3), custom_call_target="tpu_custom_call" | custom-call | tf_op jit(solution)/shard_map/conv_shuffle/pallas_call | solution.py:361
  84.7 0.0 copy-done.10
  84.7 0.0 copy-done.9
  84.7 1.6 reorder_rows.1.chosen
  86.4 105.3 %spread_rows.1.rows = bf16[2,320,4096]{2,1,0:T(8,128)(2,1)S(1)} custom-call(bf16[8,320,128]{2,1,0:T(8,128)(2,1)S(1)} %reorder_rows.1.chosen), custom_call_target="tpu_custom_call" | custom-call | tf_op jit(solution)/shard_map/spread_rows/pallas_call | solution.py:598
  191.7 0.0 copy-start
  191.7 2.4 %copy-done = bf16[2,320,4096]{2,1,0:T(8,128)(2,1)} copy-done((bf16[2,320,4096]{2,1,0:T(8,128)(2,1)}, bf16[2,320,4096]{2,1,0:T(8,128)(2,1)S(1)}, u32[]{:S(2)}) %copy-start) | copy-done | bytes 5242904
  194.1 2.5 %copy-done.1 = bf16[2,320,4096]{2,1,0:T(8,128)(2,1)S(1)} copy-done((bf16[2,320,4096]{2,1,0:T(8,128)(2,1)S(1)}, bf16[2,320,4096]{2,1,0:T(8,128)(2,1)}, u32[]{:S(2)}) %copy-start.1) | copy-done | bytes 5242904
  196.6 3.4 %copy-done.2 = bf16[4096,1024]{1,0:T(8,128)(2,1)S(1)} copy-done((bf16[4096,1024]{1,0:T(8,128)(2,1)S(1)}, bf16[4096,1024]{1,0:T(8,128)(2,1)}, u32[]{:S(2)}) %copy-start.2) | copy-done | bytes 8388632
  200.0 19.2 %project_rows.1 = bf16[320,1024]{1,0:T(8,128)(2,1)S(1)} custom-call(bf16[2,320,4096]{2,1,0:T(8,128)(2,1)S(1)} %copy-done.1, bf16[4096,1024]{1,0:T(8,128)(2,1)S(1)} %copy-done.2), custom_call_target="tpu_custom_call" | custom-call | tf_op jit(solution)/shard_map/project_rows/pallas_call | solution.py:674
  219.2 0.8 copy.11
  (6 shorter events, 0.0 us)
Async XLA Ops:
  6.5 78.2 %copy-start.10 = (s32[28]{0:T(128)S(1)}, s32[28]{0:T(128)}, u32[]{:S(2)}) copy-start(s32[28]{0:T(128)} %remaining.1) | copy-start | bytes 340
  6.5 78.2 %copy-start.9 = (s32[28]{0:T(128)S(1)}, s32[28]{0:T(128)}, u32[]{:S(2)}) copy-start(s32[28]{0:T(128)} %updated.1) | copy-start | bytes 340
  6.5 187.6 %all-gather.2.cloned.1.call-start = ((), (), s32[]{:S(2)}) async-start(), calls=%async_computation | async-start | bytes 8912896 | tf_op jit(solution)/shard_map/all_gather | solution.py:708
  7.3 1.5 copy-start.3
  8.8 0.8 copy-start.4
  9.6 0.8 copy-start.5
  10.5 0.8 copy-start.6
  11.3 0.7 copy-start.7
  12.0 0.7 copy-start.8
  191.7 2.4 %copy-start = (bf16[2,320,4096]{2,1,0:T(8,128)(2,1)}, bf16[2,320,4096]{2,1,0:T(8,128)(2,1)S(1)}, u32[]{:S(2)}) copy-start(bf16[2,320,4096]{2,1,0:T(8,128)(2,1)S(1)} %spread_rows.1.rows) | copy-start | bytes 15728644
  194.1 2.5 %copy-start.1 = (bf16[2,320,4096]{2,1,0:T(8,128)(2,1)S(1)}, bf16[2,320,4096]{2,1,0:T(8,128)(2,1)}, u32[]{:S(2)}) copy-start(bf16[2,320,4096]{2,1,0:T(8,128)(2,1)} %copy-done) | copy-start | bytes 15728644
  196.6 3.4 %copy-start.2 = (bf16[4096,1024]{1,0:T(8,128)(2,1)S(1)}, bf16[4096,1024]{1,0:T(8,128)(2,1)}, u32[]{:S(2)}) copy-start(bf16[4096,1024]{1,0:T(8,128)(2,1)} %all-gather.2.cloned.1.call-done.projector) | copy-start | bytes 25165828
Sparse Core Ops, SparseCore 0:
  9.1 119.9 all-gather.1

commit v5 on v4

--- a/solution.py
+++ b/solution.py
@@ -10,6 +10,7 @@
 
 MESH = pl.DeviceIdType.MESH
 LANES = 128
+VMEM = 56 << 20
 SUBS = 8
 AXES = ("x_high", "x_low", "z", "y", "core")
 SEQ = ("x_high", "x_low", "z")
@@ -36,12 +37,11 @@
 
 def conv_kernel(
     x_count, z_count,
-    sizes, streams, taps, residue, damping, direct,
-    gathered,
-    padded, tail, rates_own, query, gated, mixed, partial, ends, end_in, carry_out, carry_in, hidden, halo,
+    sizes, streams_far, taps_far, residue_far, damping_far, direct_far, block,
+    gathered, swapped,
+    streams, taps, residue, damping, direct, padded, tail, rates_own, query, gated, mixed, partial, ends, end_in, carry_out, carry_in, hidden, halo,
     halo_send, halo_recv, end_send, end_recv, carry_send, carry_recv,
-    z_send, z_recv, right_send, right_recv, left_send, left_recv,
-    far_a_send, far_a_recv, far_b_send, far_b_recv, local_sem,
+    z_send, z_recv, swap_send, swap_recv, load_sem, local_sem,
 ):
     modes = residue.shape[0]
     cap = streams.shape[1]
@@ -54,6 +54,16 @@
     me = my_x * z_count + my_z
     valid = sizes[me]
 
+    loads = [
+        pltpu.make_async_copy(far, near, load_sem.at[i])
+        for i, (far, near) in enumerate((
+            (streams_far, streams), (taps_far, taps), (residue_far, residue),
+            (damping_far, damping), (direct_far, direct),
+        ))
+    ]
+    for load in loads:
+        load.start()
+
     def seq_device(index):
         return {**at_x(index // z_count), "z": lax.rem(index, z_count)}
 
@@ -68,6 +78,8 @@
             barrier, inc=1, device_id=seq_device(lax.rem(me + k, seq_count)), device_id_type=MESH
         )
 
+    for load in loads:
+        load.wait()
     last = SUBS - 1 + valid
     second = jnp.maximum(last - 1, SUBS)
 
@@ -88,8 +100,13 @@
             recv_sem=halo_recv.at[distance - 1], device_id=seq_device(target), device_id_type=MESH,
         )
 
+    swap = pltpu.make_async_remote_copy(
+        src_ref=block, dst_ref=swapped, send_sem=swap_send, recv_sem=swap_recv,
+        device_id={"x_low": 1 - lax.axis_index("x_low")}, device_id_type=MESH,
+    )
     for distance in (1, 2):
         halo_copy(distance).start()
+    swap.start()
     for distance in (1, 2):
         halo_copy(distance).wait_recv()
 
@@ -216,17 +233,17 @@
 
     def z_copy(g):
         return pltpu.make_async_remote_copy(
-            src_ref=hidden.at[g], dst_ref=gathered.at[me], send_sem=z_send.at[g],
+            src_ref=hidden.at[g], dst_ref=gathered.at[my_z], send_sem=z_send.at[g],
             recv_sem=z_recv.at[my_z], device_id={"z": g}, device_id_type=MESH,
         )
 
     def z_arrival(z):
         return pltpu.make_async_remote_copy(
-            src_ref=hidden.at[0], dst_ref=gathered.at[my_x * z_count + z], send_sem=z_send.at[0],
+            src_ref=hidden.at[0], dst_ref=gathered.at[z], send_sem=z_send.at[0],
             recv_sem=z_recv.at[z], device_id={"z": z}, device_id_type=MESH,
         )
 
-    own_copy = pltpu.make_async_copy(hidden.at[my_z], gathered.at[me], local_sem)
+    own_copy = pltpu.make_async_copy(hidden.at[my_z], gathered.at[my_z], local_sem)
 
     @pl.loop(0, groups)
     def _(k):
@@ -262,74 +279,16 @@
         def _():
             own_copy.start()
 
-    right, left = lax.rem(my_x + 1, x_count), lax.rem(my_x + x_count - 1, x_count)
-    half = cap // 2
-
-    def x_copy(source_x, z, to, send, recv, first, rows):
-        slot = source_x * z_count + z
-        view = gathered.at[slot, pl.ds(first, rows)]
-        return pltpu.make_async_remote_copy(
-            src_ref=view, dst_ref=view, send_sem=send.at[z], recv_sem=recv.at[z],
-            device_id=at_x(to), device_id_type=MESH,
-        )
-
-    def to_right(source_x, z):
-        return x_copy(source_x, z, right, right_send, right_recv, 0, cap)
-
-    def to_left(source_x, z):
-        return x_copy(source_x, z, left, left_send, left_recv, 0, cap)
-
-    def far_right(source_x, z):
-        return x_copy(source_x, z, right, far_a_send, far_a_recv, 0, half)
-
-    def far_left(source_x, z):
-        return x_copy(source_x, z, left, far_b_send, far_b_recv, half, half)
-
-    def arrival_order(k):
-        return lax.rem(my_z + 2 * z_count - 1 - k, z_count)
-
-    lag = min(2, z_count)
-
-    @pl.loop(0, z_count + lag)
-    def _(k):
-        @pl.when(k < z_count)
-        def _():
-            z = arrival_order(k)
-
-            @pl.when(z != my_z)
-            def _():
-                z_arrival(z).wait_recv()
-
-            @pl.when(z == my_z)
-            def _():
-                own_copy.wait()
-
-            to_right(my_x, z).start()
-            to_left(my_x, z).start()
-
-        @pl.when(k >= lag)
-        def _():
-            z = arrival_order(k - lag)
-            to_right(left, z).wait_recv()
-            far_right(left, z).start()
-            to_left(right, z).wait_recv()
-            far_left(right, z).start()
-
-    opposite = lax.rem(my_x + 2, x_count)
+    own_copy.wait()
 
     @pl.loop(0, z_count)
     def _(z):
-        far_right(opposite, z).wait_recv()
-        far_left(opposite, z).wait_recv()
-        far_right(left, z).wait_send()
-        far_left(right, z).wait_send()
-        to_right(my_x, z).wait_send()
-        to_left(my_x, z).wait_send()
-
         @pl.when(z != my_z)
         def _():
+            z_arrival(z).wait_recv()
             z_copy(z).wait_send()
 
+    swap.wait()
     for distance in (1, 2):
         halo_copy(distance).wait_send()
 
@@ -348,7 +307,7 @@
                 carry_copy(target).wait_send()
 
 
-def conv_call(dims, streams, sizes, taps, residue, damping, direct):
+def conv_call(dims, streams, sizes, taps, residue, damping, direct, block):
     x_count, z_count = dims["x"], dims["z"]
     cap, width = streams.shape[1:]
     modes = residue.shape[0]
@@ -358,12 +317,21 @@
     f32, bf16 = jnp.float32, jnp.bfloat16
     dma = pltpu.SemaphoreType.DMA
     vmem = pl.BlockSpec(memory_space=pltpu.VMEM)
+    far = pl.BlockSpec(memory_space=pl.ANY)
     return pl.pallas_call(
         functools.partial(conv_kernel, x_count, z_count),
-        out_shape=jax.ShapeDtypeStruct((seq_count, cap, LANES), bf16),
-        in_specs=[pl.BlockSpec(memory_space=pltpu.SMEM)] + [vmem] * 5,
-        out_specs=pl.BlockSpec(memory_space=pl.ANY),
+        out_shape=[
+            jax.ShapeDtypeStruct((z_count, cap, LANES), bf16),
+            jax.ShapeDtypeStruct(block.shape, bf16),
+        ],
+        in_specs=[pl.BlockSpec(memory_space=pltpu.SMEM)] + [far] * 6,
+        out_specs=[far, far],
         scratch_shapes=[
+            pltpu.VMEM(streams.shape, bf16),
+            pltpu.VMEM(taps.shape, f32),
+            pltpu.VMEM(residue.shape, f32),
+            pltpu.VMEM(damping.shape, f32),
+            pltpu.VMEM(direct.shape, f32),
             pltpu.VMEM((3, z_count, cap + SUBS, LANES), f32),
             pltpu.VMEM((z_count, SUBS, LANES), f32),
             pltpu.VMEM((per_owner, z_count, LANES), f32),
@@ -380,13 +348,98 @@
             dma((2,)), dma((2,)),
             dma((owners,)), dma((seq_count,)), dma((seq_count,)), dma((owners,)),
         ]
-        + [dma((z_count,))] * 10
-        + [dma],
+        + [dma((z_count,))] * 2
+        + [dma, dma, dma((5,)), dma],
         compiler_params=pltpu.CompilerParams(
-            collective_id=0, has_side_effects=True, vmem_limit_bytes=24 << 20
+            collective_id=0, has_side_effects=True, vmem_limit_bytes=VMEM
         ),
-        name="conv_shuffle",
-    )(sizes, streams, taps, residue, damping, direct)
+        name="convolve",
+    )(sizes, streams, taps, residue, damping, direct, block)
+
+
+def ring_kernel(
+    x_count, z_count,
+    own, gathered,
+    right_send, right_recv, left_send, left_recv,
+    far_a_send, far_a_recv, far_b_send, far_b_recv, local_sem,
+):
+    my_x = x_index()
+    cap = own.shape[1]
+    half = cap // 2
+    right, left = lax.rem(my_x + 1, x_count), lax.rem(my_x + x_count - 1, x_count)
+    opposite = lax.rem(my_x + 2, x_count)
+    local = pltpu.make_async_copy(
+        own, gathered.at[pl.ds(my_x * z_count, z_count)], local_sem
+    )
+    local.start()
+    barrier = pltpu.get_barrier_semaphore()
+    for to in (right, left):
+        pl.semaphore_signal(barrier, inc=1, device_id=at_x(to), device_id_type=MESH)
+    pl.semaphore_wait(barrier, 2)
+
+    def x_copy(source, source_x, z, to, send, recv, first, rows):
+        at = pl.ds(first, rows)
+        return pltpu.make_async_remote_copy(
+            src_ref=source.at[at], dst_ref=gathered.at[source_x * z_count + z, at],
+            send_sem=send.at[z], recv_sem=recv.at[z], device_id=at_x(to), device_id_type=MESH,
+        )
+
+    def to_right(source_x, z):
+        return x_copy(own.at[z], source_x, z, right, right_send, right_recv, 0, cap)
+
+    def to_left(source_x, z):
+        return x_copy(own.at[z], source_x, z, left, left_send, left_recv, 0, cap)
+
+    def onward(source_x, z):
+        return gathered.at[source_x * z_count + z]
+
+    def far_right(source_x, z):
+        return x_copy(
+            onward(source_x, z), source_x, z, right, far_a_send, far_a_recv, 0, half
+        )
+
+    def far_left(source_x, z):
+        return x_copy(
+            onward(source_x, z), source_x, z, left, far_b_send, far_b_recv, half, half
+        )
+
+    @pl.loop(0, z_count)
+    def _(z):
+        to_right(my_x, z).start()
+        to_left(my_x, z).start()
+
+    @pl.loop(0, z_count)
+    def _(z):
+        to_right(left, z).wait_recv()
+        far_right(left, z).start()
+        to_left(right, z).wait_recv()
+        far_left(right, z).start()
+
+    local.wait()
+
+    @pl.loop(0, z_count)
+    def _(z):
+        far_right(opposite, z).wait_recv()
+        far_left(opposite, z).wait_recv()
+        far_right(left, z).wait_send()
+        far_left(right, z).wait_send()
+        to_right(my_x, z).wait_send()
+        to_left(my_x, z).wait_send()
+
+
+def ring_call(dims, own):
+    x_count, z_count = dims["x"], dims["z"]
+    dma = pltpu.SemaphoreType.DMA
+    far = pl.BlockSpec(memory_space=pl.ANY)
+    return pl.pallas_call(
+        functools.partial(ring_kernel, x_count, z_count),
+        out_shape=jax.ShapeDtypeStruct((x_count * z_count,) + own.shape[1:], own.dtype),
+        in_specs=[far],
+        out_specs=far,
+        scratch_shapes=[dma((z_count,))] * 8 + [dma],
+        compiler_params=pltpu.CompilerParams(collective_id=3, has_side_effects=True),
+        name="ring_rows",
+    )(own)
 
 
 def select_kernel(z_count, former, updated, remaining, pieces, chosen, sequence):
@@ -602,18 +655,20 @@
         out_specs=pl.BlockSpec(memory_space=pl.ANY),
         scratch_shapes=[dma((z_count,))] * 10 + [dma((y_count, z_count))] * 2 + [dma],
         compiler_params=pltpu.CompilerParams(
-            collective_id=1, has_side_effects=True, vmem_limit_bytes=16 << 20
+            collective_id=1, has_side_effects=True, vmem_limit_bytes=VMEM
         ),
         name="spread_rows",
     )(chosen)
 
 
 def project_kernel(
-    rows, projector, out,
-    weights, own_sum, partial_out, partial_in,
-    load_sem, sum_send, sum_recv,
+    rows_far, near_block, far_block, out,
+    rows, weights, own_sum, partial_out, partial_in,
+    rows_sem, load_sem, sum_send, sum_recv,
 ):
-    parts, _, tile = weights.shape
+    parts, depth, tile = weights.shape
+    half = depth // 2
+    my_low = lax.axis_index("x_low")
     partner = at_x(3 - x_index())
 
     barrier = pltpu.get_barrier_semaphore()
@@ -622,10 +677,22 @@
     def span(part):
         return pl.ds(pl.multiple_of(part * tile, tile), tile)
 
-    def load(part):
+    def load(block, low, part, sem):
+        first = pl.multiple_of(low * half, half)
         return pltpu.make_async_copy(
-            projector.at[:, span(part)], weights.at[part], load_sem.at[part]
-        )
+            block.at[:, span(part)], weights.at[part, pl.ds(first, half)], sem.at[part]
+        )
+
+    def near(part):
+        return load(near_block, my_low, part, load_sem.at[0])
+
+    def far(part):
+        return load(far_block, 1 - my_low, part, load_sem.at[1])
+
+    def row_load(k):
+        return pltpu.make_async_copy(rows_far.at[k], rows.at[k], rows_sem.at[k])
+
+    row_load(1).start()
 
     def exchange(part):
         return pltpu.make_async_remote_copy(
@@ -636,17 +703,23 @@
 
     @pl.loop(0, parts)
     def _(part):
-        load(part).start()
-
+        near(part).start()
+        far(part).start()
+
+    row_load(0).start()
+    row_load(1).wait()
     pl.semaphore_wait(barrier, 1)
 
     @pl.loop(0, parts)
     def _(part):
-        load(part).wait()
+        near(part).wait()
+        far(part).wait()
         partial_out[part] = jnp.dot(
             rows[1], weights[part], preferred_element_type=jnp.float32
         ).astype(jnp.bfloat16)
         exchange(part).start()
+
+    row_load(0).wait()
 
     @pl.loop(0, parts)
     def _(part):
@@ -663,9 +736,9 @@
         exchange(part).wait_send()
 
 
-def project_call(rows, projector):
-    cap = rows.shape[1]
-    depth, width = projector.shape
+def project_call(rows, near_block, far_block):
+    _, cap, depth = rows.shape
+    width = near_block.shape[1]
     tile = min(256, width)
     parts = width // tile
     f32, bf16 = jnp.float32, jnp.bfloat16
@@ -674,20 +747,21 @@
     return pl.pallas_call(
         project_kernel,
         out_shape=jax.ShapeDtypeStruct((cap, width), bf16),
-        in_specs=[vmem, pl.BlockSpec(memory_space=pl.ANY)],
+        in_specs=[pl.BlockSpec(memory_space=pl.ANY)] * 3,
         out_specs=vmem,
         scratch_shapes=[
+            pltpu.VMEM(rows.shape, bf16),
             pltpu.VMEM((parts, depth, tile), bf16),
             pltpu.VMEM((parts, cap, tile), f32),
             pltpu.VMEM((parts, cap, tile), bf16),
             pltpu.VMEM((parts, cap, tile), bf16),
-            dma((parts,)), dma((parts,)), dma((parts,)),
+            dma((2,)), dma((2, parts)), dma((parts,)), dma((parts,)),
         ],
         compiler_params=pltpu.CompilerParams(
-            collective_id=2, has_side_effects=True, vmem_limit_bytes=32 << 20
+            collective_id=2, has_side_effects=True, vmem_limit_bytes=VMEM
         ),
         name="project_rows",
-    )(rows, projector)
+    )(rows, near_block, far_block)
 
 
 def shards(
@@ -705,8 +779,8 @@
     cap = input_triple_streams.shape[0]
     seq_len = cap * 4 // 5 * dims["x"] * dims["z"]
 
-    projector = lax.all_gather(final_projector, ("x_low", "z"), axis=0, tiled=True)
-    pieces = conv_call(
+    near_block = lax.all_gather(final_projector, "z", axis=0, tiled=True)
+    own, swapped = conv_call(
         dims,
         jnp.transpose(input_triple_streams, (1, 0, 2)),
         former_piece_sizes,
@@ -714,11 +788,14 @@
         pole_coefficients,
         pole_damping,
         direct_coefficient[None, :],
+        final_projector,
     )
+    far_block = lax.all_gather(swapped, "z", axis=0, tiled=True)
+    pieces = ring_call(dims, own)
     chosen = select_call(
         dims, seq_len, pieces, former_piece_sizes, updated_piece_sizes, remaining_indices
     )
-    return project_call(spread_call(dims, chosen), projector)
+    return project_call(spread_call(dims, chosen), near_block, far_block)
 
 
 def solution(mesh):

time: 228 us -> 184 us (0.81)
  Pallas kernels: 198 us -> 154 us
  local copies, waits for them, and re-layouts: 14.5 us -> 4.54 us
  waiting for transfers between devices: 0.71 us -> 9.64 us
    pallas_call x1, Pallas kernels: 105 us -> 50.3 us  [spread_call(): pl.pallas_call(functools.partial(spread_kernel, z_count, y_count), out_sh...]
    pallas_call x0 -> x1, Pallas kernels: none -> 25.6 us  [ring_call(): pl.pallas_call(functools.partial(ring_kernel, x_count, z_count), out_shap...]
    pallas_call x1, Pallas kernels: 72.1 us -> 54.3 us  [conv_call(): pl.pallas_call(functools.partial(conv_kernel, x_count, z_count), out_shap...]
    unnamed x23 -> x11, local copies, waits for them, and re-layouts: 14.5 us -> 4.54 us
    all_gather x1 -> x2, waiting for transfers between devices: 0.01 us -> 8.91 us  [the longest x1 8.89 us: shards(): far_block = lax.all_gather(swapped, 'z', axis=0, tiled=True)]
    pallas_call x1, Pallas kernels: 19.2 us -> 21.7 us  [project_call(): pl.pallas_call(project_kernel, out_shape=jax.ShapeDtypeStruct((cap, width...]
  transfers between devices with their start and end apart: 1 -> 2, of which waited for: 0 -> 1; matrix products, arithmetic and copies ran while one was open for 0% -> 0% of each run, Pallas kernels for 79% -> 73%
where the time goes in v5:
time: 184 us; the launch traced here: 181 us
  Pallas kernels  154 us (84%)
  between operations  13.5 us (7%)
  waiting for transfers between devices  9.64 us (5%)
  local copies, waits for them, and re-layouts  4.54 us (2%)
    pallas_call x1, Pallas kernels, conv_call(): pl.pallas_call(functools.partial(conv_kernel, x_count, z_count), out_shap...  54.3 us
    pallas_call x1, Pallas kernels, spread_call(): pl.pallas_call(functools.partial(spread_kernel, z_count, y_count), out_sh...  50.3 us
    pallas_call x1, Pallas kernels, ring_call(): pl.pallas_call(functools.partial(ring_kernel, x_count, z_count), out_shap...  25.6 us
    pallas_call x1, Pallas kernels, project_call(): pl.pallas_call(project_kernel, out_shape=jax.ShapeDtypeStruct((cap, width...  21.7 us
    all_gather x1, waiting for transfers between devices, shards(): far_block = lax.all_gather(swapped, 'z', axis=0, tiled=True)  8.89 us
    unnamed x11, local copies, waits for them, and re-layouts  4.54 us
  transfers between devices with their start and end apart: 2, of which 1 were waited for; matrix products, arithmetic and copies ran while one was open for 0% of the time, Pallas kernels for 73%

profile of v5, /device:TPU:32, one launch (start us, length us, event | category | flops | bytes accessed | tf_op | source)
XLA Modules:
  0.0 181.2 jit_solution(18308873642106753245)
XLA Ops:
  6.5 0.0 copy-start.2
  6.5 0.0 copy-start.4
  6.5 0.0 copy-start.3
  6.5 0.0 all-gather.3.cloned.1.call-start
  6.5 0.7 all-gather.3.cloned.1.call-update
  7.3 0.0 all-gather.5.cloned.1.call-start
  7.3 54.3 %convolve.1 = (bf16[8,320,128]{2,1,0:T(8,128)(2,1)}, bf16[256,1024]{1,0:T(8,128)(2,1)}) custom-call(s32[32]{0:T(128)} %former.1, bf16[3,320,1024]{2,1,0:T(8,128)(2,1)} %bitcast.2, f32[3,3,1024]{2,1,0:T(4,128)} %taps_far.1, f32[16,1024]{1,0:T(8,128)} %residue_far.1, f32[16,1024]{1,0:T(8,128)} %damping_far.1, f32[1,1024]{1,0:T(1,128)} %bitcast.3, ...), custom_call_target="tpu_custom_call" | custom-call | tf_op jit(solution)/shard_map/convolve/pallas_call | solution.py:321
  61.6 0.0 all-gather.5.cloned.1.call-update
  61.7 25.6 %ring_rows.1.pieces = bf16[32,320,128]{2,1,0:T(8,128)(2,1)} custom-call(bf16[8,320,128]{2,1,0:T(8,128)(2,1)} %get-tuple-element.7.own), custom_call_target="tpu_custom_call" | custom-call | tf_op jit(solution)/shard_map/ring_rows/pallas_call | solution.py:434
  87.3 0.0 copy-done.2
  87.3 0.0 copy-done.4
  87.3 0.0 copy-done.3
  87.3 0.0 copy-start
  87.3 1.7 copy-done
  89.0 1.6 reorder_rows.1.chosen
  90.6 0.0 copy-start.1
  90.6 0.8 copy-done.1
  91.5 50.3 %spread_rows.1.rows_far = bf16[2,320,4096]{2,1,0:T(8,128)(2,1)} custom-call(bf16[8,320,128]{2,1,0:T(8,128)(2,1)} %copy-done.1), custom_call_target="tpu_custom_call" | custom-call | tf_op jit(solution)/shard_map/spread_rows/pallas_call | solution.py:651
  141.8 0.0 all-gather.3.cloned.1.call-done.near_block
  141.8 8.9 %all-gather.5.cloned.1.call-done.far_block = bf16[2048,1024]{1,0:T(8,128)(2,1)} async-done(((bf16[256,1024]{1,0:T(8,128)(2,1)}), bf16[2048,1024]{1,0:T(8,128)(2,1)}) %all-gather.5.cloned.1.call-update) | async-done | bytes 4194320 | tf_op jit(solution)/shard_map/all_gather | solution.py:793
  150.7 21.7 %project_rows.1 = bf16[320,1024]{1,0:T(8,128)(2,1)} custom-call(bf16[2,320,4096]{2,1,0:T(8,128)(2,1)} %spread_rows.1.rows_far, bf16[2048,1024]{1,0:T(8,128)(2,1)} %all-gather.3.cloned.1.call-done.near_block, bf16[2048,1024]{1,0:T(8,128)(2,1)} %all-gather.5.cloned.1.call-done.far_block), custom_call_target="tpu_custom_call" | custom-call | tf_op jit(solution)/shard_map/project_rows/pallas_call | solution.py:747
  172.4 2.0 %copy.11 = bf16[320,1024]{1,0:T(8,128)(2,1)} copy(bf16[320,1024]{1,0:T(8,128)(2,1)} %project_rows.1) | data formatting | bytes 1310720
Async XLA Ops:
  6.5 80.7 %copy-start.2 = (s32[32]{0:T(128)S(1)}, s32[32]{0:T(128)}, u32[]{:S(2)}) copy-start(s32[32]{0:T(128)} %former.1) | copy-start | bytes 388
  6.5 80.7 %copy-start.4 = (s32[28]{0:T(128)S(1)}, s32[28]{0:T(128)}, u32[]{:S(2)}) copy-start(s32[28]{0:T(128)} %remaining.1) | copy-start | bytes 340
  6.5 80.8 %copy-start.3 = (s32[28]{0:T(128)S(1)}, s32[28]{0:T(128)}, u32[]{:S(2)}) copy-start(s32[28]{0:T(128)} %updated.1) | copy-start | bytes 340
  6.5 135.3 %all-gather.3.cloned.1.call-start = ((), (), s32[]{:S(2)}) async-start(), calls=%async_computation | async-start | bytes 4718592 | tf_op jit(solution)/shard_map/all_gather | solution.py:782
  7.3 143.4 %all-gather.5.cloned.1.call-start = ((), (), s32[]{:S(2)}) async-start(), calls=%async_computation.1 | async-start | bytes 4718592 | tf_op jit(solution)/shard_map/all_gather | solution.py:793
  87.3 1.7 copy-start
  90.6 0.8 copy-start.1
Sparse Core Ops, SparseCore 0:
  9.2 73.8 all-gather.2
  84.9 65.7 all-gather.4

commit v6 on v5

--- a/solution.py
+++ b/solution.py
@@ -24,6 +24,37 @@
     return {"x_high": x // 2, "x_low": lax.rem(x, 2)}
 
 
+def repack(quarters, k):
+    group = lax.broadcasted_iota(jnp.int32, quarters[0].shape, 1) // (LANES // 4)
+    result = jnp.zeros_like(quarters[0])
+    for q in range(4):
+        turned = pltpu.roll(quarters[q], ((q - k) % 4) * (LANES // 4), 1)
+        result = jnp.where(group == q, turned, result)
+    return result
+
+
+def block_step(step, z_count, my_z, held, passed, sems):
+    up_send, up_recv, down_send, down_recv = sems
+    rows = held.shape[1]
+    last = step == z_count // 2
+    half = rows // 2
+    copies = []
+    for source, to, first, send, recv in (
+        (my_z + 1 - step, my_z + 1, 0, up_send, up_recv),
+        (my_z - 1 + step, my_z - 1, half, down_send, down_recv),
+    ):
+        source = lax.rem(source + z_count, z_count)
+        at = pl.ds(first, half) if last else pl.ds(0, rows)
+        copies.append(
+            pltpu.make_async_remote_copy(
+                src_ref=held.at[source, at], dst_ref=passed.at[source, at],
+                send_sem=send.at[step - 1], recv_sem=recv.at[step - 1],
+                device_id={"z": lax.rem(to + z_count, z_count)}, device_id_type=MESH,
+            )
+        )
+    return copies
+
+
 def shift_down(value, by):
     row = lax.broadcasted_iota(jnp.int32, value.shape, 0)
     return jnp.where(row >= by, pltpu.roll(value, by, 0), 0.0)
@@ -38,10 +69,11 @@
 def conv_kernel(
     x_count, z_count,
     sizes, streams_far, taps_far, residue_far, damping_far, direct_far, block,
-    gathered, swapped,
+    gathered, blocks,
     streams, taps, residue, damping, direct, padded, tail, rates_own, query, gated, mixed, partial, ends, end_in, carry_out, carry_in, hidden, halo,
     halo_send, halo_recv, end_send, end_recv, carry_send, carry_recv,
-    z_send, z_recv, swap_send, swap_recv, load_sem, local_sem,
+    piece_send, piece_recv, swap_send, swap_recv, up_send, up_recv, down_send, down_recv,
+    load_sem, local_sem,
 ):
     modes = residue.shape[0]
     cap = streams.shape[1]
@@ -101,7 +133,7 @@
         )
 
     swap = pltpu.make_async_remote_copy(
-        src_ref=block, dst_ref=swapped, send_sem=swap_send, recv_sem=swap_recv,
+        src_ref=block, dst_ref=blocks.at[my_z], send_sem=swap_send, recv_sem=swap_recv,
         device_id={"x_low": 1 - lax.axis_index("x_low")}, device_id_type=MESH,
     )
     for distance in (1, 2):
@@ -157,6 +189,11 @@
             partial[g, m] = shift_down(total, 1)
             ends[m, pl.ds(g, 1), :] = total[SUBS - 1 : SUBS, :] * jnp.exp(rate * left_over)
 
+    swap.wait_recv()
+    block_sems = (up_send, up_recv, down_send, down_recv)
+    for copy in block_step(1, z_count, my_z, blocks, blocks, block_sems):
+        copy.start()
+
     def end_copy(owner):
         return pltpu.make_async_remote_copy(
             src_ref=ends.at[pl.ds(owner * per_owner, per_owner)], dst_ref=end_in.at[me],
@@ -231,19 +268,20 @@
         def _():
             carry_arrival(owner).wait_recv()
 
-    def z_copy(g):
-        return pltpu.make_async_remote_copy(
-            src_ref=hidden.at[g], dst_ref=gathered.at[my_z], send_sem=z_send.at[g],
-            recv_sem=z_recv.at[my_z], device_id={"z": g}, device_id_type=MESH,
-        )
-
-    def z_arrival(z):
-        return pltpu.make_async_remote_copy(
-            src_ref=hidden.at[0], dst_ref=gathered.at[z], send_sem=z_send.at[0],
-            recv_sem=z_recv.at[z], device_id={"z": z}, device_id_type=MESH,
-        )
-
-    own_copy = pltpu.make_async_copy(hidden.at[my_z], gathered.at[my_z], local_sem)
+    def piece_copy(x, z):
+        return pltpu.make_async_remote_copy(
+            src_ref=hidden.at[z, x], dst_ref=gathered.at[me], send_sem=piece_send.at[x, z],
+            recv_sem=piece_recv.at[me], device_id={**at_x(x), "z": z}, device_id_type=MESH,
+        )
+
+    def piece_arrival(source):
+        return pltpu.make_async_remote_copy(
+            src_ref=hidden.at[0, 0], dst_ref=gathered.at[source], send_sem=piece_send.at[0, 0],
+            recv_sem=piece_recv.at[source], device_id=seq_device(source), device_id_type=MESH,
+        )
+
+    own_copy = pltpu.make_async_copy(hidden.at[my_z, my_x], gathered.at[me], local_sem)
+    quarter = cap // 4
 
     @pl.loop(0, groups)
     def _(k):
@@ -269,26 +307,31 @@
 
         lax.fori_loop(0, step_rows, step, start, unroll=4)
         conv = mixed[...] + direct[0:1, at] * gated[g]
-        hidden[g] = (query[g] * conv).astype(jnp.bfloat16)
-
-        @pl.when(g != my_z)
+        value = query[g] * conv
+        quarters = [value[q * quarter : (q + 1) * quarter] for q in range(4)]
+        for x in range(x_count):
+            hidden[g, x] = repack(quarters, x).astype(jnp.bfloat16)
+
+            @pl.when(jnp.logical_or(g != my_z, x != my_x))
+            def _():
+                piece_copy(x, g).start()
+
+            @pl.when(jnp.logical_and(g == my_z, x == my_x))
+            def _():
+                own_copy.start()
+
+    own_copy.wait()
+
+    @pl.loop(0, seq_count)
+    def _(other):
+        @pl.when(other != me)
         def _():
-            z_copy(g).start()
-
-        @pl.when(g == my_z)
-        def _():
-            own_copy.start()
-
-    own_copy.wait()
-
-    @pl.loop(0, z_count)
-    def _(z):
-        @pl.when(z != my_z)
-        def _():
-            z_arrival(z).wait_recv()
-            z_copy(z).wait_send()
-
-    swap.wait()
+            piece_arrival(other).wait_recv()
+            piece_copy(other // z_count, lax.rem(other, z_count)).wait_send()
+
+    for copy in block_step(1, z_count, my_z, blocks, blocks, block_sems):
+        copy.wait()
+    swap.wait_send()
     for distance in (1, 2):
         halo_copy(distance).wait_send()
 
@@ -321,8 +364,8 @@
     return pl.pallas_call(
         functools.partial(conv_kernel, x_count, z_count),
         out_shape=[
-            jax.ShapeDtypeStruct((z_count, cap, LANES), bf16),
-            jax.ShapeDtypeStruct(block.shape, bf16),
+            jax.ShapeDtypeStruct((seq_count, cap // 4, LANES), bf16),
+            jax.ShapeDtypeStruct((z_count,) + block.shape, bf16),
         ],
         in_specs=[pl.BlockSpec(memory_space=pltpu.SMEM)] + [far] * 6,
         out_specs=[far, far],
@@ -343,13 +386,14 @@
             pltpu.VMEM((seq_count, per_owner, z_count, LANES), f32),
             pltpu.VMEM((seq_count, per_owner, z_count, LANES), f32),
             pltpu.VMEM((owners, per_owner, z_count, LANES), f32),
-            pltpu.VMEM((z_count, cap, LANES), bf16),
+            pltpu.VMEM((z_count, x_count, cap // 4, LANES), bf16),
             pltpu.VMEM((2, z_count, SUBS, LANES), f32),
             dma((2,)), dma((2,)),
             dma((owners,)), dma((seq_count,)), dma((seq_count,)), dma((owners,)),
         ]
-        + [dma((z_count,))] * 2
-        + [dma, dma, dma((5,)), dma],
+        + [dma((x_count, z_count)), dma((seq_count,)), dma, dma]
+        + [dma((1,))] * 4
+        + [dma((5,)), dma],
         compiler_params=pltpu.CompilerParams(
             collective_id=0, has_side_effects=True, vmem_limit_bytes=VMEM
         ),
@@ -357,137 +401,53 @@
     )(sizes, streams, taps, residue, damping, direct, block)
 
 
-def ring_kernel(
-    x_count, z_count,
-    own, gathered,
-    right_send, right_recv, left_send, left_recv,
-    far_a_send, far_a_recv, far_b_send, far_b_recv, local_sem,
-):
-    my_x = x_index()
-    cap = own.shape[1]
-    half = cap // 2
-    right, left = lax.rem(my_x + 1, x_count), lax.rem(my_x + x_count - 1, x_count)
-    opposite = lax.rem(my_x + 2, x_count)
-    local = pltpu.make_async_copy(
-        own, gathered.at[pl.ds(my_x * z_count, z_count)], local_sem
-    )
-    local.start()
-    barrier = pltpu.get_barrier_semaphore()
-    for to in (right, left):
-        pl.semaphore_signal(barrier, inc=1, device_id=at_x(to), device_id_type=MESH)
-    pl.semaphore_wait(barrier, 2)
-
-    def x_copy(source, source_x, z, to, send, recv, first, rows):
-        at = pl.ds(first, rows)
-        return pltpu.make_async_remote_copy(
-            src_ref=source.at[at], dst_ref=gathered.at[source_x * z_count + z, at],
-            send_sem=send.at[z], recv_sem=recv.at[z], device_id=at_x(to), device_id_type=MESH,
-        )
-
-    def to_right(source_x, z):
-        return x_copy(own.at[z], source_x, z, right, right_send, right_recv, 0, cap)
-
-    def to_left(source_x, z):
-        return x_copy(own.at[z], source_x, z, left, left_send, left_recv, 0, cap)
-
-    def onward(source_x, z):
-        return gathered.at[source_x * z_count + z]
-
-    def far_right(source_x, z):
-        return x_copy(
-            onward(source_x, z), source_x, z, right, far_a_send, far_a_recv, 0, half
-        )
-
-    def far_left(source_x, z):
-        return x_copy(
-            onward(source_x, z), source_x, z, left, far_b_send, far_b_recv, half, half
-        )
-
-    @pl.loop(0, z_count)
-    def _(z):
-        to_right(my_x, z).start()
-        to_left(my_x, z).start()
-
-    @pl.loop(0, z_count)
-    def _(z):
-        to_right(left, z).wait_recv()
-        far_right(left, z).start()
-        to_left(right, z).wait_recv()
-        far_left(right, z).start()
-
-    local.wait()
-
-    @pl.loop(0, z_count)
-    def _(z):
-        far_right(opposite, z).wait_recv()
-        far_left(opposite, z).wait_recv()
-        far_right(left, z).wait_send()
-        far_left(right, z).wait_send()
-        to_right(my_x, z).wait_send()
-        to_left(my_x, z).wait_send()
-
-
-def ring_call(dims, own):
-    x_count, z_count = dims["x"], dims["z"]
-    dma = pltpu.SemaphoreType.DMA
-    far = pl.BlockSpec(memory_space=pl.ANY)
-    return pl.pallas_call(
-        functools.partial(ring_kernel, x_count, z_count),
-        out_shape=jax.ShapeDtypeStruct((x_count * z_count,) + own.shape[1:], own.dtype),
-        in_specs=[far],
-        out_specs=far,
-        scratch_shapes=[dma((z_count,))] * 8 + [dma],
-        compiler_params=pltpu.CompilerParams(collective_id=3, has_side_effects=True),
-        name="ring_rows",
-    )(own)
-
-
-def select_kernel(z_count, former, updated, remaining, pieces, chosen, sequence):
-    seq_count, cap, _ = pieces.shape
+def select_kernel(former, updated, remaining, pieces, chosen, sequence):
+    seq_count, quarter, _ = pieces.shape
+    lane_group = LANES // 4
 
     def place(s, start):
-        sequence[pl.ds(start, cap), :] = pieces[s].astype(jnp.float32)
+        piece = pieces[s].astype(jnp.float32)
+        for q in range(4):
+            turned = pltpu.roll(piece, (4 - q) % 4 * lane_group, 1)
+            sequence[pl.ds(start + q * quarter, quarter), :] = turned
         return start + former[s]
 
     lax.fori_loop(0, seq_count, place, 0)
-    row = lax.broadcasted_iota(jnp.int32, (cap, LANES), 0)
-    first = x_index() * z_count
+    row = lax.broadcasted_iota(jnp.int32, (quarter, LANES), 0)
     chosen[...] = jnp.zeros_like(chosen)
 
     def pick(k, start):
-        own = remaining[k] - first
-
-        @pl.when(jnp.logical_and(own >= 0, own < z_count))
-        def _():
-            rows = sequence[pl.ds(start, cap), :]
-            chosen[own] = jnp.where(row < updated[k], rows, 0.0).astype(jnp.bfloat16)
-
+        quarters = []
+        for q in range(4):
+            rows = sequence[pl.ds(start + q * quarter, quarter), :]
+            quarters.append(jnp.where(row + q * quarter < updated[k], rows, 0.0))
+        chosen[remaining[k]] = repack(quarters, 0).astype(jnp.bfloat16)
         return start + updated[k]
 
     lax.fori_loop(0, updated.shape[0], pick, 0)
 
 
-def select_call(dims, seq_len, pieces, former, updated, remaining):
-    cap = pieces.shape[1]
+def select_call(seq_len, pieces, former, updated, remaining):
     smem = pl.BlockSpec(memory_space=pltpu.SMEM)
     vmem = pl.BlockSpec(memory_space=pltpu.VMEM)
     return pl.pallas_call(
-        functools.partial(select_kernel, dims["z"]),
-        out_shape=jax.ShapeDtypeStruct((dims["z"], cap, LANES), jnp.bfloat16),
+        select_kernel,
+        out_shape=jax.ShapeDtypeStruct(pieces.shape, jnp.bfloat16),
         in_specs=[smem] * 3 + [vmem],
         out_specs=vmem,
-        scratch_shapes=[pltpu.VMEM((seq_len + cap, LANES), jnp.float32)],
+        scratch_shapes=[pltpu.VMEM((seq_len + 4 * pieces.shape[1], LANES), jnp.float32)],
         compiler_params=pltpu.CompilerParams(vmem_limit_bytes=24 << 20),
         name="reorder_rows",
     )(former, updated, remaining, pieces)
 
 
 def spread_kernel(
-    z_count, y_count,
-    chosen, rows_in,
-    z_send, z_recv, right_send, right_recv, left_send, left_recv,
+    x_count, z_count, y_count,
+    chosen, held, rows_in, passed,
+    landing, pieces,
+    piece_send, piece_recv, right_send, right_recv, left_send, left_recv,
     far_a_send, far_a_recv, far_b_send, far_b_recv, core_send, core_recv,
-    local_sem,
+    up_send, up_recv, down_send, down_recv, own_sem, local_sem,
 ):
     cap = rows_in.shape[1]
     my_x, my_z = x_index(), lax.axis_index("z")
@@ -495,36 +455,56 @@
     right, left = lax.rem(my_y + 1, y_count), lax.rem(my_y + y_count - 1, y_count)
     opposite = lax.rem(my_y + 2, y_count)
     other = 1 - my_core
-    half = cap // 2
+    half, quarter = cap // 2, cap // 4
     stays = my_x // 2 == my_y // 2
-    target_x = jnp.where(stays, my_x, 3 - my_x)
-    target_y = jnp.where(stays, my_y, 3 - my_y)
-
-    def crossed(z):
-        return {**at_x(target_x), "y": target_y, "z": z}
-
-    def is_me(z):
-        return jnp.logical_and(stays, z == my_z)
+    source_row = jnp.where(stays, my_y, 3 - my_y)
+
+    def target(x, z):
+        native = x // 2 == my_y // 2
+        return {
+            **at_x(jnp.where(native, x, 3 - x)),
+            "y": jnp.where(native, my_y, 3 - my_y),
+            "z": z,
+        }
+
+    def is_me(x, z):
+        return jnp.logical_and(stays, jnp.logical_and(x == my_x, z == my_z))
 
     barrier = pltpu.get_barrier_semaphore()
 
     @pl.loop(0, z_count)
     def _(k):
         z = lax.rem(my_z + k, z_count)
-
-        @pl.when(jnp.logical_not(is_me(z)))
-        def _():
-            pl.semaphore_signal(barrier, inc=1, device_id=crossed(z), device_id_type=MESH)
-
-    for to in ({"y": right}, {"y": left}, {"core": other}):
+        for x in range(x_count):
+
+            @pl.when(jnp.logical_not(is_me(x, z)))
+            def _():
+                pl.semaphore_signal(
+                    barrier, inc=1, device_id={**at_x(x), "y": source_row, "z": z},
+                    device_id_type=MESH,
+                )
+
+    up, down = lax.rem(my_z + 1, z_count), lax.rem(my_z + z_count - 1, z_count)
+    for to in ({"y": right}, {"y": left}, {"core": other}, {"z": up}, {"z": down}):
         pl.semaphore_signal(barrier, inc=1, device_id=to, device_id_type=MESH)
+
     @pl.when(stays)
     def _():
-        pl.semaphore_wait(barrier, z_count - 1 + 3)
+        pl.semaphore_wait(barrier, x_count * z_count - 1 + 5)
 
     @pl.when(jnp.logical_not(stays))
     def _():
-        pl.semaphore_wait(barrier, z_count + 3)
+        pl.semaphore_wait(barrier, x_count * z_count + 5)
+
+    block_sems = (up_send, up_recv, down_send, down_recv)
+
+    def steps(step):
+        return block_step(step, z_count, my_z, held if step == 2 else passed, passed, block_sems)
+
+    last_step = z_count // 2
+    if last_step >= 2:
+        for copy in steps(2):
+            copy.start()
 
     def columns(source_y, core, z):
         block = (lax.rem(source_y, 2) * 2 + core) * z_count + z
@@ -537,22 +517,23 @@
             jnp.where(native, 0, 1), pl.ds(first, rows), columns(source_y, core, z)
         ]
 
-    def z_copy(z):
-        return pltpu.make_async_remote_copy(
-            src_ref=chosen.at[z], dst_ref=rows_in.at[jnp.where(stays, 0, 1), :, columns(my_y, my_core, my_z)],
-            send_sem=z_send.at[z], recv_sem=z_recv.at[my_z],
-            device_id=crossed(z), device_id_type=MESH,
-        )
-
-    def z_arrival(z):
-        return pltpu.make_async_remote_copy(
-            src_ref=chosen.at[0], dst_ref=place(my_y, my_core, z, 0, cap),
-            send_sem=z_send.at[0], recv_sem=z_recv.at[z],
-            device_id=crossed(z), device_id_type=MESH,
+    def piece_copy(x, z):
+        owner = x * z_count + z
+        return pltpu.make_async_remote_copy(
+            src_ref=chosen.at[owner], dst_ref=landing.at[my_x, my_z],
+            send_sem=piece_send.at[owner], recv_sem=piece_recv.at[my_x, my_z],
+            device_id=target(x, z), device_id_type=MESH,
+        )
+
+    def piece_arrival(x, z):
+        return pltpu.make_async_remote_copy(
+            src_ref=chosen.at[0], dst_ref=landing.at[x, z],
+            send_sem=piece_send.at[0], recv_sem=piece_recv.at[x, z],
+            device_id={**at_x(x), "y": source_row, "z": z}, device_id_type=MESH,
         )
 
     own_copy = pltpu.make_async_copy(
-        chosen.at[my_z], rows_in.at[0, :, columns(my_y, my_core, my_z)], local_sem
+        chosen.at[my_x * z_count + my_z], landing.at[my_x, my_z], own_sem
     )
 
     @pl.when(stays)
@@ -562,23 +543,28 @@
     @pl.loop(0, z_count)
     def _(k):
         z = lax.rem(my_z + k, z_count)
-
-        @pl.when(jnp.logical_not(is_me(z)))
-        def _():
-            z_copy(z).start()
-
-    def onward(y, core, z, to, send, recv, first, rows):
+        for x in range(x_count):
+
+            @pl.when(jnp.logical_not(is_me(x, z)))
+            def _():
+                piece_copy(x, z).start()
+
+    def onward(y, core, z, to, send, recv, first, rows, source=None):
         view = place(y, core, z, first, rows)
         return pltpu.make_async_remote_copy(
-            src_ref=view, dst_ref=view, send_sem=send, recv_sem=recv,
-            device_id=to, device_id_type=MESH,
+            src_ref=view if source is None else source, dst_ref=view, send_sem=send,
+            recv_sem=recv, device_id=to, device_id_type=MESH,
         )
 
     def to_right(y, z):
-        return onward(y, my_core, z, {"y": right}, right_send.at[z], right_recv.at[z], 0, cap)
+        return onward(
+            y, my_core, z, {"y": right}, right_send.at[z], right_recv.at[z], 0, cap, pieces.at[z]
+        )
 
     def to_left(y, z):
-        return onward(y, my_core, z, {"y": left}, left_send.at[z], left_recv.at[z], 0, cap)
+        return onward(
+            y, my_core, z, {"y": left}, left_send.at[z], left_recv.at[z], 0, cap, pieces.at[z]
+        )
 
     def far_right(y, z):
         return onward(y, my_core, z, {"y": right}, far_a_send.at[z], far_a_recv.at[z], 0, half)
@@ -586,8 +572,15 @@
     def far_left(y, z):
         return onward(y, my_core, z, {"y": left}, far_b_send.at[z], far_b_recv.at[z], half, half)
 
-    def to_core(y, core, z):
-        return onward(y, core, z, {"core": other}, core_send.at[y, z], core_recv.at[y, z], 0, cap)
+    def to_core(y, core, z, source=None):
+        return onward(
+            y, core, z, {"core": other}, core_send.at[y, z], core_recv.at[y, z], 0, cap, source
+        )
+
+    def keep(z):
+        return pltpu.make_async_copy(
+            pieces.at[z], place(my_y, my_core, z, 0, cap), local_sem.at[z]
+        )
 
     def arrival_order(k):
         return lax.rem(my_z + z_count - k, z_count)
@@ -600,17 +593,23 @@
         def _():
             z = arrival_order(k)
 
-            @pl.when(jnp.logical_not(is_me(z)))
-            def _():
-                z_arrival(z).wait_recv()
-
-            @pl.when(is_me(z))
-            def _():
-                own_copy.wait()
-
+            for x in range(x_count):
+
+                @pl.when(jnp.logical_not(is_me(x, z)))
+                def _():
+                    piece_arrival(x, z).wait_recv()
+
+                @pl.when(is_me(x, z))
+                def _():
+                    own_copy.wait()
+
+            packed = [landing[x, z].astype(jnp.float32) for x in range(x_count)]
+            for q in range(4):
+                pieces[z, q * quarter : (q + 1) * quarter] = repack(packed, q).astype(jnp.bfloat16)
             to_right(my_y, z).start()
             to_left(my_y, z).start()
-            to_core(my_y, my_core, z).start()
+            to_core(my_y, my_core, z, pieces.at[z]).start()
+            keep(z).start()
 
         @pl.when(k >= lag)
         def _():
@@ -622,12 +621,24 @@
             far_left(right, z).start()
             to_core(right, my_core, z).start()
 
+    if last_step >= 3:
+        for copy in steps(2):
+            copy.wait_recv()
+        for copy in steps(3):
+            copy.start()
+
     @pl.loop(0, z_count)
     def _(k):
         z = arrival_order(k)
         far_right(opposite, z).wait_recv()
         far_left(opposite, z).wait_recv()
         to_core(opposite, my_core, z).start()
+
+    if last_step >= 4:
+        for copy in steps(3):
+            copy.wait_recv()
+        for copy in steps(4):
+            copy.start()
 
     @pl.loop(0, z_count)
     def _(z):
@@ -639,36 +650,60 @@
         far_right(left, z).wait_send()
         far_left(right, z).wait_send()
 
-        @pl.when(jnp.logical_not(is_me(z)))
-        def _():
-            z_copy(z).wait_send()
-
-
-def spread_call(dims, chosen):
-    z_count, cap, _ = chosen.shape
-    y_count = dims["y"]
+        keep(z).wait()
+        for x in range(x_count):
+
+            @pl.when(jnp.logical_not(is_me(x, z)))
+            def _():
+                piece_copy(x, z).wait_send()
+
+    for step in range(2, last_step + 1):
+        for copy in steps(step):
+            copy.wait_send()
+            if step == last_step:
+                copy.wait_recv()
+
+
+def spread_call(dims, chosen, held):
+    x_count, y_count, z_count = dims["x"], dims["y"], dims["z"]
+    cap = chosen.shape[1] * 4
+    bf16 = jnp.bfloat16
     dma = pltpu.SemaphoreType.DMA
+    far = pl.BlockSpec(memory_space=pl.ANY)
     return pl.pallas_call(
-        functools.partial(spread_kernel, z_count, y_count),
-        out_shape=jax.ShapeDtypeStruct((2, cap, y_count * z_count * LANES), jnp.bfloat16),
-        in_specs=[pl.BlockSpec(memory_space=pltpu.VMEM)],
-        out_specs=pl.BlockSpec(memory_space=pl.ANY),
-        scratch_shapes=[dma((z_count,))] * 10 + [dma((y_count, z_count))] * 2 + [dma],
+        functools.partial(spread_kernel, x_count, z_count, y_count),
+        out_shape=[
+            jax.ShapeDtypeStruct((2, cap, y_count * z_count * LANES), bf16),
+            jax.ShapeDtypeStruct(held.shape, bf16),
+        ],
+        in_specs=[pl.BlockSpec(memory_space=pltpu.VMEM), far],
+        out_specs=[far, far],
+        scratch_shapes=[
+            pltpu.VMEM((x_count, z_count, cap // 4, LANES), bf16),
+            pltpu.VMEM((z_count, cap, LANES), bf16),
+            dma((x_count * z_count,)), dma((x_count, z_count)),
+        ]
+        + [dma((z_count,))] * 8
+        + [dma((y_count, z_count))] * 2
+        + [dma((max(1, z_count // 2),))] * 4
+        + [dma, dma((z_count,))],
         compiler_params=pltpu.CompilerParams(
             collective_id=1, has_side_effects=True, vmem_limit_bytes=VMEM
         ),
         name="spread_rows",
-    )(chosen)
+    )(chosen, held)
 
 
 def project_kernel(
-    rows_far, near_block, far_block, out,
+    rows_far, near_block, held, passed, out,
     rows, weights, own_sum, partial_out, partial_in,
     rows_sem, load_sem, sum_send, sum_recv,
 ):
-    parts, depth, tile = weights.shape
+    depth, width = weights.shape
+    parts, _, tile = partial_out.shape
     half = depth // 2
-    my_low = lax.axis_index("x_low")
+    z_count, block_rows, _ = held.shape
+    my_low, my_z = lax.axis_index("x_low"), lax.axis_index("z")
     partner = at_x(3 - x_index())
 
     barrier = pltpu.get_barrier_semaphore()
@@ -677,22 +712,28 @@
     def span(part):
         return pl.ds(pl.multiple_of(part * tile, tile), tile)
 
-    def load(block, low, part, sem):
-        first = pl.multiple_of(low * half, half)
-        return pltpu.make_async_copy(
-            block.at[:, span(part)], weights.at[part, pl.ds(first, half)], sem.at[part]
-        )
-
-    def near(part):
-        return load(near_block, my_low, part, load_sem.at[0])
-
-    def far(part):
-        return load(far_block, 1 - my_low, part, load_sem.at[1])
+    loads = [
+        pltpu.make_async_copy(
+            near_block, weights.at[pl.ds(pl.multiple_of(my_low * half, half), half)],
+            load_sem.at[z_count],
+        )
+    ]
+    for d in range(z_count):
+        z = lax.rem(my_z + d, z_count)
+        first = pl.multiple_of((1 - my_low) * half + z * block_rows, block_rows)
+        loads.append(
+            pltpu.make_async_copy(
+                (held if min(d, z_count - d) <= 1 and 2 * d != z_count or z_count == 2 else passed).at[z],
+                weights.at[pl.ds(first, block_rows)], load_sem.at[d],
+            )
+        )
 
     def row_load(k):
         return pltpu.make_async_copy(rows_far.at[k], rows.at[k], rows_sem.at[k])
 
     row_load(1).start()
+    for load in loads:
+        load.start()
 
     def exchange(part):
         return pltpu.make_async_remote_copy(
@@ -701,29 +742,26 @@
             device_id=partner, device_id_type=MESH,
         )
 
+    row_load(0).start()
+    row_load(1).wait()
+    for load in loads:
+        load.wait()
+    pl.semaphore_wait(barrier, 1)
+
     @pl.loop(0, parts)
     def _(part):
-        near(part).start()
-        far(part).start()
-
-    row_load(0).start()
-    row_load(1).wait()
-    pl.semaphore_wait(barrier, 1)
+        partial_out[part] = jnp.dot(
+            rows[1], weights[:, span(part)], preferred_element_type=jnp.float32
+        ).astype(jnp.bfloat16)
+        exchange(part).start()
+
+    row_load(0).wait()
 
     @pl.loop(0, parts)
     def _(part):
-        near(part).wait()
-        far(part).wait()
-        partial_out[part] = jnp.dot(
-            rows[1], weights[part], preferred_element_type=jnp.float32
-        ).astype(jnp.bfloat16)
-        exchange(part).start()
-
-    row_load(0).wait()
-
-    @pl.loop(0, parts)
-    def _(part):
-        own_sum[part] = jnp.dot(rows[0], weights[part], preferred_element_type=jnp.float32)
+        own_sum[part] = jnp.dot(
+            rows[0], weights[:, span(part)], preferred_element_type=jnp.float32
+        )
 
     @pl.loop(0, parts)
     def _(part):
@@ -736,7 +774,7 @@
         exchange(part).wait_send()
 
 
-def project_call(rows, near_block, far_block):
+def project_call(rows, near_block, held, passed):
     _, cap, depth = rows.shape
     width = near_block.shape[1]
     tile = min(256, width)
@@ -747,21 +785,21 @@
     return pl.pallas_call(
         project_kernel,
         out_shape=jax.ShapeDtypeStruct((cap, width), bf16),
-        in_specs=[pl.BlockSpec(memory_space=pl.ANY)] * 3,
+        in_specs=[pl.BlockSpec(memory_space=pl.ANY)] * 4,
         out_specs=vmem,
         scratch_shapes=[
             pltpu.VMEM(rows.shape, bf16),
-            pltpu.VMEM((parts, depth, tile), bf16),
+            pltpu.VMEM((depth, width), bf16),
             pltpu.VMEM((parts, cap, tile), f32),
             pltpu.VMEM((parts, cap, tile), bf16),
             pltpu.VMEM((parts, cap, tile), bf16),
-            dma((2,)), dma((2, parts)), dma((parts,)), dma((parts,)),
+            dma((2,)), dma((held.shape[0] + 1,)), dma((parts,)), dma((parts,)),
         ],
         compiler_params=pltpu.CompilerParams(
             collective_id=2, has_side_effects=True, vmem_limit_bytes=VMEM
         ),
         name="project_rows",
-    )(rows, near_block, far_block)
+    )(rows, near_block, held, passed)
 
 
 def shards(
@@ -780,7 +818,7 @@
     seq_len = cap * 4 // 5 * dims["x"] * dims["z"]
 
     near_block = lax.all_gather(final_projector, "z", axis=0, tiled=True)
-    own, swapped = conv_call(
+    pieces, held = conv_call(
         dims,
         jnp.transpose(input_triple_streams, (1, 0, 2)),
         former_piece_sizes,
@@ -790,12 +828,11 @@
         direct_coefficient[None, :],
         final_projector,
     )
-    far_block = lax.all_gather(swapped, "z", axis=0, tiled=True)
-    pieces = ring_call(dims, own)
     chosen = select_call(
-        dims, seq_len, pieces, former_piece_sizes, updated_piece_sizes, remaining_indices
+        seq_len, pieces, former_piece_sizes, updated_piece_sizes, remaining_indices
     )
-    return project_call(spread_call(dims, chosen), near_block, far_block)
+    rows, passed = spread_call(dims, chosen, held)
+    return project_call(rows, near_block, held, passed)
 
 
 def solution(mesh):

time: 184 us -> 200 us (1.087); the launches traced: 181 us -> 199 us
  Pallas kernels: 154 us -> 179 us
  waiting for transfers between devices: 9.64 us -> 0.73 us
    pallas_call x1, Pallas kernels: 54.3 us -> 83.5 us  [conv_call(): pl.pallas_call(functools.partial(conv_kernel, x_count, z_count), out_shap...]
    all_gather x1 -> x0, waiting for transfers between devices: 8.89 us -> none  [shards(): far_block = lax.all_gather(swapped, 'z', axis=0, tiled=True)]
    pallas_call x1, Pallas kernels: 21.7 us -> 19.4 us  [project_call(): pl.pallas_call(project_kernel, out_shape=jax.ShapeDtypeStruct((cap, width...]
    pallas_call x3 -> x2, Pallas kernels: 77.5 us -> 76.4 us  [the longest x1 70.5 us: spread_call(): pl.pallas_call(functools.partial(spread_kernel, x_count, z_count, y_count...]
  transfers between devices with their start and end apart: 2 -> 1, of which waited for: 1 -> 0; matrix products, arithmetic and copies ran while one was open for 0% -> 0% of each run, Pallas kernels for 73% -> 80%
where the time goes in v6:
time: 200 us; the launch traced here: 199 us
  Pallas kernels  179 us (90%)
  between operations  13.4 us (7%)
  local copies, waits for them, and re-layouts  5.84 us (3%)
    pallas_call x1, Pallas kernels, conv_call(): pl.pallas_call(functools.partial(conv_kernel, x_count, z_count), out_shap...  83.5 us
    pallas_call x1, Pallas kernels, spread_call(): pl.pallas_call(functools.partial(spread_kernel, x_count, z_count, y_count...  70.5 us
    pallas_call x1, Pallas kernels, project_call(): pl.pallas_call(project_kernel, out_shape=jax.ShapeDtypeStruct((cap, width...  19.4 us
    pallas_call x1, Pallas kernels, select_call(): pl.pallas_call(select_kernel, out_shape=jax.ShapeDtypeStruct(pieces.shape...  5.94 us
    unnamed x11, local copies, waits for them, and re-layouts  5.84 us
  transfers between devices with their start and end apart: 1, of which 0 were waited for; matrix products, arithmetic and copies ran while one was open for 0% of the time, Pallas kernels for 80%

profile of v6, /device:TPU:32, one launch (start us, length us, event | category | flops | bytes accessed | tf_op | source)
XLA Modules:
  0.0 199.3 jit_solution(16292496792089093854)
XLA Ops:
  6.5 0.0 all-gather.2.cloned.1.call-start
  6.5 0.7 all-gather.2.cloned.1.call-update
  7.3 83.5 %convolve.1 = (bf16[32,80,128]{2,1,0:T(8,128)(2,1)}, bf16[8,256,1024]{2,1,0:T(8,128)(2,1)}) custom-call(s32[32]{0:T(128)} %former.1, bf16[3,320,1024]{2,1,0:T(8,128)(2,1)} %bitcast.2, f32[3,3,1024]{2,1,0:T(4,128)} %taps_far.1, f32[16,1024]{1,0:T(8,128)} %residue_far.1, f32[16,1024]{1,0:T(8,128)} %damping_far.1, f32[1,1024]{1,0:T(1,128)} %bitcast.3, ...), custom_call_target="tpu_custom_call" | custom-call | tf_op jit(solution)/shard_map/convolve/pallas_call | solution.py:364
  90.8 0.0 copy-start.1
  90.8 1.1 copy-done.1
  91.9 0.0 copy-start.2
  91.9 0.7 copy-done.2
  92.6 0.0 copy-start.3
  92.6 0.7 copy-done.3
  93.2 0.0 copy-start.4
  93.2 0.7 copy-done.4
  93.9 5.9 %reorder_rows.1.chosen = bf16[32,80,128]{2,1,0:T(8,128)(2,1)S(1)} custom-call(s32[32]{0:T(128)S(1)} %copy-done.2, s32[28]{0:T(128)S(1)} %copy-done.3, s32[28]{0:T(128)S(1)} %copy-done.4, bf16[32,80,128]{2,1,0:T(8,128)(2,1)S(1)} %copy-done.1), custom_call_target="tpu_custom_call" | custom-call | tf_op jit(solution)/shard_map/reorder_rows/pallas_call | solution.py:433
  99.8 0.0 copy-start
  99.8 0.8 copy-done
  100.6 70.5 %spread_rows.1 = (bf16[2,320,4096]{2,1,0:T(8,128)(2,1)}, bf16[8,256,1024]{2,1,0:T(8,128)(2,1)}) custom-call(bf16[32,80,128]{2,1,0:T(8,128)(2,1)} %copy-done, bf16[8,256,1024]{2,1,0:T(8,128)(2,1)} %get-tuple-element.10.held), custom_call_target="tpu_custom_call" | custom-call | tf_op jit(solution)/shard_map/spread_rows/pallas_call | solution.py:673
  171.1 0.0 all-gather.2.cloned.1.call-done.near_block
  171.2 19.4 %project_rows.1 = bf16[320,1024]{1,0:T(8,128)(2,1)} custom-call(bf16[2,320,4096]{2,1,0:T(8,128)(2,1)} %get-tuple-element.11.rows_far, bf16[2048,1024]{1,0:T(8,128)(2,1)} %all-gather.2.cloned.1.call-done.near_block, bf16[8,256,1024]{2,1,0:T(8,128)(2,1)} %get-tuple-element.10.held, bf16[8,256,1024]{2,1,0:T(8,128)(2,1)} %get-tuple-element.12.passed), custom_call_target="tpu_custom_call" | custom-call | tf_op jit(solution)/shard_map/project_rows/pallas_call | solution.py:785
  190.5 2.0 copy.11
Async XLA Ops:
  6.5 164.6 %all-gather.2.cloned.1.call-start = ((), (), s32[]{:S(2)}) async-start(), calls=%async_computation | async-start | bytes 4718592 | tf_op jit(solution)/shard_map/all_gather | solution.py:820
  90.8 1.1 copy-start.1
  91.9 0.7 copy-start.2
  92.6 0.7 copy-start.3
  93.2 0.7 copy-start.4
  99.8 0.8 copy-start
Sparse Core Ops, SparseCore 0:
  9.1 85.1 all-gather.1

commit v7 on v3

v7 whole, which is shorter than its diff:
```python
import functools

import jax
import jax.numpy as jnp
from jax import lax
from jax.experimental import pallas as pl
from jax.experimental.pallas import tpu as pltpu
from jax.sharding import Mesh
from jax.sharding import PartitionSpec as P

MESH = pl.DeviceIdType.MESH
LANES = 128
VMEM = 56 << 20
SUBS = 8
AXES = ("x_high", "x_low", "z", "y", "core")
SEQ = ("x_high", "x_low", "z")


def x_index():
    return lax.axis_index("x_high") * 2 + lax.axis_index("x_low")


def at_x(x):
    return {"x_high": x // 2, "x_low": lax.rem(x, 2)}


def repack(quarters, k):
    group = lax.broadcasted_iota(jnp.int32, quarters[0].shape, 1) // (LANES // 4)
    result = jnp.zeros_like(quarters[0])
    for q in range(4):
        turned = pltpu.roll(quarters[q], ((q - k) % 4) * (LANES // 4), 1)
        result = jnp.where(group == q, turned, result)
    return result


def shift_down(value, by):
    row = lax.broadcasted_iota(jnp.int32, value.shape, 0)
    return jnp.where(row >= by, pltpu.roll(value, by, 0), 0.0)


def tree_sum(terms):
    while len(terms) > 1:
        terms = [a + b for a, b in zip(terms[::2], terms[1::2], strict=True)]
    return terms[0]


def conv_kernel(
    x_count, z_count,
    sizes, streams_far, taps_far, residue_far, damping_far, direct_far,
    gathered,
    streams, taps, residue, damping, direct, padded, tail, rates_own, query, gated, mixed, partial, ends, end_in, carry_out, carry_in, hidden, halo,
    halo_send, halo_recv, end_send, end_recv, carry_send, carry_recv,
    piece_send, piece_recv, load_sem, local_sem,
):
    modes = residue.shape[0]
    cap = streams.shape[1]
    groups = z_count
    step_rows = cap // SUBS
    seq_count = x_count * z_count
    per_owner = max(1, modes // seq_count)
    owners = modes // per_owner
    my_x, my_z, my_core = x_index(), lax.axis_index("z"), lax.axis_index("core")
    me = my_x * z_count + my_z
    valid = sizes[me]

    def seq_device(index):
        return {**at_x(index // z_count), "z": lax.rem(index, z_count)}

    source_core = my_z // (z_count // 2)

    @pl.when(source_core != lax.axis_index("core"))
    def _():
        @pl.loop(0, seq_count)
        def _(k):
            pl.semaphore_signal(
                pltpu.get_barrier_semaphore(), inc=1,
                device_id={**seq_device(lax.rem(me + k, seq_count)), "core": source_core},
                device_id_type=MESH,
            )

    loads = [
        pltpu.make_async_copy(far, near, load_sem.at[i])
        for i, (far, near) in enumerate((
            (streams_far, streams), (taps_far, taps), (residue_far, residue),
            (damping_far, damping), (direct_far, direct),
        ))
    ]
    for load in loads:
        load.start()

    def lanes(g):
        return pl.ds(pl.multiple_of(g * LANES, LANES), LANES)

    barrier = pltpu.get_barrier_semaphore()

    @pl.loop(1, seq_count)
    def _(k):
        pl.semaphore_signal(
            barrier, inc=1, device_id=seq_device(lax.rem(me + k, seq_count)), device_id_type=MESH
        )

    for load in loads:
        load.wait()
    last = SUBS - 1 + valid
    second = jnp.maximum(last - 1, SUBS)

    @pl.loop(0, groups)
    def _(g):
        for p in range(3):
            padded[p, g, SUBS : SUBS + cap, :] = streams[p, :, lanes(g)].astype(jnp.float32)
            tail[g, p : p + 1, :] = padded[p, g, pl.ds(last, 1), :]
            tail[g, 3 + p : 4 + p, :] = padded[p, g, pl.ds(second, 1), :]
        tail[g, 6:8, :] = jnp.zeros((2, LANES), jnp.float32)

    pl.semaphore_wait(barrier, seq_count - 1 + seq_count // 2)

    def halo_copy(distance):
        target = lax.rem(me + distance, seq_count)
        return pltpu.make_async_remote_copy(
            src_ref=tail, dst_ref=halo.at[distance - 1], send_sem=halo_send.at[distance - 1],
            recv_sem=halo_recv.at[distance - 1], device_id=seq_device(target), device_id_type=MESH,
        )

    for distance in (1, 2):
        halo_copy(distance).start()
    for distance in (1, 2):
        halo_copy(distance).wait_recv()

    row = lax.broadcasted_iota(jnp.int32, (cap, LANES), 0)
    before_size = sizes[lax.rem(me + seq_count - 1, seq_count)]

    @pl.loop(0, groups)
    def _(g):
        at = lanes(g)
        features = []
        for p in range(3):
            last_one = jnp.where(me >= 1, halo[0, g, p : p + 1, :], 0.0)
            own_second = halo[0, g, 3 + p : 4 + p, :]
            far_last = jnp.where(me >= 2, halo[1, g, p : p + 1, :], 0.0)
            last_two = jnp.where(me >= 1, jnp.where(before_size >= 2, own_second, far_last), 0.0)
            padded[p, g, 6:7, :] = last_two
            padded[p, g, 7:8, :] = last_one
            features.append(
                taps[p, 0:1, at] * padded[p, g, 8 : 8 + cap, :]
                + taps[p, 1:2, at] * padded[p, g, 7 : 7 + cap, :]
                + taps[p, 2:3, at] * padded[p, g, 6 : 6 + cap, :]
            )
        query[g] = features[0].astype(jnp.bfloat16).astype(jnp.float32)
        product = (features[1] * features[2]).astype(jnp.bfloat16).astype(jnp.float32)
        gated[g] = jnp.where(row < valid, product, 0.0)

    def mode_rows(ref, at):
        return [jnp.broadcast_to(ref[m : m + 1, at], (SUBS, LANES)) for m in range(modes)]

    @pl.loop(0, groups)
    def _(g):
        at = lanes(g)
        decay = [jnp.exp(-d) for d in mode_rows(damping, at)]
        weight = mode_rows(residue, at)

        def step(i, states):
            u = gated[g, pl.ds(i, SUBS, stride=step_rows), :]
            return tuple(a * h + r * u for a, h, r in zip(decay, states, weight, strict=True))

        zero = jnp.zeros((SUBS, LANES), jnp.float32)
        states = lax.fori_loop(0, step_rows, step, (zero,) * modes, unroll=4)
        left_over = (cap - valid).astype(jnp.float32)
        for m in range(modes):
            rate = damping[m : m + 1, at]
            total = states[m]
            for by in (1, 2, 4):
                total = total + jnp.exp(-rate * (step_rows * by)) * shift_down(total, by)
            partial[g, m] = shift_down(total, 1)
            ends[m, pl.ds(g, 1), :] = total[SUBS - 1 : SUBS, :] * jnp.exp(rate * left_over)

    def end_copy(owner):
        return pltpu.make_async_remote_copy(
            src_ref=ends.at[pl.ds(owner * per_owner, per_owner)], dst_ref=end_in.at[me],
            send_sem=end_send.at[owner], recv_sem=end_recv.at[me],
            device_id=seq_device(owner), device_id_type=MESH,
        )

    def end_arrival(source):
        return pltpu.make_async_remote_copy(
            src_ref=ends.at[pl.ds(0, per_owner)], dst_ref=end_in.at[source],
            send_sem=end_send.at[0], recv_sem=end_recv.at[source],
            device_id=seq_device(source), device_id_type=MESH,
        )

    def carry_copy(target):
        return pltpu.make_async_remote_copy(
            src_ref=carry_out.at[target], dst_ref=carry_in.at[me],
            send_sem=carry_send.at[target], recv_sem=carry_recv.at[me],
            device_id=seq_device(target), device_id_type=MESH,
        )

    def carry_arrival(owner):
        return pltpu.make_async_remote_copy(
            src_ref=carry_out.at[0], dst_ref=carry_in.at[owner],
            send_sem=carry_send.at[0], recv_sem=carry_recv.at[owner],
            device_id=seq_device(owner), device_id_type=MESH,
        )

    @pl.loop(0, owners)
    def _(k):
        owner = lax.rem(me + k, owners)

        @pl.when(owner != me)
        def _():
            end_copy(owner).start()

    @pl.when(me < owners)
    def _():
        end_in[me] = ends[pl.ds(me * per_owner, per_owner)]
        mode = lax.broadcasted_iota(jnp.int32, (modes, LANES), 0)
        for j in range(per_owner):
            for g in range(groups):
                block = damping[:, g * LANES : (g + 1) * LANES]
                rates_own[j, g : g + 1, :] = jnp.sum(
                    jnp.where(mode == me * per_owner + j, block, 0.0), axis=0, keepdims=True
                )

        @pl.loop(0, seq_count)
        def _(source):
            @pl.when(source != me)
            def _():
                end_arrival(source).wait_recv()

        rate = rates_own[...]

        def advance(source, carry):
            carry_out[source] = carry
            return jnp.exp(-rate * sizes[source].astype(jnp.float32)) * carry + end_in[source]

        lax.fori_loop(0, seq_count, advance, jnp.zeros_like(rate), unroll=8)
        carry_in[me] = carry_out[me]

        @pl.loop(0, seq_count)
        def _(target):
            @pl.when(target != me)
            def _():
                carry_copy(target).start()

    @pl.loop(0, owners)
    def _(owner):
        @pl.when(owner != me)
        def _():
            carry_arrival(owner).wait_recv()

    def goes_to(g):
        return my_core * (z_count // 2) + g // 2, lax.rem(g, 2)

    def is_me(x, g):
        z, core = goes_to(g)
        return jnp.logical_and(jnp.logical_and(x == my_x, z == my_z), core == my_core)

    def piece_copy(x, g):
        z, core = goes_to(g)
        return pltpu.make_async_remote_copy(
            src_ref=hidden.at[g, x], dst_ref=gathered.at[me], send_sem=piece_send.at[x, g],
            recv_sem=piece_recv.at[me], device_id={**at_x(x), "z": z, "core": core},
            device_id_type=MESH,
        )

    def piece_arrival(source):
        return pltpu.make_async_remote_copy(
            src_ref=hidden.at[0, 0], dst_ref=gathered.at[source], send_sem=piece_send.at[0, 0],
            recv_sem=piece_recv.at[source],
            device_id={**seq_device(source), "core": source_core}, device_id_type=MESH,
        )

    own_group = lax.rem(my_z, z_count // 2) * 2 + my_core
    own_copy = pltpu.make_async_copy(hidden.at[own_group, my_x], gathered.at[me], local_sem)
    quarter = cap // 4

    @pl.loop(0, groups)
    def _(k):
        g = lax.rem(my_z + 1 + k, groups)
        at = lanes(g)
        rates = mode_rows(damping, at)
        decay = [jnp.exp(-d) for d in rates]
        weight = mode_rows(residue, at)
        sub = lax.broadcasted_iota(jnp.int32, (SUBS, LANES), 0).astype(jnp.float32) * step_rows
        start = tuple(
            partial[g, m]
            + jnp.exp(-rates[m] * sub)
            * carry_in[m // per_owner, m % per_owner, pl.ds(g, 1), :]
            for m in range(modes)
        )

        def step(i, states):
            rows = pl.ds(i, SUBS, stride=step_rows)
            u = gated[g, rows, :]
            states = tuple(a * h + r * u for a, h, r in zip(decay, states, weight, strict=True))
            mixed[rows, :] = tree_sum(list(states))
            return states

        lax.fori_loop(0, step_rows, step, start, unroll=4)
        conv = mixed[...] + direct[0:1, at] * gated[g]
        value = query[g] * conv
        quarters = [value[q * quarter : (q + 1) * quarter] for q in range(4)]
        for x in range(x_count):
            hidden[g, x] = repack(quarters, x).astype(jnp.bfloat16)

            @pl.when(jnp.logical_not(is_me(x, g)))
            def _():
                piece_copy(x, g).start()

            @pl.when(is_me(x, g))
            def _():
                own_copy.start()

    from_self = source_core == my_core

    @pl.when(from_self)
    def _():
        own_copy.wait()

    @pl.loop(0, seq_count)
    def _(other):
        @pl.when(jnp.logical_not(jnp.logical_and(from_self, other == me)))
        def _():
            piece_arrival(other).wait_recv()

        x, g = other // z_count, lax.rem(other, z_count)

        @pl.when(jnp.logical_not(is_me(x, g)))
        def _():
            piece_copy(x, g).wait_send()

    for distance in (1, 2):
        halo_copy(distance).wait_send()

    @pl.loop(0, owners)
    def _(owner):
        @pl.when(owner != me)
        def _():
            end_copy(owner).wait_send()

    @pl.when(me < owners)
    def _():
        @pl.loop(0, seq_count)
        def _(target):
            @pl.when(target != me)
            def _():
                carry_copy(target).wait_send()


def conv_call(dims, streams, sizes, taps, residue, damping, direct):
    x_count, z_count = dims["x"], dims["z"]
    cap, width = streams.shape[1:]
    modes = residue.shape[0]
    seq_count = x_count * z_count
    per_owner = max(1, modes // seq_count)
    owners = modes // per_owner
    f32, bf16 = jnp.float32, jnp.bfloat16
    dma = pltpu.SemaphoreType.DMA
    vmem = pl.BlockSpec(memory_space=pltpu.VMEM)
    far = pl.BlockSpec(memory_space=pl.ANY)
    return pl.pallas_call(
        functools.partial(conv_kernel, x_count, z_count),
        out_shape=jax.ShapeDtypeStruct((seq_count, cap // 4, LANES), bf16),
        in_specs=[pl.BlockSpec(memory_space=pltpu.SMEM)] + [far] * 5,
        out_specs=far,
        scratch_shapes=[
            pltpu.VMEM(streams.shape, bf16),
            pltpu.VMEM(taps.shape, f32),
            pltpu.VMEM(residue.shape, f32),
            pltpu.VMEM(damping.shape, f32),
            pltpu.VMEM(direct.shape, f32),
            pltpu.VMEM((3, z_count, cap + SUBS, LANES), f32),
            pltpu.VMEM((z_count, SUBS, LANES), f32),
            pltpu.VMEM((per_owner, z_count, LANES), f32),
            pltpu.VMEM((z_count, cap, LANES), f32),
            pltpu.VMEM((z_count, cap, LANES), f32),
            pltpu.VMEM((cap, LANES), f32),
            pltpu.VMEM((z_count, modes, SUBS, LANES), f32),
            pltpu.VMEM((modes, z_count, LANES), f32),
            pltpu.VMEM((seq_count, per_owner, z_count, LANES), f32),
            pltpu.VMEM((seq_count, per_owner, z_count, LANES), f32),
            pltpu.VMEM((owners, per_owner, z_count, LANES), f32),
            pltpu.VMEM((z_count, x_count, cap // 4, LANES), bf16),
            pltpu.VMEM((2, z_count, SUBS, LANES), f32),
            dma((2,)), dma((2,)),
            dma((owners,)), dma((seq_count,)), dma((seq_count,)), dma((owners,)),
        ]
        + [dma((x_count, z_count)), dma((seq_count,)), dma((5,)), dma],
        compiler_params=pltpu.CompilerParams(
            collective_id=0, has_side_effects=True, vmem_limit_bytes=VMEM
        ),
        name="convolve",
    )(sizes, streams, taps, residue, damping, direct)


def select_kernel(former, updated, remaining, pieces, chosen, sequence):
    seq_count, quarter, _ = pieces.shape
    lane_group = LANES // 4

    def place(s, start):
        piece = pieces[s].astype(jnp.float32)
        for q in range(4):
            turned = pltpu.roll(piece, (4 - q) % 4 * lane_group, 1)
            sequence[pl.ds(start + q * quarter, quarter), :] = turned
        return start + former[s]

    lax.fori_loop(0, seq_count, place, 0)
    row = lax.broadcasted_iota(jnp.int32, (quarter, LANES), 0)
    chosen[...] = jnp.zeros_like(chosen)

    def pick(k, start):
        quarters = []
        for q in range(4):
            rows = sequence[pl.ds(start + q * quarter, quarter), :]
            quarters.append(jnp.where(row + q * quarter < updated[k], rows, 0.0))
        chosen[remaining[k]] = repack(quarters, 0).astype(jnp.bfloat16)
        return start + updated[k]

    lax.fori_loop(0, updated.shape[0], pick, 0)


def select_call(seq_len, pieces, former, updated, remaining):
    smem = pl.BlockSpec(memory_space=pltpu.SMEM)
    vmem = pl.BlockSpec(memory_space=pltpu.VMEM)
    return pl.pallas_call(
        select_kernel,
        out_shape=jax.ShapeDtypeStruct(pieces.shape, jnp.bfloat16),
        in_specs=[smem] * 3 + [vmem],
        out_specs=vmem,
        scratch_shapes=[pltpu.VMEM((seq_len + 4 * pieces.shape[1], LANES), jnp.float32)],
        compiler_params=pltpu.CompilerParams(vmem_limit_bytes=24 << 20),
        name="reorder_rows",
    )(former, updated, remaining, pieces)


def project_kernel(
    x_count, z_count, y_count,
    chosen, block, out,
    landing, rows_in, weights, sum_out, sum_in,
    load_sem, own_sem, piece_send, piece_recv,
    right_send, right_recv, left_send, left_recv,
    far_a_send, far_a_recv, far_b_send, far_b_recv, core_send, core_recv,
    sum_send, sum_recv,
):
    cap, width = out.shape
    part_width = width // 2
    half, quarter = cap // 2, cap // 4
    reach = z_count // 2
    my_x, my_z = x_index(), lax.axis_index("z")
    my_y, my_core = lax.axis_index("y"), lax.axis_index("core")
    right, left = lax.rem(my_y + 1, y_count), lax.rem(my_y + y_count - 1, y_count)
    opposite = lax.rem(my_y + 2, y_count)
    other = 1 - my_core
    above, below = lax.rem(my_z + 1, z_count), lax.rem(my_z + z_count - 1, z_count)

    load = pltpu.make_async_copy(block, weights, load_sem)
    load.start()
    own_copy = pltpu.make_async_copy(
        chosen.at[pl.ds(my_x * z_count, z_count)], landing.at[my_x], own_sem
    )
    own_copy.start()

    barrier = pltpu.get_barrier_semaphore()
    for k in range(1, x_count):
        pl.semaphore_signal(
            barrier, inc=1, device_id=at_x(lax.rem(my_x + k, x_count)), device_id_type=MESH
        )
    for to in ({"y": right}, {"y": left}, {"core": other}, {"z": above}, {"z": below}):
        pl.semaphore_signal(barrier, inc=1, device_id=to, device_id_type=MESH)
    pl.semaphore_wait(barrier, x_count - 1 + 5)

    def piece_copy(x):
        return pltpu.make_async_remote_copy(
            src_ref=chosen.at[pl.ds(x * z_count, z_count)], dst_ref=landing.at[my_x],
            send_sem=piece_send.at[x], recv_sem=piece_recv.at[my_x],
            device_id=at_x(x), device_id_type=MESH,
        )

    def piece_arrival(x):
        return pltpu.make_async_remote_copy(
            src_ref=chosen.at[pl.ds(0, z_count)], dst_ref=landing.at[x],
            send_sem=piece_send.at[x], recv_sem=piece_recv.at[x],
            device_id=at_x(x), device_id_type=MESH,
        )

    others = [lax.rem(my_x + k, x_count) for k in (1, 3, 2)]
    for x in others:
        piece_copy(x).start()

    def columns(y, core):
        return pl.ds(pl.multiple_of((y * 2 + core) * LANES, LANES), LANES)

    def onward(y, core, owner, to, send, recv, first, rows):
        view = rows_in.at[owner, pl.ds(first, rows), columns(y, core)]
        return pltpu.make_async_remote_copy(
            src_ref=view, dst_ref=view, send_sem=send, recv_sem=recv,
            device_id=to, device_id_type=MESH,
        )

    def to_right(y, o):
        return onward(y, my_core, o, {"y": right}, right_send.at[o], right_recv.at[o], 0, cap)

    def to_left(y, o):
        return onward(y, my_core, o, {"y": left}, left_send.at[o], left_recv.at[o], 0, cap)

    def far_right(y, o):
        return onward(y, my_core, o, {"y": right}, far_a_send.at[o], far_a_recv.at[o], 0, half)

    def far_left(y, o):
        return onward(y, my_core, o, {"y": left}, far_b_send.at[o], far_b_recv.at[o], half, half)

    def to_core(y, core, o):
        return onward(y, core, o, {"core": other}, core_send.at[y, o], core_recv.at[y, o], 0, cap)

    def travels(way, distance, part):
        return distance < reach or part == way

    def slot(distance, part):
        return (distance - 1) * 2 + part

    def sum_copy(way, distance, part):
        at = slot(distance, part)
        return pltpu.make_async_remote_copy(
            src_ref=sum_out.at[way, at], dst_ref=sum_in.at[way, at],
            send_sem=sum_send.at[way, at], recv_sem=sum_recv.at[way, at],
            device_id={"z": below if way else above}, device_id_type=MESH,
        )

    def partial(owner, part):
        return jnp.dot(
            rows_in[owner], weights[:, part * part_width : (part + 1) * part_width],
            preferred_element_type=jnp.float32,
        )

    def ready(owner):
        @pl.loop(0, y_count)
        def _(y):
            to_core(y, other, owner).wait_recv()

    def send_sums(distance):
        owners = [lax.rem(my_z + d, z_count) for d in (distance, z_count - distance)]
        for owner in owners[: 1 if distance == reach else 2]:
            ready(owner)
        for part in range(2):
            for way in range(2):
                if travels(way, distance, part):
                    total = partial(owners[way], part)
                    if distance < reach and travels(way, distance + 1, part):
                        sum_copy(way, distance + 1, part).wait_recv()
                        total = total + sum_in[way, slot(distance + 1, part)].astype(jnp.float32)
                    sum_out[way, slot(distance, part)] = total.astype(jnp.bfloat16)
                    sum_copy(way, distance, part).start()

    order = [reach]
    for distance in range(reach - 1, 0, -1):
        order += [distance, z_count - distance]
    order = [lax.rem(my_z + d, z_count) for d in order + [0]]

    own_copy.wait()
    for x in others:
        piece_arrival(x).wait_recv()
    for owner in order:
        packed = [landing[x, owner].astype(jnp.float32) for x in range(x_count)]
        for q in range(4):
            rows_in[owner, q * quarter : (q + 1) * quarter, columns(my_y, my_core)] = repack(
                packed, q
            ).astype(jnp.bfloat16)
        to_right(my_y, owner).start()
        to_left(my_y, owner).start()
        to_core(my_y, my_core, owner).start()

    def finish(owner):
        far_right(opposite, owner).wait_recv()
        far_left(opposite, owner).wait_recv()
        to_core(opposite, my_core, owner).start()

    load.wait()
    for k, owner in enumerate(order):
        to_right(left, owner).wait_recv()
        far_right(left, owner).start()
        to_core(left, my_core, owner).start()
        to_left(right, owner).wait_recv()
        far_left(right, owner).start()
        to_core(right, my_core, owner).start()
        if k >= 1:
            finish(order[k - 1])
        if k == 2:
            send_sums(reach)
        if k == 5 and reach > 1:
            send_sums(reach - 1)
    finish(order[-1])
    if len(order) <= 2:
        send_sums(reach)
    for distance in range(reach - 2 if reach > 1 else 0, 0, -1):
        send_sums(distance)

    ready(my_z)
    for part in range(2):
        total = partial(my_z, part)
        for way in range(2):
            if travels(way, 1, part):
                sum_copy(way, 1, part).wait_recv()
                total = total + sum_in[way, slot(1, part)].astype(jnp.float32)
        out[:, part * part_width : (part + 1) * part_width] = total.astype(jnp.bfloat16)

    for distance in range(1, reach + 1):
        for part in range(2):
            for way in range(2):
                if travels(way, distance, part):
                    sum_copy(way, distance, part).wait_send()
    for x in others:
        piece_copy(x).wait_send()

    @pl.loop(0, z_count)
    def _(o):
        for y in range(y_count):
            to_core(y, my_core, o).wait_send()
        to_right(my_y, o).wait_send()
        to_left(my_y, o).wait_send()
        far_right(left, o).wait_send()
        far_left(right, o).wait_send()


def project_call(dims, chosen, block):
    x_count, y_count, z_count = dims["x"], dims["y"], dims["z"]
    cap = chosen.shape[1] * 4
    depth, width = block.shape
    reach = z_count // 2
    bf16 = jnp.bfloat16
    dma = pltpu.SemaphoreType.DMA
    vmem = pl.BlockSpec(memory_space=pltpu.VMEM)
    return pl.pallas_call(
        functools.partial(project_kernel, x_count, z_count, y_count),
        out_shape=jax.ShapeDtypeStruct((cap, width), bf16),
        in_specs=[vmem, pl.BlockSpec(memory_space=pl.ANY)],
        out_specs=vmem,
        scratch_shapes=[
            pltpu.VMEM((x_count, z_count, cap // 4, LANES), bf16),
            pltpu.VMEM((z_count, cap, depth), bf16),
            pltpu.VMEM((depth, width), bf16),
            pltpu.VMEM((2, 2 * reach, cap, width // 2), bf16),
            pltpu.VMEM((2, 2 * reach, cap, width // 2), bf16),
            dma, dma, dma((x_count,)), dma((x_count,)),
        ]
        + [dma((z_count,))] * 8
        + [dma((y_count, z_count))] * 2
        + [dma((2, 2 * reach))] * 2,
        compiler_params=pltpu.CompilerParams(
            collective_id=1, has_side_effects=True, vmem_limit_bytes=48 << 20
        ),
        name="project_rows",
    )(chosen, block)


def shards(
    dims,
    input_triple_streams,
    former_piece_sizes,
    updated_piece_sizes,
    remaining_indices,
    short_causal_filters,
    pole_coefficients,
    pole_damping,
    direct_coefficient,
    final_projector,
):
    cap = input_triple_streams.shape[0]
    seq_len = cap * 4 // 5 * dims["x"] * dims["z"]

    block = lax.all_gather(final_projector, ("x_high", "x_low"), axis=0, tiled=True)
    pieces = conv_call(
        dims,
        jnp.transpose(input_triple_streams, (1, 0, 2)),
        former_piece_sizes,
        short_causal_filters,
        pole_coefficients,
        pole_damping,
        direct_coefficient[None, :],
    )
    chosen = select_call(
        seq_len, pieces, former_piece_sizes, updated_piece_sizes, remaining_indices
    )
    return project_call(dims, chosen, block)


def solution(mesh):
    grid = (2, 2, mesh.shape["seq"] // 4, mesh.shape["chan"] // 2, 2)
    dims = {"x": 4, "z": grid[2], "y": grid[3]}
    rows, channels = SEQ, ("y", "core")
    return jax.shard_map(
        functools.partial(shards, dims),
        mesh=Mesh(mesh.devices.reshape(grid), AXES),
        in_specs=(
            P(rows, None, channels),
            P(),
            P(),
            P(),
            P(None, None, channels),
            P(None, channels),
            P(None, channels),
            P(channels),
            P(rows, channels),
        ),
        out_specs=P(rows, channels),
        check_vma=False,
    )
```

time: 193 us -> 166 us (0.86)
  Pallas kernels: 167 us -> 146 us
  local copies, waits for them, and re-layouts: 8.38 us -> 3.51 us
    pallas_call x1, Pallas kernels: 72 us -> 52.3 us  [conv_call(): pl.pallas_call(functools.partial(conv_kernel, x_count, z_count), out_shap...]
    pallas_call x1, Pallas kernels: 93.8 us -> 88 us  [project_call(): pl.pallas_call(functools.partial(project_kernel, x_count, z_count, y_coun...]
    unnamed x19 -> x11, local copies, waits for them, and re-layouts: 8.38 us -> 3.51 us
    pallas_call x1, Pallas kernels: 1.6 us -> 5.94 us  [select_call(): pl.pallas_call(select_kernel, out_shape=jax.ShapeDtypeStruct(pieces.shape...]
  transfers between devices with their start and end apart: 1 -> 1, of which waited for: 0 -> 0; matrix products, arithmetic and copies ran while one was open for 0% -> 0% of each run, Pallas kernels for 39% -> 36%
where the time goes in v7:
time: 166 us; the launch traced here: 164 us
  Pallas kernels  146 us (88%)
  between operations  13.5 us (8%)
  local copies, waits for them, and re-layouts  3.51 us (2%)
    pallas_call x1, Pallas kernels, project_call(): pl.pallas_call(functools.partial(project_kernel, x_count, z_count, y_coun...  88 us
    pallas_call x1, Pallas kernels, conv_call(): pl.pallas_call(functools.partial(conv_kernel, x_count, z_count), out_shap...  52.3 us
    pallas_call x1, Pallas kernels, select_call(): pl.pallas_call(select_kernel, out_shape=jax.ShapeDtypeStruct(pieces.shape...  5.94 us
    unnamed x11, local copies, waits for them, and re-layouts  3.51 us
  transfers between devices with their start and end apart: 1, of which 0 were waited for; matrix products, arithmetic and copies ran while one was open for 0% of the time, Pallas kernels for 36%

profile of v7, /device:TPU:32, one launch (start us, length us, event | category | flops | bytes accessed | tf_op | source)
XLA Modules:
  0.0 163.9 jit_solution(16734821164905243103)
XLA Ops:
  6.5 0.0 copy-start.2
  6.5 0.0 copy-start.4
  6.5 0.0 copy-start.3
  6.5 0.0 all-gather.2.cloned.1.call-start
  6.5 0.7 all-gather.2.cloned.1.call-update
  7.3 52.3 %convolve.1.pieces = bf16[32,80,128]{2,1,0:T(8,128)(2,1)} custom-call(s32[32]{0:T(128)} %former.1, bf16[3,320,1024]{2,1,0:T(8,128)(2,1)} %bitcast.2, f32[3,3,1024]{2,1,0:T(4,128)} %taps_far.1, f32[16,1024]{1,0:T(8,128)} %residue_far.1, f32[16,1024]{1,0:T(8,128)} %damping_far.1, f32[1,1024]{1,0:T(1,128)} %bitcast.3), custom_call_target="tpu_custom_call" | custom-call | tf_op jit(solution)/shard_map/convolve/pallas_call | solution.py:360
  59.5 0.0 copy-done.2
  59.5 0.0 copy-done.4
  59.5 0.0 copy-done.3
  59.6 0.0 copy-start
  59.6 1.1 copy-done
  60.6 5.9 %reorder_rows.1.chosen = bf16[32,80,128]{2,1,0:T(8,128)(2,1)S(1)} custom-call(s32[32]{0:T(128)S(1)} %copy-done.2, s32[28]{0:T(128)S(1)} %copy-done.3, s32[28]{0:T(128)S(1)} %copy-done.4, bf16[32,80,128]{2,1,0:T(8,128)(2,1)S(1)} %copy-done), custom_call_target="tpu_custom_call" | custom-call | tf_op jit(solution)/shard_map/reorder_rows/pallas_call | solution.py:424
  66.6 0.0 all-gather.2.cloned.1.call-done.block
  66.6 0.0 copy-start.1
  66.6 1.6 copy-done.1
  68.2 88.0 %project_rows.1 = bf16[320,1024]{1,0:T(8,128)(2,1)S(1)} custom-call(bf16[32,80,128]{2,1,0:T(8,128)(2,1)S(1)} %reorder_rows.1.chosen, bf16[1024,1024]{1,0:T(8,128)(2,1)S(1)} %copy-done.1), custom_call_target="tpu_custom_call" | custom-call | tf_op jit(solution)/shard_map/project_rows/pallas_call | solution.py:631
  156.2 0.8 copy.11
Async XLA Ops:
  6.5 53.0 %copy-start.2 = (s32[32]{0:T(128)S(1)}, s32[32]{0:T(128)}, u32[]{:S(2)}) copy-start(s32[32]{0:T(128)} %former.1) | copy-start | bytes 388
  6.5 53.0 %copy-start.4 = (s32[28]{0:T(128)S(1)}, s32[28]{0:T(128)}, u32[]{:S(2)}) copy-start(s32[28]{0:T(128)} %remaining.1) | copy-start | bytes 340
  6.5 53.0 %copy-start.3 = (s32[28]{0:T(128)S(1)}, s32[28]{0:T(128)}, u32[]{:S(2)}) copy-start(s32[28]{0:T(128)} %updated.1) | copy-start | bytes 340
  6.5 60.1 %all-gather.2.cloned.1.call-start = ((), (), s32[]{:S(2)}) async-start(), calls=%async_computation | async-start | bytes 2621440 | tf_op jit(solution)/shard_map/all_gather | solution.py:669
  59.6 1.1 copy-start
  66.6 1.6 copy-start.1
Sparse Core Ops, SparseCore 0:
  9.2 41.1 all-gather.1

commit v8 on v7

--- a/solution.py
+++ b/solution.py
@@ -10,7 +10,6 @@
 
 MESH = pl.DeviceIdType.MESH
 LANES = 128
-VMEM = 56 << 20
 SUBS = 8
 AXES = ("x_high", "x_low", "z", "y", "core")
 SEQ = ("x_high", "x_low", "z")
@@ -129,24 +128,23 @@
     row = lax.broadcasted_iota(jnp.int32, (cap, LANES), 0)
     before_size = sizes[lax.rem(me + seq_count - 1, seq_count)]
 
+    def feature(p, g):
+        at = lanes(g)
+        last_one = jnp.where(me >= 1, halo[0, g, p : p + 1, :], 0.0)
+        own_second = halo[0, g, 3 + p : 4 + p, :]
+        far_last = jnp.where(me >= 2, halo[1, g, p : p + 1, :], 0.0)
+        last_two = jnp.where(me >= 1, jnp.where(before_size >= 2, own_second, far_last), 0.0)
+        padded[p, g, 6:7, :] = last_two
+        padded[p, g, 7:8, :] = last_one
+        return (
+            taps[p, 0:1, at] * padded[p, g, 8 : 8 + cap, :]
+            + taps[p, 1:2, at] * padded[p, g, 7 : 7 + cap, :]
+            + taps[p, 2:3, at] * padded[p, g, 6 : 6 + cap, :]
+        )
+
     @pl.loop(0, groups)
     def _(g):
-        at = lanes(g)
-        features = []
-        for p in range(3):
-            last_one = jnp.where(me >= 1, halo[0, g, p : p + 1, :], 0.0)
-            own_second = halo[0, g, 3 + p : 4 + p, :]
-            far_last = jnp.where(me >= 2, halo[1, g, p : p + 1, :], 0.0)
-            last_two = jnp.where(me >= 1, jnp.where(before_size >= 2, own_second, far_last), 0.0)
-            padded[p, g, 6:7, :] = last_two
-            padded[p, g, 7:8, :] = last_one
-            features.append(
-                taps[p, 0:1, at] * padded[p, g, 8 : 8 + cap, :]
-                + taps[p, 1:2, at] * padded[p, g, 7 : 7 + cap, :]
-                + taps[p, 2:3, at] * padded[p, g, 6 : 6 + cap, :]
-            )
-        query[g] = features[0].astype(jnp.bfloat16).astype(jnp.float32)
-        product = (features[1] * features[2]).astype(jnp.bfloat16).astype(jnp.float32)
+        product = (feature(1, g) * feature(2, g)).astype(jnp.bfloat16).astype(jnp.float32)
         gated[g] = jnp.where(row < valid, product, 0.0)
 
     def mode_rows(ref, at):
@@ -240,6 +238,10 @@
             @pl.when(target != me)
             def _():
                 carry_copy(target).start()
+
+    @pl.loop(0, groups)
+    def _(g):
+        query[g] = feature(0, g).astype(jnp.bfloat16).astype(jnp.float32)
 
     @pl.loop(0, owners)
     def _(owner):
@@ -356,12 +358,12 @@
     f32, bf16 = jnp.float32, jnp.bfloat16
     dma = pltpu.SemaphoreType.DMA
     vmem = pl.BlockSpec(memory_space=pltpu.VMEM)
-    far = pl.BlockSpec(memory_space=pl.ANY)
+    far = pl.BlockSpec(memory_space=pltpu.HBM)
     return pl.pallas_call(
         functools.partial(conv_kernel, x_count, z_count),
         out_shape=jax.ShapeDtypeStruct((seq_count, cap // 4, LANES), bf16),
         in_specs=[pl.BlockSpec(memory_space=pltpu.SMEM)] + [far] * 5,
-        out_specs=far,
+        out_specs=pl.BlockSpec(memory_space=pl.ANY),
         scratch_shapes=[
             pltpu.VMEM(streams.shape, bf16),
             pltpu.VMEM(taps.shape, f32),
@@ -386,7 +388,7 @@
         ]
         + [dma((x_count, z_count)), dma((seq_count,)), dma((5,)), dma],
         compiler_params=pltpu.CompilerParams(
-            collective_id=0, has_side_effects=True, vmem_limit_bytes=VMEM
+            collective_id=0, has_side_effects=True, vmem_limit_bytes=56 << 20
         ),
         name="convolve",
     )(sizes, streams, taps, residue, damping, direct)
@@ -468,23 +470,28 @@
         pl.semaphore_signal(barrier, inc=1, device_id=to, device_id_type=MESH)
     pl.semaphore_wait(barrier, x_count - 1 + 5)
 
-    def piece_copy(x):
-        return pltpu.make_async_remote_copy(
-            src_ref=chosen.at[pl.ds(x * z_count, z_count)], dst_ref=landing.at[my_x],
-            send_sem=piece_send.at[x], recv_sem=piece_recv.at[my_x],
+    def piece_copy(x, owner):
+        return pltpu.make_async_remote_copy(
+            src_ref=chosen.at[x * z_count + owner], dst_ref=landing.at[my_x, owner],
+            send_sem=piece_send.at[x, owner], recv_sem=piece_recv.at[my_x, owner],
             device_id=at_x(x), device_id_type=MESH,
         )
 
-    def piece_arrival(x):
-        return pltpu.make_async_remote_copy(
-            src_ref=chosen.at[pl.ds(0, z_count)], dst_ref=landing.at[x],
-            send_sem=piece_send.at[x], recv_sem=piece_recv.at[x],
+    def piece_arrival(x, owner):
+        return pltpu.make_async_remote_copy(
+            src_ref=chosen.at[owner], dst_ref=landing.at[x, owner],
+            send_sem=piece_send.at[x, owner], recv_sem=piece_recv.at[x, owner],
             device_id=at_x(x), device_id_type=MESH,
         )
 
+    order = [reach]
+    for distance in range(reach - 1, 0, -1):
+        order += [distance, z_count - distance]
+    order = [lax.rem(my_z + d, z_count) for d in order + [0]]
     others = [lax.rem(my_x + k, x_count) for k in (1, 3, 2)]
-    for x in others:
-        piece_copy(x).start()
+    for owner in order:
+        for x in others:
+            piece_copy(x, owner).start()
 
     def columns(y, core):
         return pl.ds(pl.multiple_of((y * 2 + core) * LANES, LANES), LANES)
@@ -540,25 +547,20 @@
         owners = [lax.rem(my_z + d, z_count) for d in (distance, z_count - distance)]
         for owner in owners[: 1 if distance == reach else 2]:
             ready(owner)
-        for part in range(2):
-            for way in range(2):
-                if travels(way, distance, part):
-                    total = partial(owners[way], part)
-                    if distance < reach and travels(way, distance + 1, part):
-                        sum_copy(way, distance + 1, part).wait_recv()
-                        total = total + sum_in[way, slot(distance + 1, part)].astype(jnp.float32)
-                    sum_out[way, slot(distance, part)] = total.astype(jnp.bfloat16)
-                    sum_copy(way, distance, part).start()
-
-    order = [reach]
-    for distance in range(reach - 1, 0, -1):
-        order += [distance, z_count - distance]
-    order = [lax.rem(my_z + d, z_count) for d in order + [0]]
+        for way, part in ((0, 1), (1, 0), (0, 0), (1, 1)):
+            if travels(way, distance, part):
+                total = partial(owners[way], part)
+                if distance < reach and travels(way, distance + 1, part):
+                    sum_copy(way, distance + 1, part).wait_recv()
+                    total = total + sum_in[way, slot(distance + 1, part)].astype(jnp.float32)
+                sum_out[way, slot(distance, part)] = total.astype(jnp.bfloat16)
+                sum_copy(way, distance, part).start()
 
     own_copy.wait()
-    for x in others:
-        piece_arrival(x).wait_recv()
-    for owner in order:
+
+    def launch(owner):
+        for x in others:
+            piece_arrival(x, owner).wait_recv()
         packed = [landing[x, owner].astype(jnp.float32) for x in range(x_count)]
         for q in range(4):
             rows_in[owner, q * quarter : (q + 1) * quarter, columns(my_y, my_core)] = repack(
@@ -573,24 +575,28 @@
         far_left(opposite, owner).wait_recv()
         to_core(opposite, my_core, owner).start()
 
+    ahead, lag = 3, 2
+    for owner in order[:ahead]:
+        launch(owner)
     load.wait()
-    for k, owner in enumerate(order):
-        to_right(left, owner).wait_recv()
-        far_right(left, owner).start()
-        to_core(left, my_core, owner).start()
-        to_left(right, owner).wait_recv()
-        far_left(right, owner).start()
-        to_core(right, my_core, owner).start()
-        if k >= 1:
-            finish(order[k - 1])
-        if k == 2:
-            send_sums(reach)
-        if k == 5 and reach > 1:
-            send_sums(reach - 1)
-    finish(order[-1])
-    if len(order) <= 2:
-        send_sums(reach)
-    for distance in range(reach - 2 if reach > 1 else 0, 0, -1):
+    sent = reach + 1
+    for k in range(len(order) + lag):
+        if k + ahead < len(order):
+            launch(order[k + ahead])
+        if k < len(order):
+            owner = order[k]
+            to_right(left, owner).wait_recv()
+            far_right(left, owner).start()
+            to_core(left, my_core, owner).start()
+            to_left(right, owner).wait_recv()
+            far_left(right, owner).start()
+            to_core(right, my_core, owner).start()
+        if k >= lag:
+            finish(order[k - lag])
+        if k == lag or k == lag + 2 and reach > 1:
+            sent -= 1
+            send_sums(sent)
+    for distance in range(sent - 1, 0, -1):
         send_sums(distance)
 
     ready(my_z)
@@ -607,8 +613,9 @@
             for way in range(2):
                 if travels(way, distance, part):
                     sum_copy(way, distance, part).wait_send()
-    for x in others:
-        piece_copy(x).wait_send()
+    for owner in order:
+        for x in others:
+            piece_copy(x, owner).wait_send()
 
     @pl.loop(0, z_count)
     def _(o):
@@ -631,7 +638,7 @@
     return pl.pallas_call(
         functools.partial(project_kernel, x_count, z_count, y_count),
         out_shape=jax.ShapeDtypeStruct((cap, width), bf16),
-        in_specs=[vmem, pl.BlockSpec(memory_space=pl.ANY)],
+        in_specs=[vmem, pl.BlockSpec(memory_space=pltpu.HBM)],
         out_specs=vmem,
         scratch_shapes=[
             pltpu.VMEM((x_count, z_count, cap // 4, LANES), bf16),
@@ -639,13 +646,13 @@
             pltpu.VMEM((depth, width), bf16),
             pltpu.VMEM((2, 2 * reach, cap, width // 2), bf16),
             pltpu.VMEM((2, 2 * reach, cap, width // 2), bf16),
-            dma, dma, dma((x_count,)), dma((x_count,)),
+            dma, dma, dma((x_count, z_count)), dma((x_count, z_count)),
         ]
         + [dma((z_count,))] * 8
         + [dma((y_count, z_count))] * 2
         + [dma((2, 2 * reach))] * 2,
         compiler_params=pltpu.CompilerParams(
-            collective_id=1, has_side_effects=True, vmem_limit_bytes=48 << 20
+            collective_id=1, has_side_effects=True, vmem_limit_bytes=60 << 20
         ),
         name="project_rows",
     )(chosen, block)

time: 166 us -> 154 us (0.928)
  Pallas kernels: 146 us -> 135 us
    pallas_call x1, Pallas kernels: 88 us -> 76.9 us  [project_call(): pl.pallas_call(functools.partial(project_kernel, x_count, z_count, y_coun...]
  transfers between devices with their start and end apart: 1 -> 1, of which waited for: 0 -> 0; matrix products, arithmetic and copies ran while one was open for 0% -> 0% of each run, Pallas kernels for 36% -> 38%
where the time goes in v8:
time: 154 us; the launch traced here: 153 us
  Pallas kernels  135 us (88%)
  between operations  13.4 us (9%)
  local copies, waits for them, and re-layouts  3.89 us (3%)
    pallas_call x1, Pallas kernels, project_call(): pl.pallas_call(functools.partial(project_kernel, x_count, z_count, y_coun...  76.9 us
    pallas_call x1, Pallas kernels, conv_call(): pl.pallas_call(functools.partial(conv_kernel, x_count, z_count), out_shap...  51.8 us
    pallas_call x1, Pallas kernels, select_call(): pl.pallas_call(select_kernel, out_shape=jax.ShapeDtypeStruct(pieces.shape...  5.94 us
    unnamed x11, local copies, waits for them, and re-layouts  3.89 us
  transfers between devices with their start and end apart: 1, of which 0 were waited for; matrix products, arithmetic and copies ran while one was open for 0% of the time, Pallas kernels for 38%

profile of v8, /device:TPU:32, one launch (start us, length us, event | category | flops | bytes accessed | tf_op | source)
XLA Modules:
  0.0 152.7 jit_solution(9854598368191095389)
XLA Ops:
  6.5 0.0 copy-start.2
  6.5 0.0 copy-start.4
  6.5 0.0 copy-start.3
  6.5 0.0 all-gather.2.cloned.1.call-start
  6.5 0.7 all-gather.2.cloned.1.call-update
  7.3 51.8 %convolve.1.pieces = bf16[32,80,128]{2,1,0:T(8,128)(2,1)} custom-call(s32[32]{0:T(128)} %former.1, bf16[3,320,1024]{2,1,0:T(8,128)(2,1)} %bitcast.2, f32[3,3,1024]{2,1,0:T(4,128)} %taps_far.1, f32[16,1024]{1,0:T(8,128)} %residue_far.1, f32[16,1024]{1,0:T(8,128)} %damping_far.1, f32[1,1024]{1,0:T(1,128)} %bitcast.3), custom_call_target="tpu_custom_call" | custom-call | tf_op jit(solution)/shard_map/convolve/pallas_call | solution.py:362
  59.1 0.0 copy-done.2
  59.1 0.0 copy-done.4
  59.1 0.0 copy-done.3
  59.1 0.0 copy-start.1
  59.1 1.1 copy-done.1
  60.2 5.9 %reorder_rows.1.chosen = bf16[32,80,128]{2,1,0:T(8,128)(2,1)S(1)} custom-call(s32[32]{0:T(128)S(1)} %copy-done.2, s32[28]{0:T(128)S(1)} %copy-done.3, s32[28]{0:T(128)S(1)} %copy-done.4, bf16[32,80,128]{2,1,0:T(8,128)(2,1)S(1)} %copy-done.1), custom_call_target="tpu_custom_call" | custom-call | tf_op jit(solution)/shard_map/reorder_rows/pallas_call | solution.py:426
  66.1 0.0 copy-start
  66.2 0.8 copy-done
  67.0 0.0 all-gather.2.cloned.1.call-done.block
  67.0 76.9 %project_rows.1 = bf16[320,1024]{1,0:T(8,128)(2,1)} custom-call(bf16[32,80,128]{2,1,0:T(8,128)(2,1)} %copy-done, bf16[1024,1024]{1,0:T(8,128)(2,1)} %all-gather.2.cloned.1.call-done.block), custom_call_target="tpu_custom_call" | custom-call | tf_op jit(solution)/shard_map/project_rows/pallas_call | solution.py:638
  143.9 2.0 %copy.11 = bf16[320,1024]{1,0:T(8,128)(2,1)} copy(bf16[320,1024]{1,0:T(8,128)(2,1)} %project_rows.1) | data formatting | bytes 1310720
Async XLA Ops:
  6.5 52.6 %copy-start.2 = (s32[32]{0:T(128)S(1)}, s32[32]{0:T(128)}, u32[]{:S(2)}) copy-start(s32[32]{0:T(128)} %former.1) | copy-start | bytes 388
  6.5 52.6 %copy-start.4 = (s32[28]{0:T(128)S(1)}, s32[28]{0:T(128)}, u32[]{:S(2)}) copy-start(s32[28]{0:T(128)} %remaining.1) | copy-start | bytes 340
  6.5 52.6 %copy-start.3 = (s32[28]{0:T(128)S(1)}, s32[28]{0:T(128)}, u32[]{:S(2)}) copy-start(s32[28]{0:T(128)} %updated.1) | copy-start | bytes 340
  6.5 60.4 %all-gather.2.cloned.1.call-start = ((), (), s32[]{:S(2)}) async-start(), calls=%async_computation | async-start | bytes 2621440 | tf_op jit(solution)/shard_map/all_gather | solution.py:676
  59.1 1.1 copy-start.1
  66.1 0.8 copy-start
Sparse Core Ops, SparseCore 0:
  9.2 41.9 all-gather.1

commit v9 on v8

--- a/solution.py
+++ b/solution.py
@@ -299,8 +299,8 @@
 
         lax.fori_loop(0, step_rows, step, start, unroll=4)
         conv = mixed[...] + direct[0:1, at] * gated[g]
-        value = query[g] * conv
-        quarters = [value[q * quarter : (q + 1) * quarter] for q in range(4)]
+        mixed[...] = query[g] * conv
+        quarters = [mixed[pl.ds(q, quarter, stride=4), :] for q in range(4)]
         for x in range(x_count):
             hidden[g, x] = repack(quarters, x).astype(jnp.bfloat16)
 
@@ -395,26 +395,31 @@
 
 
 def select_kernel(former, updated, remaining, pieces, chosen, sequence):
-    seq_count, quarter, _ = pieces.shape
-    lane_group = LANES // 4
+    seq_count, packed_rows, _ = pieces.shape
+    width = LANES // 4
+    lane = lax.broadcasted_iota(jnp.int32, (packed_rows, LANES), 1)
+    line = lax.broadcasted_iota(jnp.int32, (packed_rows, LANES), 0)
 
     def place(s, start):
-        piece = pieces[s].astype(jnp.float32)
-        for q in range(4):
-            turned = pltpu.roll(piece, (4 - q) % 4 * lane_group, 1)
-            sequence[pl.ds(start + q * quarter, quarter), :] = turned
+        at, offset = start // 4, lax.rem(start, 4) * width
+        turned = pltpu.roll(pieces[s].astype(jnp.float32), offset, 1)
+        present = jnp.broadcast_to(sequence[pl.ds(at, 1), :], turned.shape)
+        before = jnp.where(line == 0, present, pltpu.roll(turned, 1, 0))
+        sequence[pl.ds(at, packed_rows), :] = jnp.where(lane < offset, before, turned)
+        sequence[pl.ds(at + packed_rows, 1), :] = turned[packed_rows - 1 :, :]
         return start + former[s]
 
     lax.fori_loop(0, seq_count, place, 0)
-    row = lax.broadcasted_iota(jnp.int32, (quarter, LANES), 0)
+    row = line * 4 + lane // width
     chosen[...] = jnp.zeros_like(chosen)
 
     def pick(k, start):
-        quarters = []
-        for q in range(4):
-            rows = sequence[pl.ds(start + q * quarter, quarter), :]
-            quarters.append(jnp.where(row + q * quarter < updated[k], rows, 0.0))
-        chosen[remaining[k]] = repack(quarters, 0).astype(jnp.bfloat16)
+        at, offset = start // 4, lax.rem(start, 4) * width
+        here = sequence[pl.ds(at, packed_rows), :]
+        after = sequence[pl.ds(at + 1, packed_rows), :]
+        both = jnp.where(lane < offset, after, here)
+        rows = pltpu.roll(both, lax.rem(LANES - offset, LANES), 1)
+        chosen[remaining[k]] = jnp.where(row < updated[k], rows, 0.0).astype(jnp.bfloat16)
         return start + updated[k]
 
     lax.fori_loop(0, updated.shape[0], pick, 0)
@@ -428,7 +433,7 @@
         out_shape=jax.ShapeDtypeStruct(pieces.shape, jnp.bfloat16),
         in_specs=[smem] * 3 + [vmem],
         out_specs=vmem,
-        scratch_shapes=[pltpu.VMEM((seq_len + 4 * pieces.shape[1], LANES), jnp.float32)],
+        scratch_shapes=[pltpu.VMEM((seq_len // 4 + pieces.shape[1] + 8, LANES), jnp.float32)],
         compiler_params=pltpu.CompilerParams(vmem_limit_bytes=24 << 20),
         name="reorder_rows",
     )(former, updated, remaining, pieces)
@@ -437,7 +442,7 @@
 def project_kernel(
     x_count, z_count, y_count,
     chosen, block, out,
-    landing, rows_in, weights, sum_out, sum_in,
+    landing, unpacked, rows_in, weights, sum_out, sum_in,
     load_sem, own_sem, piece_send, piece_recv,
     right_send, right_recv, left_send, left_recv,
     far_a_send, far_a_recv, far_b_send, far_b_recv, core_send, core_recv,
@@ -563,9 +568,8 @@
             piece_arrival(x, owner).wait_recv()
         packed = [landing[x, owner].astype(jnp.float32) for x in range(x_count)]
         for q in range(4):
-            rows_in[owner, q * quarter : (q + 1) * quarter, columns(my_y, my_core)] = repack(
-                packed, q
-            ).astype(jnp.bfloat16)
+            unpacked[pl.ds(q, quarter, stride=4), :] = repack(packed, q)
+        rows_in[owner, :, columns(my_y, my_core)] = unpacked[...].astype(jnp.bfloat16)
         to_right(my_y, owner).start()
         to_left(my_y, owner).start()
         to_core(my_y, my_core, owner).start()
@@ -575,7 +579,7 @@
         far_left(opposite, owner).wait_recv()
         to_core(opposite, my_core, owner).start()
 
-    ahead, lag = 3, 2
+    ahead, lag = 2, 1
     for owner in order[:ahead]:
         launch(owner)
     load.wait()
@@ -642,6 +646,7 @@
         out_specs=vmem,
         scratch_shapes=[
             pltpu.VMEM((x_count, z_count, cap // 4, LANES), bf16),
+            pltpu.VMEM((cap, LANES), jnp.float32),
             pltpu.VMEM((z_count, cap, depth), bf16),
             pltpu.VMEM((depth, width), bf16),
             pltpu.VMEM((2, 2 * reach, cap, width // 2), bf16),
@@ -652,7 +657,7 @@
         + [dma((y_count, z_count))] * 2
         + [dma((2, 2 * reach))] * 2,
         compiler_params=pltpu.CompilerParams(
-            collective_id=1, has_side_effects=True, vmem_limit_bytes=60 << 20
+            collective_id=1, has_side_effects=True, vmem_limit_bytes=53 << 20
         ),
         name="project_rows",
     )(chosen, block)

time: 154 us -> 149 us (0.968)
  Pallas kernels: 135 us -> 131 us
    pallas_call x1, Pallas kernels: 76.9 us -> 74 us  [project_call(): pl.pallas_call(functools.partial(project_kernel, x_count, z_count, y_coun...]
  transfers between devices with their start and end apart: 1 -> 1, of which waited for: 0 -> 0; matrix products, arithmetic and copies ran while one was open for 0% -> 0% of each run, Pallas kernels for 38% -> 39%
where the time goes in v9:
time: 149 us; the launch traced here: 148 us
  Pallas kernels  131 us (88%)
  between operations  13.4 us (9%)
  local copies, waits for them, and re-layouts  2.76 us (2%)
    pallas_call x1, Pallas kernels, project_call(): pl.pallas_call(functools.partial(project_kernel, x_count, z_count, y_coun...  74 us
    pallas_call x1, Pallas kernels, conv_call(): pl.pallas_call(functools.partial(conv_kernel, x_count, z_count), out_shap...  51.9 us
    pallas_call x1, Pallas kernels, select_call(): pl.pallas_call(select_kernel, out_shape=jax.ShapeDtypeStruct(pieces.shape...  5.33 us
  transfers between devices with their start and end apart: 1, of which 0 were waited for; matrix products, arithmetic and copies ran while one was open for 0% of the time, Pallas kernels for 39%

profile of v9, /device:TPU:32, one launch (start us, length us, event | category | flops | bytes accessed | tf_op | source)
XLA Modules:
  0.0 148.2 jit_solution(2676156050943696197)
XLA Ops:
  6.5 0.0 copy-start.2
  6.5 0.0 copy-start.4
  6.5 0.0 copy-start.3
  6.5 0.0 all-gather.2.cloned.1.call-start
  6.5 0.7 all-gather.2.cloned.1.call-update
  7.3 51.9 %convolve.1.pieces = bf16[32,80,128]{2,1,0:T(8,128)(2,1)} custom-call(s32[32]{0:T(128)} %former.1, bf16[3,320,1024]{2,1,0:T(8,128)(2,1)} %bitcast.2, f32[3,3,1024]{2,1,0:T(4,128)} %taps_far.1, f32[16,1024]{1,0:T(8,128)} %residue_far.1, f32[16,1024]{1,0:T(8,128)} %damping_far.1, f32[1,1024]{1,0:T(1,128)} %bitcast.3), custom_call_target="tpu_custom_call" | custom-call | tf_op jit(solution)/shard_map/convolve/pallas_call | solution.py:362
  59.2 0.0 copy-done.2
  59.2 0.0 copy-done.4
  59.2 0.0 copy-done.3
  59.2 0.0 copy-start.1
  59.2 1.1 copy-done.1
  60.3 5.3 %reorder_rows.1.chosen = bf16[32,80,128]{2,1,0:T(8,128)(2,1)S(1)} custom-call(s32[32]{0:T(128)S(1)} %copy-done.2, s32[28]{0:T(128)S(1)} %copy-done.3, s32[28]{0:T(128)S(1)} %copy-done.4, bf16[32,80,128]{2,1,0:T(8,128)(2,1)S(1)} %copy-done.1), custom_call_target="tpu_custom_call" | custom-call | tf_op jit(solution)/shard_map/reorder_rows/pallas_call | solution.py:431
  65.6 0.0 copy-start
  65.6 0.8 copy-done
  66.5 0.0 all-gather.2.cloned.1.call-done.block
  66.5 74.0 %project_rows.1 = bf16[320,1024]{1,0:T(8,128)(2,1)S(1)} custom-call(bf16[32,80,128]{2,1,0:T(8,128)(2,1)} %copy-done, bf16[1024,1024]{1,0:T(8,128)(2,1)} %all-gather.2.cloned.1.call-done.block), custom_call_target="tpu_custom_call" | custom-call | tf_op jit(solution)/shard_map/project_rows/pallas_call | solution.py:642
  140.5 0.8 copy.11
Async XLA Ops:
  6.5 52.6 %copy-start.2 = (s32[32]{0:T(128)S(1)}, s32[32]{0:T(128)}, u32[]{:S(2)}) copy-start(s32[32]{0:T(128)} %former.1) | copy-start | bytes 388
  6.5 52.7 %copy-start.4 = (s32[28]{0:T(128)S(1)}, s32[28]{0:T(128)}, u32[]{:S(2)}) copy-start(s32[28]{0:T(128)} %remaining.1) | copy-start | bytes 340
  6.5 52.7 %copy-start.3 = (s32[28]{0:T(128)S(1)}, s32[28]{0:T(128)}, u32[]{:S(2)}) copy-start(s32[28]{0:T(128)} %updated.1) | copy-start | bytes 340
  6.5 59.9 %all-gather.2.cloned.1.call-start = ((), (), s32[]{:S(2)}) async-start(), calls=%async_computation | async-start | bytes 2621440 | tf_op jit(solution)/shard_map/all_gather | solution.py:681
  59.2 1.1 copy-start.1
  65.6 0.8 copy-start
Sparse Core Ops, SparseCore 0:
  9.2 42.0 all-gather.1

commit v10 on v9

--- a/solution.py
+++ b/solution.py
@@ -409,7 +409,7 @@
         sequence[pl.ds(at + packed_rows, 1), :] = turned[packed_rows - 1 :, :]
         return start + former[s]
 
-    lax.fori_loop(0, seq_count, place, 0)
+    lax.fori_loop(0, seq_count, place, 0, unroll=8)
     row = line * 4 + lane // width
     chosen[...] = jnp.zeros_like(chosen)
 
@@ -422,7 +422,7 @@
         chosen[remaining[k]] = jnp.where(row < updated[k], rows, 0.0).astype(jnp.bfloat16)
         return start + updated[k]
 
-    lax.fori_loop(0, updated.shape[0], pick, 0)
+    lax.fori_loop(0, updated.shape[0], pick, 0, unroll=7)
 
 
 def select_call(seq_len, pieces, former, updated, remaining):
@@ -597,7 +597,7 @@
             to_core(right, my_core, owner).start()
         if k >= lag:
             finish(order[k - lag])
-        if k == lag or k == lag + 2 and reach > 1:
+        if k == lag or k in (lag + 2, lag + 4) and reach > 1:
             sent -= 1
             send_sums(sent)
     for distance in range(sent - 1, 0, -1):

time: 149 us -> 145 us (0.973)
  Pallas kernels: 131 us -> 128 us
    pallas_call x1, Pallas kernels: 5.33 us -> 1.61 us  [select_call(): pl.pallas_call(select_kernel, out_shape=jax.ShapeDtypeStruct(pieces.shape...]
  transfers between devices with their start and end apart: 1 -> 1, of which waited for: 0 -> 0; matrix products, arithmetic and copies ran while one was open for 0% -> 0% of each run, Pallas kernels for 39% -> 37%
where the time goes in v10:
time: 145 us; the launch traced here: 144 us
  Pallas kernels  128 us (88%)
  between operations  13.4 us (9%)
  local copies, waits for them, and re-layouts  2.76 us (2%)
    pallas_call x1, Pallas kernels, project_call(): pl.pallas_call(functools.partial(project_kernel, x_count, z_count, y_coun...  74 us
    pallas_call x1, Pallas kernels, conv_call(): pl.pallas_call(functools.partial(conv_kernel, x_count, z_count), out_shap...  51.9 us
  transfers between devices with their start and end apart: 1, of which 0 were waited for; matrix products, arithmetic and copies ran while one was open for 0% of the time, Pallas kernels for 37%

profile of v10, /device:TPU:32, one launch (start us, length us, event | category | flops | bytes accessed | tf_op | source)
XLA Modules:
  0.0 144.4 jit_solution(299066460837576012)
XLA Ops:
  6.5 0.0 copy-start.2
  6.5 0.0 copy-start.4
  6.5 0.0 copy-start.3
  6.5 0.0 all-gather.2.cloned.1.call-start
  6.5 0.7 all-gather.2.cloned.1.call-update
  7.3 51.9 %convolve.1.pieces = bf16[32,80,128]{2,1,0:T(8,128)(2,1)} custom-call(s32[32]{0:T(128)} %former.1, bf16[3,320,1024]{2,1,0:T(8,128)(2,1)} %bitcast.2, f32[3,3,1024]{2,1,0:T(4,128)} %taps_far.1, f32[16,1024]{1,0:T(8,128)} %residue_far.1, f32[16,1024]{1,0:T(8,128)} %damping_far.1, f32[1,1024]{1,0:T(1,128)} %bitcast.3), custom_call_target="tpu_custom_call" | custom-call | tf_op jit(solution)/shard_map/convolve/pallas_call | solution.py:362
  59.2 0.0 copy-done.2
  59.2 0.0 copy-done.4
  59.2 0.0 copy-done.3
  59.2 0.0 copy-start.1
  59.2 1.1 copy-done.1
  60.3 1.6 %reorder_rows.1.chosen = bf16[32,80,128]{2,1,0:T(8,128)(2,1)S(1)} custom-call(s32[32]{0:T(128)S(1)} %copy-done.2, s32[28]{0:T(128)S(1)} %copy-done.3, s32[28]{0:T(128)S(1)} %copy-done.4, bf16[32,80,128]{2,1,0:T(8,128)(2,1)S(1)} %copy-done.1), custom_call_target="tpu_custom_call" | custom-call | tf_op jit(solution)/shard_map/reorder_rows/pallas_call | solution.py:431
  61.9 0.0 copy-start
  61.9 0.8 copy-done
  62.8 0.0 all-gather.2.cloned.1.call-done.block
  62.8 74.0 %project_rows.1 = bf16[320,1024]{1,0:T(8,128)(2,1)S(1)} custom-call(bf16[32,80,128]{2,1,0:T(8,128)(2,1)} %copy-done, bf16[1024,1024]{1,0:T(8,128)(2,1)} %all-gather.2.cloned.1.call-done.block), custom_call_target="tpu_custom_call" | custom-call | tf_op jit(solution)/shard_map/project_rows/pallas_call | solution.py:642
  136.8 0.8 copy.11
Async XLA Ops:
  6.5 52.6 %copy-start.2 = (s32[32]{0:T(128)S(1)}, s32[32]{0:T(128)}, u32[]{:S(2)}) copy-start(s32[32]{0:T(128)} %former.1) | copy-start | bytes 388
  6.5 52.7 %copy-start.4 = (s32[28]{0:T(128)S(1)}, s32[28]{0:T(128)}, u32[]{:S(2)}) copy-start(s32[28]{0:T(128)} %remaining.1) | copy-start | bytes 340
  6.5 52.7 %copy-start.3 = (s32[28]{0:T(128)S(1)}, s32[28]{0:T(128)}, u32[]{:S(2)}) copy-start(s32[28]{0:T(128)} %updated.1) | copy-start | bytes 340
  6.5 56.2 %all-gather.2.cloned.1.call-start = ((), (), s32[]{:S(2)}) async-start(), calls=%async_computation | async-start | bytes 2621440 | tf_op jit(solution)/shard_map/all_gather | solution.py:681
  59.2 1.1 copy-start.1
  61.9 0.8 copy-start
Sparse Core Ops, SparseCore 0:
  9.2 42.0 all-gather.1

commit v11 on v10

--- a/solution.py
+++ b/solution.py
@@ -494,9 +494,12 @@
         order += [distance, z_count - distance]
     order = [lax.rem(my_z + d, z_count) for d in order + [0]]
     others = [lax.rem(my_x + k, x_count) for k in (1, 3, 2)]
-    for owner in order:
-        for x in others:
-            piece_copy(x, owner).start()
+    def send_pieces(owners):
+        for owner in owners:
+            for x in others:
+                piece_copy(x, owner).start()
+
+    send_pieces(order[:2])
 
     def columns(y, core):
         return pl.ds(pl.multiple_of((y * 2 + core) * LANES, LANES), LANES)
@@ -580,7 +583,9 @@
         to_core(opposite, my_core, owner).start()
 
     ahead, lag = 2, 1
-    for owner in order[:ahead]:
+    launch(order[0])
+    send_pieces(order[2:])
+    for owner in order[1:ahead]:
         launch(owner)
     load.wait()
     sent = reach + 1

time: 145 us -> 145 us (level)
  no operation moved by 1% of the time
where the time goes in v11:
time: 145 us; the launch traced here: 144 us
  Pallas kernels  127 us (88%)
  between operations  13.4 us (9%)
  local copies, waits for them, and re-layouts  2.76 us (2%)
    pallas_call x1, Pallas kernels, project_call(): pl.pallas_call(functools.partial(project_kernel, x_count, z_count, y_coun...  73.9 us
    pallas_call x1, Pallas kernels, conv_call(): pl.pallas_call(functools.partial(conv_kernel, x_count, z_count), out_shap...  51.9 us
  transfers between devices with their start and end apart: 1, of which 0 were waited for; matrix products, arithmetic and copies ran while one was open for 0% of the time, Pallas kernels for 37%

profile of v11, /device:TPU:32, one launch (start us, length us, event | category | flops | bytes accessed | tf_op | source)
XLA Modules:
  0.0 144.4 jit_solution(14088651220010699435)
XLA Ops:
  6.5 0.0 copy-start.2
  6.5 0.0 copy-start.4
  6.5 0.0 copy-start.3
  6.5 0.0 all-gather.2.cloned.1.call-start
  6.5 0.7 all-gather.2.cloned.1.call-update
  7.3 51.9 %convolve.1.pieces = bf16[32,80,128]{2,1,0:T(8,128)(2,1)} custom-call(s32[32]{0:T(128)} %former.1, bf16[3,320,1024]{2,1,0:T(8,128)(2,1)} %bitcast.2, f32[3,3,1024]{2,1,0:T(4,128)} %taps_far.1, f32[16,1024]{1,0:T(8,128)} %residue_far.1, f32[16,1024]{1,0:T(8,128)} %damping_far.1, f32[1,1024]{1,0:T(1,128)} %bitcast.3), custom_call_target="tpu_custom_call" | custom-call | tf_op jit(solution)/shard_map/convolve/pallas_call | solution.py:362
  59.2 0.0 copy-done.2
  59.2 0.0 copy-done.4
  59.2 0.0 copy-done.3
  59.2 0.0 copy-start.1
  59.2 1.1 copy-done.1
  60.3 1.6 %reorder_rows.1.chosen = bf16[32,80,128]{2,1,0:T(8,128)(2,1)S(1)} custom-call(s32[32]{0:T(128)S(1)} %copy-done.2, s32[28]{0:T(128)S(1)} %copy-done.3, s32[28]{0:T(128)S(1)} %copy-done.4, bf16[32,80,128]{2,1,0:T(8,128)(2,1)S(1)} %copy-done.1), custom_call_target="tpu_custom_call" | custom-call | tf_op jit(solution)/shard_map/reorder_rows/pallas_call | solution.py:431
  61.9 0.0 copy-start
  61.9 0.8 copy-done
  62.8 0.0 all-gather.2.cloned.1.call-done.block
  62.8 73.9 %project_rows.1 = bf16[320,1024]{1,0:T(8,128)(2,1)S(1)} custom-call(bf16[32,80,128]{2,1,0:T(8,128)(2,1)} %copy-done, bf16[1024,1024]{1,0:T(8,128)(2,1)} %all-gather.2.cloned.1.call-done.block), custom_call_target="tpu_custom_call" | custom-call | tf_op jit(solution)/shard_map/project_rows/pallas_call | solution.py:647
  136.7 0.8 copy.11
Async XLA Ops:
  6.5 52.6 %copy-start.2 = (s32[32]{0:T(128)S(1)}, s32[32]{0:T(128)}, u32[]{:S(2)}) copy-start(s32[32]{0:T(128)} %former.1) | copy-start | bytes 388
  6.5 52.7 %copy-start.4 = (s32[28]{0:T(128)S(1)}, s32[28]{0:T(128)}, u32[]{:S(2)}) copy-start(s32[28]{0:T(128)} %remaining.1) | copy-start | bytes 340
  6.5 52.7 %copy-start.3 = (s32[28]{0:T(128)S(1)}, s32[28]{0:T(128)}, u32[]{:S(2)}) copy-start(s32[28]{0:T(128)} %updated.1) | copy-start | bytes 340
  6.5 56.2 %all-gather.2.cloned.1.call-start = ((), (), s32[]{:S(2)}) async-start(), calls=%async_computation | async-start | bytes 2621440 | tf_op jit(solution)/shard_map/all_gather | solution.py:686
  59.2 1.1 copy-start.1
  61.9 0.8 copy-start
Sparse Core Ops, SparseCore 0:
  9.2 42.0 all-gather.1
